TPU v7x, 32 devices: a whole 2x2x4 slice. The times are simulated.
32 devices in a mesh: seq: 8 (over z, core), fsdp: 4 (over y, x).
Axes of the slice: x: 2, y: 2, z: 4, core: 2. Of those that a mesh axis runs over, the one named last changes fastest.
Arguments:
- hidden_in: bfloat16 [8, 2048, 1024], P('fsdp', 'seq'), may hold values from -6 to 6
- norm1_gain: bfloat16 [1024], P(('seq', 'fsdp')), may hold values from 0.5 to 1.5
- norm1_bias: bfloat16 [1024], P(('seq', 'fsdp')), may hold values from -1.75 to 1.75
- qkv_weight: bfloat16 [1024, 3072], P(('seq', 'fsdp')), may hold values from -0.1875 to 0.1875
- qv_bias: bfloat16 [2048], P(('seq', 'fsdp')), may hold values from -1.75 to 1.75
- alibi_slopes: float32 [16], replicated, may hold values from 0.00048828125 to 0.2
- out_weight: bfloat16 [1024, 1024], P(('seq', 'fsdp')), may hold values from -0.75 to 0.75
- out_bias: bfloat16 [1024], P(('seq', 'fsdp')), may hold values from -1.75 to 1.75
- norm2_gain: bfloat16 [1024], P(('seq', 'fsdp')), may hold values from 0.5 to 1.5
- norm2_bias: bfloat16 [1024], P(('seq', 'fsdp')), may hold values from -1.75 to 1.75
- up_weight: bfloat16 [1024, 4096], P(('seq', 'fsdp')), may hold values from -0.1875 to 0.1875
- up_bias: bfloat16 [4096], P(('seq', 'fsdp')), may hold values from -1.75 to 1.75
- down_weight: bfloat16 [4096, 1024], P(('seq', 'fsdp')), may hold values from -0.09375 to 0.09375
- down_bias: bfloat16 [1024], P(('seq', 'fsdp')), may hold values from -1.75 to 1.75
- out_grad: bfloat16 [8, 2048, 1024], P('fsdp', 'seq'), may hold values from -6 to 6
Outputs:
- block_out: bfloat16 [8, 2048, 1024], P('fsdp', 'seq')
- input_grad: float32 [8, 2048, 1024], P('fsdp', 'seq')
- grad_norm1_gain: float32 [1024], P(('seq', 'fsdp'))
- grad_norm1_bias: float32 [1024], P(('seq', 'fsdp'))
- grad_qkv_weight: float32 [1024, 3072], P(('seq', 'fsdp'))
- grad_qv_bias: float32 [2048], P(('seq', 'fsdp'))
- grad_out_weight: float32 [1024, 1024], P(('seq', 'fsdp'))
- grad_out_bias: float32 [1024], P(('seq', 'fsdp'))
- grad_norm2_gain: float32 [1024], P(('seq', 'fsdp'))
- grad_norm2_bias: float32 [1024], P(('seq', 'fsdp'))
- grad_up_weight: float32 [1024, 4096], P(('seq', 'fsdp'))
- grad_up_bias: float32 [4096], P(('seq', 'fsdp'))
- grad_down_weight: float32 [4096, 1024], P(('seq', 'fsdp'))
- grad_down_bias: float32 [1024], P(('seq', 'fsdp'))
All inputs are finite; a program needn't handle non-finite values.
Results may differ from a plain program's by a relative error of at most 0.0095.
Values may be sent and summed in bfloat16 or wider, within the bound.
No kernel may reach another device: no remote copies, remote signals or barrier semaphores. Data moves between devices by JAX's collectives and lax.ppermute only.
A program may use at most 192 MiB of HBM per device.

v0:
```python
import jax
import jax.numpy as jnp
from jax import lax
from jax.sharding import PartitionSpec as P

H = 16
HD = 64


def layer_norm(values, norm_gain, norm_shift):
    average = jnp.mean(values, -1, keepdims=True)
    centered = values - average
    variance = jnp.mean(centered * centered, -1, keepdims=True)
    return centered * lax.rsqrt(variance + 1e-05) * norm_gain + norm_shift


def gelu_tanh(values):
    inside = 0.7978845608 * (values + 0.044715 * values * values * values)
    return 0.5 * values * (1.0 + jnp.tanh(inside))


def outer_sum(left, right):
    return lax.dot_general(
        left, right, (((0,), (0,)), ((), ())), preferred_element_type=jnp.float32
    )


def times_rows(left, right):
    return lax.dot_general(
        left, right, (((1,), (1,)), ((), ())), preferred_element_type=jnp.float32
    )


def alibi_scores(query_rows, keys_all, offset, slopes):
    factor = HD ** (-0.5)
    raw_scores = (
        jnp.einsum("nqhd,nkhd->nhqk", query_rows, keys_all, preferred_element_type=jnp.float32)
        * factor
    )
    query_pos = offset + jnp.arange(query_rows.shape[1], dtype=jnp.int32)
    key_pos = jnp.arange(keys_all.shape[1], dtype=jnp.int32)
    distance = query_pos[:, None] - key_pos[None, :]
    raw_scores = raw_scores - slopes[None, :, None, None] * distance.astype(jnp.float32)
    return jnp.where(distance >= 0, raw_scores, -1e30)


def split_parts(exchanged):
    amount = exchanged.shape[0]
    full_len = exchanged.shape[1]
    heads_here = exchanged.shape[3] // HD
    queries = exchanged[:, :, 0].reshape(amount, full_len, heads_here, HD)
    keys_all = exchanged[:, :, 1].reshape(amount, full_len, heads_here, HD)
    values_all = exchanged[:, :, 2].reshape(amount, full_len, heads_here, HD)
    return (amount, full_len, heads_here, queries, keys_all, values_all)


def attend_items(exchanged, slopes):
    amount, full_len, heads_here, queries, keys_all, values_all = split_parts(exchanged)
    row_block = min(512, full_len)
    num_blocks = full_len // row_block
    start_out = jnp.zeros((amount, full_len, heads_here * HD), jnp.bfloat16)
    start_lse = jnp.zeros((amount, heads_here, full_len), jnp.float32)

    def one_block(number, carry):
        out_rows, lse_rows = carry
        offset = number * row_block
        query_rows = lax.dynamic_slice_in_dim(queries, offset, row_block, 1)
        scores = alibi_scores(query_rows, keys_all, offset, slopes)
        highest = jnp.max(scores, -1, keepdims=True)
        weights = jnp.exp(scores - highest)
        totals = jnp.sum(weights, -1, keepdims=True)
        probs_low = (weights / totals).astype(jnp.bfloat16)
        blended = jnp.einsum(
            "nhqk,nkhd->nqhd", probs_low, values_all, preferred_element_type=jnp.float32
        )
        blended = blended.reshape(amount, row_block, heads_here * HD).astype(jnp.bfloat16)
        out_rows = lax.dynamic_update_slice_in_dim(out_rows, blended, offset, 1)
        lse_rows = lax.dynamic_update_slice_in_dim(
            lse_rows, (highest + jnp.log(totals))[..., 0], offset, 2
        )
        return (out_rows, lse_rows)

    blended_all, log_totals = lax.fori_loop(0, num_blocks, one_block, (start_out, start_lse))
    return (blended_all, log_totals, exchanged)


def attend_back(exchanged, grad_items, log_totals, slopes):
    amount, full_len, heads_here, queries, keys_all, values_all = split_parts(exchanged)
    grad_blended = grad_items.reshape(amount, full_len, heads_here, HD)
    row_block = min(512, full_len)
    num_blocks = full_len // row_block
    factor = HD ** (-0.5)
    empty_sum = jnp.zeros((amount, full_len, heads_here, HD), jnp.float32)
    empty_query = jnp.zeros((amount, full_len, heads_here * HD), jnp.bfloat16)

    def one_block(number, carry):
        key_total, value_total, query_all = carry
        offset = number * row_block
        query_rows = lax.dynamic_slice_in_dim(queries, offset, row_block, 1)
        grad_rows = lax.dynamic_slice_in_dim(grad_blended, offset, row_block, 1)
        lse_rows = lax.dynamic_slice_in_dim(log_totals, offset, row_block, 2)
        scores = alibi_scores(query_rows, keys_all, offset, slopes)
        attn_probs = jnp.exp(scores - lse_rows[..., None])
        probs_low = attn_probs.astype(jnp.bfloat16)
        value_total = value_total + jnp.einsum(
            "nhqk,nqhd->nkhd", probs_low, grad_rows, preferred_element_type=jnp.float32
        )
        grad_probs = jnp.einsum(
            "nqhd,nkhd->nhqk", grad_rows, values_all, preferred_element_type=jnp.float32
        )
        centre = jnp.sum(attn_probs * grad_probs, -1, keepdims=True)
        grad_scores = (attn_probs * (grad_probs - centre)).astype(jnp.bfloat16)
        query_grad = (
            jnp.einsum("nhqk,nkhd->nqhd", grad_scores, keys_all, preferred_element_type=jnp.float32)
            * factor
        )
        key_total = (
            key_total
            + jnp.einsum(
                "nhqk,nqhd->nkhd", grad_scores, query_rows, preferred_element_type=jnp.float32
            )
            * factor
        )
        query_low = query_grad.reshape(amount, row_block, heads_here * HD).astype(jnp.bfloat16)
        query_all = lax.dynamic_update_slice_in_dim(query_all, query_low, offset, 1)
        return (key_total, value_total, query_all)

    key_total, value_total, query_all = lax.fori_loop(
        0, num_blocks, one_block, (empty_sum, empty_sum, empty_query)
    )
    key_low = key_total.reshape(amount, full_len, heads_here * HD).astype(jnp.bfloat16)
    value_low = value_total.reshape(amount, full_len, heads_here * HD).astype(jnp.bfloat16)
    return jnp.stack([query_all, key_low, value_low], 2)


def body(
    hidden_in,
    norm1_gain,
    norm1_bias,
    qkv_weight,
    qv_bias,
    alibi_slopes,
    out_weight,
    out_bias,
    norm2_gain,
    norm2_bias,
    up_weight,
    up_bias,
    down_weight,
    down_bias,
    out_grad,
):
    seq_devices = lax.axis_size("seq")
    sequences, local_len, model_width = hidden_in.shape
    tokens = sequences * local_len
    heads_local = H // seq_devices
    slopes = lax.dynamic_slice_in_dim(
        alibi_slopes, lax.axis_index("seq") * heads_local, heads_local
    )
    first_gain, first_shift, w_qkv, bias_qv = (
        lax.all_gather(norm1_gain, ("seq", "fsdp"), axis=0, tiled=True),
        lax.all_gather(norm1_bias, ("seq", "fsdp"), axis=0, tiled=True),
        lax.all_gather(qkv_weight, ("seq", "fsdp"), axis=0, tiled=True),
        lax.all_gather(qv_bias, ("seq", "fsdp"), axis=0, tiled=True),
    )
    flat_in = hidden_in.reshape(tokens, model_width).astype(jnp.float32)
    first_norm, first_back = jax.vjp(
        layer_norm, flat_in, first_gain.astype(jnp.float32), first_shift.astype(jnp.float32)
    )
    first_low = first_norm.astype(jnp.bfloat16)
    bias_wide = bias_qv.astype(jnp.float32)
    full_bias = jnp.concatenate(
        [bias_wide[:model_width], jnp.zeros((model_width,), jnp.float32), bias_wide[model_width:]]
    )
    projected = (jnp.dot(first_low, w_qkv, preferred_element_type=jnp.float32) + full_bias).astype(
        jnp.bfloat16
    )
    packed = projected.reshape(sequences, local_len, 3, model_width)
    attended, log_totals, qkv_heads = attend_items(
        lax.all_to_all(packed, "seq", split_axis=3, concat_axis=1, tiled=True), slopes
    )
    returned = lax.all_to_all(attended, "seq", split_axis=1, concat_axis=2, tiled=True)
    attended_low = returned.reshape(tokens, model_width)
    w_out, b_out, second_gain, second_shift, w_up, b_up, w_down, b_down = (
        lax.all_gather(out_weight, ("seq", "fsdp"), axis=0, tiled=True),
        lax.all_gather(out_bias, ("seq", "fsdp"), axis=0, tiled=True),
        lax.all_gather(norm2_gain, ("seq", "fsdp"), axis=0, tiled=True),
        lax.all_gather(norm2_bias, ("seq", "fsdp"), axis=0, tiled=True),
        lax.all_gather(up_weight, ("seq", "fsdp"), axis=0, tiled=True),
        lax.all_gather(up_bias, ("seq", "fsdp"), axis=0, tiled=True),
        lax.all_gather(down_weight, ("seq", "fsdp"), axis=0, tiled=True),
        lax.all_gather(down_bias, ("seq", "fsdp"), axis=0, tiled=True),
    )
    middle = (
        flat_in
        + jnp.dot(attended_low, w_out, preferred_element_type=jnp.float32)
        + b_out.astype(jnp.float32)
    )
    second_norm, second_back = jax.vjp(
        layer_norm, middle, second_gain.astype(jnp.float32), second_shift.astype(jnp.float32)
    )
    second_low = second_norm.astype(jnp.bfloat16)
    hidden_pre = jnp.dot(second_low, w_up, preferred_element_type=jnp.float32) + b_up.astype(
        jnp.float32
    )
    activated, gelu_back = jax.vjp(gelu_tanh, hidden_pre)
    activated_low = activated.astype(jnp.bfloat16)
    result = (
        middle
        + jnp.dot(activated_low, w_down, preferred_element_type=jnp.float32)
        + b_down.astype(jnp.float32)
    )
    block_out = result.astype(jnp.bfloat16).reshape(sequences, local_len, model_width)
    w_qkv_back = lax.all_gather(qkv_weight, ("seq", "fsdp"), axis=0, tiled=True)
    w_out_back, w_up_back, w_down_back = (
        lax.all_gather(out_weight, ("seq", "fsdp"), axis=0, tiled=True),
        lax.all_gather(up_weight, ("seq", "fsdp"), axis=0, tiled=True),
        lax.all_gather(down_weight, ("seq", "fsdp"), axis=0, tiled=True),
    )
    cot_low = out_grad.reshape(tokens, model_width)
    cotangent = cot_low.astype(jnp.float32)
    grad_down = outer_sum(activated_low, cot_low)
    grad_down_bias = jnp.sum(cotangent, 0)
    grad_act = times_rows(cot_low, w_down_back)
    (grad_pre,) = gelu_back(grad_act)
    grad_hidden = grad_pre.astype(jnp.bfloat16)
    grad_up = outer_sum(second_low, grad_hidden)
    grad_up_bias = jnp.sum(grad_hidden.astype(jnp.float32), 0)
    grad_second = times_rows(grad_hidden, w_up_back)
    grad_mid_norm, grad_gain_two, grad_shift_two = second_back(grad_second)
    grad_middle = cotangent + grad_mid_norm
    grad_branch = grad_middle.astype(jnp.bfloat16)
    grad_outw = outer_sum(attended_low, grad_branch)
    grad_out_bias = jnp.sum(grad_branch.astype(jnp.float32), 0)
    grad_attended = times_rows(grad_branch, w_out_back).astype(jnp.bfloat16)
    rear_sums = (
        lax.psum_scatter(grad_outw, ("seq", "fsdp"), scatter_dimension=0, tiled=True),
        lax.psum_scatter(grad_out_bias, ("seq", "fsdp"), scatter_dimension=0, tiled=True),
        lax.psum_scatter(grad_gain_two, ("seq", "fsdp"), scatter_dimension=0, tiled=True),
        lax.psum_scatter(grad_shift_two, ("seq", "fsdp"), scatter_dimension=0, tiled=True),
        lax.psum_scatter(grad_up, ("seq", "fsdp"), scatter_dimension=0, tiled=True),
        lax.psum_scatter(grad_up_bias, ("seq", "fsdp"), scatter_dimension=0, tiled=True),
        lax.psum_scatter(grad_down, ("seq", "fsdp"), scatter_dimension=0, tiled=True),
        lax.psum_scatter(grad_down_bias, ("seq", "fsdp"), scatter_dimension=0, tiled=True),
    )
    grad_packed = grad_attended.reshape(sequences, local_len, model_width)
    grad_heads = lax.all_to_all(grad_packed, "seq", split_axis=2, concat_axis=1, tiled=True)
    grad_qkv_heads = attend_back(qkv_heads, grad_heads, log_totals, slopes)
    grad_returned = lax.all_to_all(grad_qkv_heads, "seq", split_axis=1, concat_axis=3, tiled=True)
    grad_projected = grad_returned.reshape(tokens, 3 * model_width)
    grad_qkvw = outer_sum(first_low, grad_projected)
    column_sums = jnp.sum(grad_projected.astype(jnp.float32), 0)
    grad_qv = jnp.concatenate([column_sums[:model_width], column_sums[2 * model_width :]])
    grad_first = times_rows(grad_projected, w_qkv_back)
    grad_in_norm, grad_gain_one, grad_shift_one = first_back(grad_first)
    input_grad = (grad_middle + grad_in_norm).reshape(sequences, local_len, model_width)
    front_sums = (
        lax.psum_scatter(grad_gain_one, ("seq", "fsdp"), scatter_dimension=0, tiled=True),
        lax.psum_scatter(grad_shift_one, ("seq", "fsdp"), scatter_dimension=0, tiled=True),
        lax.psum_scatter(grad_qkvw, ("seq", "fsdp"), scatter_dimension=0, tiled=True),
        lax.psum_scatter(grad_qv, ("seq", "fsdp"), scatter_dimension=0, tiled=True),
    )
    return (
        block_out,
        input_grad,
        front_sums[0],
        front_sums[1],
        front_sums[2],
        front_sums[3],
        rear_sums[0],
        rear_sums[1],
        rear_sums[2],
        rear_sums[3],
        rear_sums[4],
        rear_sums[5],
        rear_sums[6],
        rear_sums[7],
    )


def solution(mesh):
    return jax.shard_map(
        body,
        mesh=mesh,
        in_specs=(
            P("fsdp", "seq", None),
            P(("seq", "fsdp")),
            P(("seq", "fsdp")),
            P(("seq", "fsdp"), None),
            P(("seq", "fsdp")),
            P(),
            P(("seq", "fsdp"), None),
            P(("seq", "fsdp")),
            P(("seq", "fsdp")),
            P(("seq", "fsdp")),
            P(("seq", "fsdp"), None),
            P(("seq", "fsdp")),
            P(("seq", "fsdp"), None),
            P(("seq", "fsdp")),
            P("fsdp", "seq", None),
        ),
        out_specs=(
            P("fsdp", "seq", None),
            P("fsdp", "seq", None),
            P(("seq", "fsdp")),
            P(("seq", "fsdp")),
            P(("seq", "fsdp"), None),
            P(("seq", "fsdp")),
            P(("seq", "fsdp"), None),
            P(("seq", "fsdp")),
            P(("seq", "fsdp")),
            P(("seq", "fsdp")),
            P(("seq", "fsdp"), None),
            P(("seq", "fsdp")),
            P(("seq", "fsdp"), None),
            P(("seq", "fsdp")),
        ),
        check_vma=False,
    )
```

profile of v0, /device:TPU:0, one launch (start us, length us, event | category | flops | bytes accessed | tf_op | source)
XLA Modules:
  0.0 1772.6 jit_solution(11565726647185323737)
XLA Ops:
  15.3 42.5 %all-reduce.16 = (bf16[1024]{0:T(1024)(128)(2,1)}, bf16[1024]{0:T(1024)(128)(2,1)S(1)}, bf16[1024]{0:T(1024)(128)(2,1)S(1)}, bf16[2048]{0:T(1024)(128)(2,1)S(1)}...) all-reduce(bf16[1024]{0:T(1024)(128)(2,1)S(1)} %dynamic-update-slic, ...), channel_id=1, replica_groups=mesh['seq'=8,'fsdp'=4] {'seq','fsdp'}, use_global_device_ids=true, to_apply=%add.3 | all-reduce | flops 8192 | bytes 32768
  65.3 18.1 %all-gather.6.cloned.1.call-done = bf16[1024,3072]{1,0:T(8,128)(2,1)} async-done(((bf16[32,3072]{1,0:T(8,128)(2,1)}), bf16[1024,3072]{1,0:T(8,128)(2,1)}) %all-gather.6.cloned.1.call-update) | async-done | bytes 6291472 | tf_op jit(solution)/shard_map/all_gather | solution.py:163
  112.0 91.9 %all-to-all-done = bf16[2,256,3,1024]{1,0,2,3:T(2,128)(2,1)S(1)} async-done(((bf16[2,256,3,1024]{1,0,2,3:T(2,128)(2,1)}), bf16[2,256,3,1024]{1,0,2,3:T(2,128)(2,1)S(1)}, u32[]{:S(2)}, u32[]{:S(2)}) %all-to-all-start) | async-done | bytes 3145760 | tf_op jit(solution)/shard_map/all_to_all | solution.py:180
  217.2 146.1 %while.33 = (s32[]{:T(128)}, bf16[2,2048,128]{2,0,1:T(2,128)(2,1)}, f32[2,2,2048]{2,1,0:T(2,128)S(1)}, bf16[2,2048,2,64]{1,3,2,0:T(8,128)(2,1)}, bf16[2,2048,2,6...) while((s32[]{:T(128)}, bf16[2,2048,128]{2,0,1:T(2,128)(2,1)}, ...), condition=%wide.region_5.6_spmd, body=%wide.region_2.5_spmd.sunk | while | flops 1143077376 | bytes 133765328 | solution.py:83
  367.8 79.1 %all-gather = bf16[32,1,128]{2,1,0:T(2,128)(2,1)S(1)} all-gather(bf16[1,1,128]{2,1,0:T(2,128)(2,1)S(1)} %bitcast.175), channel_id=1, replica_groups=mesh['seq'=8,'fsdp'=4] {'seq','fsdp'}, dimensions={0}, use_global_device_ids=true | all-gather | bytes 8448 | tf_op jit(solution)/shard_map/all_gather | solution.py:190
  454.4 11.9 fusion.69
  466.4 15.2 convert_reduce_fusion
  504.2 23.9 %all-to-all-done.2 = bf16[2,256,1024]{1,0,2:T(2,128)(2,1)} async-done(((bf16[2,256,1024]{1,0,2:T(2,128)(2,1)}), bf16[2,256,1024]{1,0,2:T(2,128)(2,1)}, u32[]{:S(2)}, u32[]{:S(2)}) %all-to-all-start.2) | async-done | bytes 1048608 | tf_op jit(solution)/shard_map/all_to_all | solution.py:247
  534.3 251.5 %while.34 = (s32[]{:T(128)}, f32[2,2048,2,64]{1,3,2,0:T(8,128)}, f32[2,2048,2,64]{1,3,2,0:T(8,128)}, bf16[2,2048,128]{1,2,0:T(8,128)(2,1)}, bf16[2,2048,2,64]{1,...) while((s32[]{:T(128)}, f32[2,2048,2,64]{1,3,2,0:T(8,128)}, ...), condition=%wide.region_12.13_spmd.clone, body=%wide.region_10.0_spmd.clone.sunk | while | flops 2735471104 | bytes 208451936 | solution.py:128
  549.1 14.8 multiply_reduce_fusion.5
  563.9 15.0 multiply_convert_fusion.2
  611.6 14.8 multiply_reduce_fusion.5
  626.4 15.1 multiply_convert_fusion.2
  674.7 14.7 multiply_reduce_fusion.5
  689.4 14.9 multiply_convert_fusion.2
  737.5 14.7 multiply_reduce_fusion.5
  752.2 14.9 multiply_convert_fusion.2
  799.4 71.0 %all-to-all-done.3 = bf16[2,2048,3,128]{3,0,2,1:T(2,128)(2,1)} async-done(((bf16[2,2048,3,128]{3,0,2,1:T(2,128)(2,1)}), bf16[2,2048,3,128]{3,0,2,1:T(2,128)(2,1)}, u32[]{:S(2)}, u32[]{:S(2)}) %all-to-all-start.3) | async-done | bytes 3145760 | tf_op jit(solution)/shard_map/all_to_all | solution.py:249
  904.1 16.8 fusion.70
  921.8 13.9 add_convert_fusion.1
  947.7 41.4 %all-reduce.15 = (f32[1024]{0:T(1024)S(1)}, f32[1024]{0:T(1024)S(1)}, f32[2048]{0:T(1024)S(1)}, f32[1024]{0:T(1024)S(1)}, f32[1024]{0:T(1024)S(1)}, /*index=5*/f...) all-reduce(f32[1024]{0:T(1024)S(1)} %get-tuple-element.367, ...), channel_id=2, replica_groups=mesh['seq'=8,'fsdp'=4] {'seq','fsdp'}, use_global_device_ids=true, to_apply=%region_16.17.clone | all-reduce | flops 12288 | bytes 98304
  997.9 45.8 %reduce-scatter.5.cloned.1.call-done = f32[32,3072]{1,0:T(8,128)} async-done(((f32[1024,3072]{1,0:T(8,128)}), f32[32,3072]{1,0:T(8,128)}) %reduce-scatter.5.cloned.1.call-update) | async-done | bytes 393232 | tf_op jit(solution)/shard_map/reduce_scatter | solution.py:260
  1043.7 359.7 %reduce-scatter.9.cloned.1.call-done = f32[32,4096]{1,0:T(8,128)} async-done(((f32[1024,4096]{1,0:T(8,128)}), f32[32,4096]{1,0:T(8,128)}) %reduce-scatter.9.cloned.1.call-update) | async-done | bytes 524304 | tf_op jit(solution)/shard_map/reduce_scatter | solution.py:241
  1403.5 362.1 %reduce-scatter.11.cloned.1.call-done = f32[128,1024]{1,0:T(8,128)} async-done(((f32[4096,1024]{1,0:T(8,128)}), f32[128,1024]{1,0:T(8,128)}) %reduce-scatter.11.cloned.1.call-update) | async-done | bytes 524304 | tf_op jit(solution)/shard_map/reduce_scatter | solution.py:243
  (347 shorter events, 444.7 us)
Async XLA Ops:
  7.2 76.2 %all-gather.6.cloned.1.call-start = ((), (), s32[]{:S(2)}) async-start(), calls=%async_computation.8 | async-start | bytes 6488064 | tf_op jit(solution)/shard_map/all_gather | solution.py:163
  7.9 441.8 %all-gather.8.cloned.1.call-start = ((), (), s32[]{:S(2)}) async-start(), calls=%async_computation.9 | async-start | bytes 2162688 | tf_op jit(solution)/shard_map/all_gather | solution.py:185
  8.7 445.7 %all-gather.10.cloned.1.call-start = ((), (), s32[]{:S(2)}) async-start(), calls=%async_computation.10 | async-start | bytes 8650752 | tf_op jit(solution)/shard_map/all_gather | solution.py:189
  107.5 96.3 %all-to-all-start = ((bf16[2,256,3,1024]{1,0,2,3:T(2,128)(2,1)}), bf16[2,256,3,1024]{1,0,2,3:T(2,128)(2,1)S(1)}, u32[]{:S(2)}, u32[]{:S(2)}) async-start(bf16[2,256,3,1024]{1,0,2,3:T(2,128)(2,1)} %copy.73), calls=%async_computation | async-start | bytes 6291456 | tf_op jit(solution)/shard_map/all_to_all | solution.py:180
  111.3 355.0 %all-gather.12.cloned.1.call-start = ((), (), s32[]{:S(2)}) async-start(), calls=%async_computation.11 | async-start | bytes 8650752 | tf_op jit(solution)/shard_map/all_gather | solution.py:191
  217.1 150.6 %copy-start.52 = (bf16[1024]{0:T(1024)(128)(2,1)S(1)}, bf16[1024]{0:T(1024)(128)(2,1)}, u32[]{:S(2)}) copy-start(bf16[1024]{0:T(1024)(128)(2,1)} %get-tuple-element.414) | copy-start | bytes 6148
  217.1 150.6 %copy-start.51 = (bf16[1024]{0:T(1024)(128)(2,1)S(1)}, bf16[1024]{0:T(1024)(128)(2,1)}, u32[]{:S(2)}) copy-start(bf16[1024]{0:T(1024)(128)(2,1)} %get-tuple-element.419) | copy-start | bytes 6148
  217.1 150.6 %copy-start.50 = (bf16[1024]{0:T(1024)(128)(2,1)S(1)}, bf16[1024]{0:T(1024)(128)(2,1)}, u32[]{:S(2)}) copy-start(bf16[1024]{0:T(1024)(128)(2,1)} %get-tuple-element.420) | copy-start | bytes 6148
  217.2 150.6 %copy-start.53 = (bf16[128]{0:T(256)(128)(2,1)S(1)}, bf16[128]{0:T(256)(128)(2,1)}, u32[]{:S(2)}) copy-start(bf16[128]{0:T(256)(128)(2,1)} %param.30) | copy-start | bytes 772
  363.3 86.5 %copy-start.4 = (bf16[2,256,1024]{2,1,0:T(8,128)(2,1)S(1)}, bf16[2,256,1024]{2,1,0:T(8,128)(2,1)}, u32[]{:S(2)}) copy-start(bf16[2,256,1024]{2,1,0:T(8,128)(2,1)} %param.19) | copy-start | bytes 3145732
  363.3 83.6 %all-to-all-start.1 = ((bf16[2,2048,128]{2,0,1:T(2,128)(2,1)}), bf16[2,2048,128]{2,0,1:T(2,128)(2,1)}, u32[]{:S(2)}, u32[]{:S(2)}) async-start(bf16[2,2048,128]{2,0,1:T(2,128)(2,1)} %get-tuple-element.310), calls=%async_computation.1 | async-start | bytes 2097152 | tf_op jit(solution)/shard_map/all_to_all | solution.py:182
  367.7 86.7 %copy-start.47 = (f32[1024]{0:T(1024)}, f32[1024]{0:T(1024)S(1)}, u32[]{:S(2)}) copy-start(f32[1024]{0:T(1024)S(1)} %convert_element_type.185) | copy-start | bytes 12292
  367.7 119.3 %copy-start.40 = (f32[1024]{0:T(1024)}, f32[1024]{0:T(1024)S(1)}, u32[]{:S(2)}) copy-start(f32[1024]{0:T(1024)S(1)} %convert_element_type.184) | copy-start | bytes 12292
  453.0 34.0 %copy-start.34 = (f32[512]{0:T(512)}, f32[512]{0:T(512)S(1)}, u32[]{:S(2)}) copy-start(f32[512]{0:T(512)S(1)} %broadcast_multiply_fusion.2) | copy-start | bytes 6148
  454.4 32.7 %copy-start.42 = (f32[512]{0:T(512)}, f32[512]{0:T(512)S(1)}, u32[]{:S(2)}) copy-start(f32[512]{0:T(512)S(1)} %fusion.63) | copy-start | bytes 6148
  495.1 32.9 %all-to-all-start.2 = ((bf16[2,256,1024]{1,0,2:T(2,128)(2,1)}), bf16[2,256,1024]{1,0,2:T(2,128)(2,1)}, u32[]{:S(2)}, u32[]{:S(2)}) async-start(bf16[2,256,1024]{1,0,2:T(2,128)(2,1)} %copy.81), calls=%async_computation.2 | async-start | bytes 2097152 | tf_op jit(solution)/shard_map/all_to_all | solution.py:247
  499.3 498.6 %reduce-scatter.7.cloned.1.call-start = ((), (), s32[]{:S(2)}) async-start(), calls=%async_computation.13 | async-start | bytes 4325376 | tf_op jit(solution)/shard_map/reduce_scatter | solution.py:237
  504.1 30.1 %copy-start.6 = (bf16[2,2048,2,64]{1,3,2,0:T(8,128)(2,1)S(1)}, bf16[2,2048,2,64]{1,3,2,0:T(8,128)(2,1)}, u32[]{:S(2)}) copy-start(bf16[2,2048,2,64]{1,3,2,0:T(8,128)(2,1)} %get-tuple-element.643) | copy-start | bytes 3145732
  794.3 76.2 %all-to-all-start.3 = ((bf16[2,2048,3,128]{3,0,2,1:T(2,128)(2,1)}), bf16[2,2048,3,128]{3,0,2,1:T(2,128)(2,1)}, u32[]{:S(2)}, u32[]{:S(2)}) async-start(bf16[2,2048,3,128]{3,0,2,1:T(2,128)(2,1)} %copy.83), calls=%async_computation.3 | async-start | bytes 6291456 | tf_op jit(solution)/shard_map/all_to_all | solution.py:249
  798.9 244.9 %reduce-scatter.5.cloned.1.call-start = ((), (), s32[]{:S(2)}) async-start(), calls=%async_computation.12 | async-start | bytes 12976128 | tf_op jit(solution)/shard_map/reduce_scatter | solution.py:260
  890.0 513.5 %reduce-scatter.9.cloned.1.call-start = ((), (), s32[]{:S(2)}) async-start(), calls=%async_computation.14 | async-start | bytes 17301504 | tf_op jit(solution)/shard_map/reduce_scatter | solution.py:241
  902.9 862.7 %reduce-scatter.11.cloned.1.call-start = ((), (), s32[]{:S(2)}) async-start(), calls=%async_computation.15 | async-start | bytes 17301504 | tf_op jit(solution)/shard_map/reduce_scatter | solution.py:243
  939.5 54.3 %copy-start.29 = (f32[512]{0:T(512)S(1)}, f32[512]{0:T(512)}, u32[]{:S(2)}) copy-start(f32[512]{0:T(512)} %copy-done.28) | copy-start | bytes 6148
  945.3 48.4 %copy-start.8 = (f32[512,1024]{1,0:T(8,128)S(1)}, f32[512,1024]{1,0:T(8,128)}, u32[]{:S(2)}) copy-start(f32[512,1024]{1,0:T(8,128)} %copy-done.7) | copy-start | bytes 6291460
  (63 other events, 405.4 us)
Sparse Core Ops, SparseCore 0:
  10.9 72.4 all-gather.5
  86.2 63.7 all-gather.7
  152.9 88.5 all-gather.9
  244.2 76.2 all-gather.11
  504.3 141.8 reduce-scatter.6
  890.1 153.5 reduce-scatter.4
  1046.7 356.7 reduce-scatter.8
  1406.4 359.0 reduce-scatter.10
where the time goes:
time: 1780 us; the launch traced here: 1770 us
  waiting for transfers between devices  975 us (55%)
  matrix products  345 us (19%)
  other arithmetic  168 us (9%)
  blocking collectives  163 us (9%)
  local copies, waits for them, and re-layouts  87.2 us (5%)
  starting transfers between devices  18.1 us (1%)
    reduce_scatter x1, waiting for transfers between devices, body(): lax.psum_scatter(grad_down, ('seq', 'fsdp'), scatter_dimension=0, tiled=T...  362 us
    reduce_scatter x1, waiting for transfers between devices, body(): lax.psum_scatter(grad_up, ('seq', 'fsdp'), scatter_dimension=0, tiled=True)  360 us
    dot_general x8, matrix products, alibi_scores(): jnp.einsum('nqhd,nkhd->nhqk', query_rows, keys_all, preferred_element_typ...  99.3 us
    all_to_all x1, waiting for transfers between devices, body(): lax.all_to_all(packed, 'seq', split_axis=3, concat_axis=1, tiled=True)  91.9 us
    unnamed x2, blocking collectives  83.8 us
    all_gather x1, blocking collectives, body(): lax.all_gather(up_bias, ('seq', 'fsdp'), axis=0, tiled=True)  79.1 us
    all_to_all x1, waiting for transfers between devices, body(): lax.all_to_all(grad_qkv_heads, 'seq', split_axis=1, concat_axis=3, tiled=...  71 us
    convert_element_type x4, other arithmetic, one_block(): grad_scores = (attn_probs * (grad_probs - centre)).astype(jnp.bfloat16)  59.9 us
  transfers between devices with their start and end apart: 12, of which 7 were waited for; matrix products, arithmetic and copies ran while one was open for 32% of the time, Pallas kernels for 0%

commit v1 on v0

v1 whole, which is shorter than its diff:
```python
import functools

import jax
import jax.numpy as jnp
from jax import lax
from jax.experimental import pallas as pl
from jax.experimental.pallas import tpu as pltpu
from jax.sharding import Mesh
from jax.sharding import PartitionSpec as P

H = 16
HD = 64
SEQ = ("z", "core")
FSDP = ("fy", "fx")
ALL = SEQ + FSDP
BF = jnp.bfloat16
F32 = jnp.float32
NT = (((1,), (1,)), ((), ()))
VMEM_BYTES = 48 * 1024 * 1024


def layer_norm(values, norm_gain, norm_shift):
    average = jnp.mean(values, -1, keepdims=True)
    centered = values - average
    variance = jnp.mean(centered * centered, -1, keepdims=True)
    return centered * lax.rsqrt(variance + 1e-05) * norm_gain + norm_shift


def gelu_tanh(values):
    inside = 0.7978845608 * (values + 0.044715 * values * values * values)
    return 0.5 * values * (1.0 + jnp.tanh(inside))


def outer_sum(left, right):
    return lax.dot_general(left, right, (((0,), (0,)), ((), ())), preferred_element_type=F32)


def times_rows(left, right):
    return lax.dot_general(left, right, NT, preferred_element_type=F32)


def swap(values, axis):
    return lax.ppermute(values, axis, [(0, 1), (1, 0)])


def gather_axis(values, axis):
    if lax.axis_size(axis) != 2:
        return lax.all_gather(values, axis, axis=0, tiled=False)
    other = swap(values, axis)
    first = lax.axis_index(axis) == 0
    return jnp.stack([jnp.where(first, values, other), jnp.where(first, other, values)])


def reduce_axis(values, axis, position):
    if lax.axis_size(axis) != 2:
        return lax.psum_scatter(values, axis, scatter_dimension=position, tiled=False)
    me = lax.axis_index(axis)
    give = lax.dynamic_index_in_dim(values, 1 - me, position, keepdims=False)
    keep = lax.dynamic_index_in_dim(values, me, position, keepdims=False)
    return (keep.astype(F32) + swap(give, axis).astype(F32)).astype(BF)


def project_kernel(x_ref, gain_ref, shift_ref, w_ref, bias_ref, low_ref, q_ref, k_ref, v_ref, kt_ref, vt_ref):
    width = q_ref.shape[1]
    low = layer_norm(x_ref[...].astype(F32), gain_ref[...], shift_ref[...]).astype(BF)
    low_ref[...] = low
    made = (jnp.dot(low, w_ref[...], preferred_element_type=F32) + bias_ref[...]).astype(BF)
    made = made.astype(F32)
    keys, values = made[:, width : 2 * width], made[:, 2 * width :]
    q_ref[...] = (made[:, :width] * (HD**-0.5)).astype(BF)
    k_ref[...] = keys.astype(BF)
    v_ref[...] = values.astype(BF)
    kt_ref[...] = keys.T.astype(BF)
    vt_ref[...] = values.T.astype(BF)


def project(rows, gain, shift, weight, bias):
    length, model_width = rows.shape
    width = weight.shape[1] // 3
    block = min(512, length)
    whole = lambda i: (0, 0)
    down = lambda i: (i, 0)
    across = lambda i: (0, i)
    return pl.pallas_call(
        project_kernel,
        grid=(length // block,),
        in_specs=[
            pl.BlockSpec((block, model_width), down),
            pl.BlockSpec((1, model_width), whole),
            pl.BlockSpec((1, model_width), whole),
            pl.BlockSpec((model_width, 3 * width), whole),
            pl.BlockSpec((1, 3 * width), whole),
        ],
        out_specs=[
            pl.BlockSpec((block, model_width), down),
            pl.BlockSpec((block, width), down),
            pl.BlockSpec((block, width), down),
            pl.BlockSpec((block, width), down),
            pl.BlockSpec((width, block), across),
            pl.BlockSpec((width, block), across),
        ],
        out_shape=[jax.ShapeDtypeStruct((length, model_width), BF)]
        + [jax.ShapeDtypeStruct((length, width), BF)] * 3
        + [jax.ShapeDtypeStruct((width, length), BF)] * 2,
        compiler_params=pltpu.CompilerParams(vmem_limit_bytes=VMEM_BYTES),
        cost_estimate=pl.CostEstimate(
            flops=2 * length * model_width * 3 * width,
            bytes_accessed=4 * length * model_width + 10 * length * width,
            transcendentals=0,
        ),
        name="project",
    )(rows, gain, shift, weight, bias)


def tile_helpers(head, slope, block, width):
    lane = lax.broadcasted_iota(jnp.int32, (block, width), 1)
    mine = (lane >= head * HD) & (lane < head * HD + HD)
    key = lax.broadcasted_iota(jnp.int32, (block, block), 0)
    query = lax.broadcasted_iota(jnp.int32, (block, block), 1)
    return mine, slope * key.astype(F32), key <= query


def attend_kernel(slope_ref, q_ref, k_ref, vt_ref, o_ref, lse_ref, score_scr, out_scr):
    block, width = q_ref.shape
    number, head = pl.program_id(0), pl.program_id(1)
    slope = slope_ref[head]
    mine, bias, causal = tile_helpers(head, slope, block, width)
    queries = jnp.where(mine, q_ref[...], jnp.zeros_like(q_ref[...]))

    def one_block(last):
        highest = None
        for t in range(last + 1):
            rows = pl.ds(t * block, block)
            scores = lax.dot_general(k_ref[rows, :], queries, NT, preferred_element_type=F32) + bias
            if t == last:
                scores = jnp.where(causal, scores, -1e30)
            score_scr[rows, :] = scores
            top = jnp.max(scores, 0, keepdims=True) + slope * (t * block)
            highest = top if highest is None else jnp.maximum(highest, top)
        total = jnp.zeros((1, block), F32)
        blended = jnp.zeros((width, block), F32)
        for t in range(last + 1):
            rows = pl.ds(t * block, block)
            weights = jnp.exp(score_scr[rows, :] - (highest - slope * (t * block)))
            total = total + jnp.sum(weights, 0, keepdims=True)
            blended = blended + jnp.dot(
                vt_ref[:, rows], weights.astype(BF), preferred_element_type=F32
            )
        lse_ref[...] = (highest + jnp.log(total)).reshape(lse_ref.shape)
        result = jnp.where(mine, (blended / total).T, 0.0)

        @pl.when(head == 0)
        def _():
            out_scr[...] = result

        @pl.when(head > 0)
        def _():
            out_scr[...] = out_scr[...] + result

    for last in range(k_ref.shape[0] // block):
        pl.when(number == last)(functools.partial(one_block, last))

    @pl.when(head == pl.num_programs(1) - 1)
    def _():
        o_ref[...] = out_scr[...].astype(BF)


def attend(slopes, queries, keys, values_t):
    length, width = queries.shape
    heads = slopes.shape[0]
    block = min(256, length)
    whole = lambda i, h: (0, 0)
    down = lambda i, h: (i, 0)
    return pl.pallas_call(
        attend_kernel,
        grid=(length // block, heads),
        in_specs=[
            pl.BlockSpec(memory_space=pltpu.SMEM),
            pl.BlockSpec((block, width), down),
            pl.BlockSpec((length, width), whole),
            pl.BlockSpec((width, length), whole),
        ],
        out_specs=[
            pl.BlockSpec((block, width), down),
            pl.BlockSpec((1, 1, block), lambda i, h: (h, 0, i)),
        ],
        out_shape=[
            jax.ShapeDtypeStruct((length, width), BF),
            jax.ShapeDtypeStruct((heads, 1, length), F32),
        ],
        scratch_shapes=[pltpu.VMEM((length, block), F32), pltpu.VMEM((block, width), F32)],
        compiler_params=pltpu.CompilerParams(vmem_limit_bytes=VMEM_BYTES),
        cost_estimate=pl.CostEstimate(
            flops=8 * heads * length * length * HD,
            bytes_accessed=8 * length * width,
            transcendentals=heads * length * length // 2,
        ),
        name="attend",
    )(slopes, queries, keys, values_t)


def attend_back_kernel(
    slope_ref, q_ref, k_ref, kt_ref, v_ref, g_ref, lse_ref,
    dq_ref, dk_ref, dv_ref, prob_scr, dp_scr, dk_scr, dv_scr, dq_scr,
):
    block, width = q_ref.shape
    number, head = pl.program_id(0), pl.program_id(1)
    slope = slope_ref[head]
    mine, bias, causal = tile_helpers(head, slope, block, width)
    queries = jnp.where(mine, q_ref[...], jnp.zeros_like(q_ref[...]))
    grads = jnp.where(mine, g_ref[...], jnp.zeros_like(g_ref[...]))
    lse = lse_ref[...].reshape(1, block)

    @pl.when((number == 0) & (head == 0))
    def _():
        dk_scr[...] = jnp.zeros_like(dk_scr)
        dv_scr[...] = jnp.zeros_like(dv_scr)

    def one_block(last):
        centre = jnp.zeros((1, block), F32)
        for t in range(last + 1):
            rows = pl.ds(t * block, block)
            scores = lax.dot_general(k_ref[rows, :], queries, NT, preferred_element_type=F32) + bias
            if t == last:
                scores = jnp.where(causal, scores, -1e30)
            probs = jnp.exp(scores - (lse - slope * (t * block)))
            dp = lax.dot_general(v_ref[rows, :], grads, NT, preferred_element_type=F32)
            prob_scr[rows, :] = probs
            dp_scr[rows, :] = dp
            centre = centre + jnp.sum(probs * dp, 0, keepdims=True)
            dv_scr[rows, :] = dv_scr[rows, :] + jnp.dot(
                probs.astype(BF), grads, preferred_element_type=F32
            )
        dq = jnp.zeros((width, block), F32)
        for t in range(last + 1):
            rows = pl.ds(t * block, block)
            ds = (prob_scr[rows, :] * (dp_scr[rows, :] - centre)).astype(BF)
            dk_scr[rows, :] = dk_scr[rows, :] + jnp.dot(ds, queries, preferred_element_type=F32)
            dq = dq + jnp.dot(kt_ref[:, rows], ds, preferred_element_type=F32)
        result = jnp.where(mine, (dq * (HD**-0.5)).T, 0.0)

        @pl.when(head == 0)
        def _():
            dq_scr[...] = result

        @pl.when(head > 0)
        def _():
            dq_scr[...] = dq_scr[...] + result

    for last in range(k_ref.shape[0] // block):
        pl.when(number == last)(functools.partial(one_block, last))

    @pl.when(head == pl.num_programs(1) - 1)
    def _():
        dq_ref[...] = dq_scr[...].astype(BF)

    @pl.when((head == pl.num_programs(1) - 1) & (number == pl.num_programs(0) - 1))
    def _():
        dk_ref[...] = dk_scr[...].astype(BF)
        dv_ref[...] = dv_scr[...].astype(BF)


def attend_back(slopes, queries, keys, keys_t, values, grads, lse):
    length, width = queries.shape
    heads = slopes.shape[0]
    block = min(256, length)
    whole = lambda i, h: (0, 0)
    down = lambda i, h: (i, 0)
    return pl.pallas_call(
        attend_back_kernel,
        grid=(length // block, heads),
        in_specs=[
            pl.BlockSpec(memory_space=pltpu.SMEM),
            pl.BlockSpec((block, width), down),
            pl.BlockSpec((length, width), whole),
            pl.BlockSpec((width, length), whole),
            pl.BlockSpec((length, width), whole),
            pl.BlockSpec((block, width), down),
            pl.BlockSpec((1, 1, block), lambda i, h: (h, 0, i)),
        ],
        out_specs=[
            pl.BlockSpec((block, width), down),
            pl.BlockSpec((length, width), whole),
            pl.BlockSpec((length, width), whole),
        ],
        out_shape=[jax.ShapeDtypeStruct((length, width), BF)] * 3,
        scratch_shapes=[
            pltpu.VMEM((length, block), F32),
            pltpu.VMEM((length, block), F32),
            pltpu.VMEM((length, width), F32),
            pltpu.VMEM((length, width), F32),
            pltpu.VMEM((block, width), F32),
        ],
        compiler_params=pltpu.CompilerParams(vmem_limit_bytes=VMEM_BYTES),
        cost_estimate=pl.CostEstimate(
            flops=20 * heads * length * length * HD,
            bytes_accessed=16 * length * width,
            transcendentals=heads * length * length // 2,
        ),
        name="attend_back",
    )(slopes, queries, keys, keys_t, values, grads, lse)


def body(
    hidden_in,
    norm1_gain,
    norm1_bias,
    qkv_weight,
    qv_bias,
    alibi_slopes,
    out_weight,
    out_bias,
    norm2_gain,
    norm2_bias,
    up_weight,
    up_bias,
    down_weight,
    down_bias,
    out_grad,
):
    seq_devices = lax.axis_size(SEQ)
    fsdp_devices = lax.axis_size(FSDP)
    devices = seq_devices * fsdp_devices
    z_size, y_size, x_size = lax.axis_size("z"), lax.axis_size("fy"), lax.axis_size("fx")
    sequences, local_len, model_width = hidden_in.shape
    tokens = sequences * local_len
    heads_local = H // seq_devices
    width = heads_local * HD
    ff_width = up_weight.shape[1]
    rows_each = qkv_weight.shape[0]
    ff_each = down_weight.shape[0]
    up_blocks = ff_width // model_width
    place = lax.axis_index(SEQ)
    slopes = lax.dynamic_slice_in_dim(alibi_slopes, place * heads_local, heads_local)

    up_stack = up_weight.reshape(rows_each, up_blocks, model_width).transpose(1, 0, 2)
    stacked = jnp.concatenate(
        [out_weight, down_weight, up_stack.reshape(up_blocks * rows_each, model_width)], 0
    )
    along_z = lax.all_gather(stacked, "z", axis=0, tiled=False)
    cut = rows_each + ff_each
    low_part, up_part = along_z[:, :cut], along_z[:, cut:]
    up_part = gather_axis(gather_axis(gather_axis(up_part, "fx"), "fy"), "core")
    low_part = gather_axis(gather_axis(gather_axis(low_part, "fy"), "fx"), "core")
    up_part = up_part.reshape(2, y_size, x_size, z_size, up_blocks, rows_each, model_width)
    w_up = up_part.transpose(3, 0, 1, 2, 5, 4, 6).reshape(model_width, ff_width)
    low_part = low_part.transpose(3, 0, 2, 1, 4, 5)
    w_out = low_part[:, :, :, :, :rows_each].reshape(model_width, model_width)
    w_down = low_part[:, :, :, :, rows_each:].reshape(ff_width, model_width)

    small_parts = (norm1_gain, norm1_bias, qv_bias, out_bias, norm2_gain, norm2_bias, up_bias, down_bias)
    small_all = lax.all_gather(jnp.concatenate(small_parts), ALL, axis=0, tiled=False)
    full, start = [], 0
    for part in small_parts:
        size = part.shape[0]
        full.append(small_all[:, start : start + size].reshape(-1).astype(F32))
        start += size
    first_gain, first_shift, bias_qv, b_out, second_gain, second_shift, b_up, b_down = full

    columns = qkv_weight.reshape(rows_each, 3, seq_devices, width).transpose(2, 0, 1, 3)
    columns = columns.reshape(seq_devices, rows_each, 3 * width)
    columns = lax.all_to_all(columns, SEQ, split_axis=0, concat_axis=0, tiled=True)
    w_heads = lax.all_gather(columns, FSDP, axis=1, tiled=False).reshape(model_width, 3 * width)
    bias_parts = bias_qv.reshape(2, seq_devices, width)
    bias_mine = lax.dynamic_index_in_dim(bias_parts, place, 1, keepdims=False)
    bias_heads = jnp.concatenate([bias_mine[0], jnp.zeros((width,), F32), bias_mine[1]])

    kept = []
    returned = []
    for n in range(sequences):
        rows = lax.all_gather(hidden_in[n], SEQ, axis=0, tiled=True)
        first_low, q, k, v, kt, vt = project(
            rows, first_gain[None], first_shift[None], w_heads, bias_heads[None]
        )
        attended, lse = attend(slopes, q, k, vt)
        returned.append(lax.all_to_all(attended, SEQ, split_axis=0, concat_axis=1, tiled=True))
        kept.append((first_low, q, k, v, kt, lse))
    attended_low = jnp.stack(returned).reshape(tokens, model_width)

    flat_in = hidden_in.reshape(tokens, model_width).astype(F32)
    middle = flat_in + jnp.dot(attended_low, w_out, preferred_element_type=F32) + b_out
    second_norm, second_back = jax.vjp(layer_norm, middle, second_gain, second_shift)
    second_low = second_norm.astype(BF)
    hidden_pre = jnp.dot(second_low, w_up, preferred_element_type=F32) + b_up
    activated, gelu_back = jax.vjp(gelu_tanh, hidden_pre)
    activated_low = activated.astype(BF)
    result = middle + jnp.dot(activated_low, w_down, preferred_element_type=F32) + b_down
    block_out = result.astype(BF).reshape(sequences, local_len, model_width)

    cot_low = out_grad.reshape(tokens, model_width)
    cotangent = cot_low.astype(F32)
    grad_act = times_rows(cot_low, w_down)
    (grad_pre,) = gelu_back(grad_act)
    grad_hidden = grad_pre.astype(BF)
    grad_second = times_rows(grad_hidden, w_up)
    grad_mid_norm, grad_gain_two, grad_shift_two = second_back(grad_second)
    grad_middle = cotangent + grad_mid_norm
    grad_branch = grad_middle.astype(BF)
    grad_attended = times_rows(grad_branch, w_out).astype(BF)
    grad_attended = grad_attended.reshape(sequences, local_len, model_width)
    grad_heads = [
        lax.all_to_all(grad_attended[n], SEQ, split_axis=1, concat_axis=0, tiled=True)
        for n in range(sequences)
    ]

    grad_down = outer_sum(activated_low, cot_low).astype(BF)
    grad_up = outer_sum(second_low, grad_hidden).astype(BF)
    grad_outw = outer_sum(attended_low, grad_branch).astype(BF)

    split = (z_size, 2, y_size, x_size)
    sum_down = grad_down.reshape(*split, ff_each, model_width)
    sum_down = reduce_axis(reduce_axis(reduce_axis(sum_down, "core", 1), "fx", 2), "fy", 1)
    sum_up = grad_up.reshape(*split, rows_each, ff_width)
    sum_up = reduce_axis(reduce_axis(reduce_axis(sum_up, "core", 1), "fy", 1), "fx", 1)
    sum_out = grad_outw.reshape(*split, rows_each, model_width)
    sum_out = reduce_axis(reduce_axis(reduce_axis(sum_out, "core", 1), "fx", 2), "fy", 1)
    sum_up = sum_up.reshape(z_size, rows_each, up_blocks, model_width).transpose(0, 2, 1, 3)
    sum_up = sum_up.reshape(z_size, up_blocks * rows_each, model_width)
    sums = lax.psum_scatter(
        jnp.concatenate([sum_out, sum_down, sum_up], 1), "z", scatter_dimension=0, tiled=False
    ).astype(F32)
    out_outw = sums[:rows_each]
    out_down = sums[rows_each:cut]
    out_up = sums[cut:].reshape(up_blocks, rows_each, model_width).transpose(1, 0, 2)
    out_up = out_up.reshape(rows_each, ff_width)

    rear = [
        jnp.sum(grad_branch.astype(F32), 0),
        grad_gain_two,
        grad_shift_two,
        jnp.sum(grad_hidden.astype(F32), 0),
        jnp.sum(cotangent, 0),
    ]
    rear_wide = jnp.concatenate([part.reshape(devices, -1) for part in rear], 1)
    rear_sum = jnp.sum(lax.all_to_all(rear_wide, ALL, split_axis=0, concat_axis=0, tiled=True), 0)

    grad_qkvw = jnp.zeros((model_width, 3 * width), F32)
    column_sums = jnp.zeros((3 * width,), F32)
    grad_first = []
    for n in range(sequences):
        first_low, q, k, v, kt, lse = kept[n]
        dq, dk, dv = attend_back(slopes, q, k, kt, v, grad_heads[n], lse)
        grad_projected = jnp.concatenate([dq, dk, dv], 1)
        partial = times_rows(grad_projected, w_heads).astype(BF)
        grad_first.append(lax.psum_scatter(partial, SEQ, scatter_dimension=0, tiled=True))
        grad_qkvw = grad_qkvw + outer_sum(first_low, grad_projected)
        column_sums = column_sums + jnp.sum(grad_projected.astype(F32), 0)
    grad_first = jnp.stack(grad_first).reshape(tokens, model_width).astype(F32)
    _, first_back = jax.vjp(layer_norm, flat_in, first_gain, first_shift)
    grad_in_norm, grad_gain_one, grad_shift_one = first_back(grad_first)
    input_grad = (grad_middle + grad_in_norm).reshape(sequences, local_len, model_width)

    wide = grad_qkvw.reshape(seq_devices, fsdp_devices, rows_each, 3 * width)
    wide = lax.psum_scatter(wide, FSDP, scatter_dimension=1, tiled=False)
    wide = lax.all_to_all(wide, SEQ, split_axis=0, concat_axis=0, tiled=True)
    wide = wide.reshape(seq_devices, rows_each, 3, width).transpose(1, 2, 0, 3)
    out_qkvw = wide.reshape(rows_each, 3 * model_width)

    qv_here = jnp.zeros((2, seq_devices, width), F32)
    qv_mine = jnp.stack([column_sums[:width], column_sums[2 * width :]])
    qv_here = lax.dynamic_update_slice_in_dim(qv_here, qv_mine[:, None], place, 1)
    front = [grad_gain_one, grad_shift_one, qv_here.reshape(-1)]
    front_wide = jnp.concatenate([part.reshape(devices, -1) for part in front], 1)
    front_sum = jnp.sum(lax.all_to_all(front_wide, ALL, split_axis=0, concat_axis=0, tiled=True), 0)

    r = rows_each
    return (
        block_out,
        input_grad,
        front_sum[:r],
        front_sum[r : 2 * r],
        out_qkvw,
        front_sum[2 * r :],
        out_outw,
        rear_sum[:r],
        rear_sum[r : 2 * r],
        rear_sum[2 * r : 3 * r],
        out_up,
        rear_sum[3 * r : 3 * r + ff_each],
        out_down,
        rear_sum[3 * r + ff_each :],
    )


def solution(mesh):
    seq_size, fsdp_size = mesh.shape["seq"], mesh.shape["fsdp"]
    fine = Mesh(mesh.devices.reshape(seq_size // 2, 2, fsdp_size // 2, 2), ALL)
    tokens = P(FSDP, SEQ, None)
    vector = P(ALL)
    matrix = P(ALL, None)
    return jax.shard_map(
        body,
        mesh=fine,
        in_specs=(
            tokens, vector, vector, matrix, vector, P(), matrix, vector, vector, vector,
            matrix, vector, matrix, vector, tokens,
        ),
        out_specs=(
            tokens, tokens, vector, vector, matrix, vector, matrix, vector, vector, vector,
            matrix, vector, matrix, vector,
        ),
        check_vma=False,
    )
```

time: 1780 us -> 753 us (0.42)
  waiting for transfers between devices: 975 us -> 262 us
  matrix products: 345 us -> 83.1 us
  other arithmetic: 168 us -> 73.9 us
  Pallas kernels: 0 us -> 89.6 us
  blocking collectives: 163 us -> 77.9 us
  starting transfers between devices: 18.1 us -> 48.2 us
    reduce_scatter x4 -> x3, waiting for transfers between devices: 768 us -> 0.01 us  [the longest x2 0.01 us: body(): lax.psum_scatter(partial, SEQ, scatter_dimension=0, tiled=True)]
    dot_general x36 -> x8, matrix products: 305 us -> 54.3 us  [the longest x5 23.7 us: times_rows(): return lax.dot_general(left, right, NT, preferred_element_type=F32)]
    ppermute x0 -> x15, waiting for transfers between devices: none -> 156 us  [swap(): return lax.ppermute(values, axis, [(0, 1), (1, 0)])]
    all_to_all x4 -> x8, waiting for transfers between devices: 187 us -> 53.7 us  [the longest x1 21 us: body(): wide = lax.all_to_all(wide, SEQ, split_axis=0, concat_axis=0, tiled=True)]
    pallas_call x0 -> x6, Pallas kernels: none -> 89.6 us  [the longest x2 44.8 us: attend_back(): pl.pallas_call(attend_back_kernel, grid=(length // block, heads), in_spec...]
    unnamed x2 -> x0, blocking collectives: 83.8 us -> none
    convert_element_type x23 -> x13, other arithmetic: 67.8 us -> 18.9 us  [the longest x9 16.8 us: reduce_axis(): return (keep.astype(F32) + swap(give, axis).astype(F32)).astype(BF)]
    reduce_sum x7 -> x6, other arithmetic: 47 us -> 2.78 us  [the longest x2 2.05 us: body(): column_sums = column_sums + jnp.sum(grad_projected.astype(F32), 0)]
  transfers between devices with their start and end apart: 12 -> 30, of which waited for: 7 -> 14; matrix products, arithmetic and copies ran while one was open for 32% -> 20% of each run, Pallas kernels for 0% -> 9%
where the time goes in v1:
time: 753 us; the launch traced here: 743 us
  waiting for transfers between devices  262 us (35%)
  local copies, waits for them, and re-layouts  93.3 us (12%)
  Pallas kernels  89.6 us (12%)
  matrix products  83.1 us (11%)
  blocking collectives  77.9 us (10%)
  other arithmetic  73.9 us (10%)
  starting transfers between devices  48.2 us (6%)
  between operations  15.5 us (2%)
    ppermute x15, waiting for transfers between devices, swap(): return lax.ppermute(values, axis, [(0, 1), (1, 0)])  156 us
    all_gather x1, blocking collectives, body(): lax.all_gather(jnp.concatenate(small_parts), ALL, axis=0, tiled=False)  68 us
    all_gather x1, waiting for transfers between devices, body(): along_z = lax.all_gather(stacked, 'z', axis=0, tiled=False)  52.2 us
    pallas_call x2, Pallas kernels, attend_back(): pl.pallas_call(attend_back_kernel, grid=(length // block, heads), in_spec...  44.8 us
    unnamed x136, local copies, waits for them, and re-layouts  38.1 us
    pallas_call x2, Pallas kernels, attend(): pl.pallas_call(attend_kernel, grid=(length // block, heads), in_specs=[pl...  29.6 us
    dot_general x5, matrix products, outer_sum(): lax.dot_general(left, right, (((0,), (0,)), ((), ())), preferred_element_...  28.9 us
    another operation x10, other arithmetic, gather_axis(): jnp.stack([jnp.where(first, values, other), jnp.where(first, other, value...  24.1 us
  transfers between devices with their start and end apart: 30, of which 14 were waited for; matrix products, arithmetic and copies ran while one was open for 20% of the time, Pallas kernels for 9%

profile of v1, /device:TPU:0, one launch (start us, length us, event | category | flops | bytes accessed | tf_op | source)
XLA Modules:
  0.0 743.4 jit_solution(9343285188935737678)
XLA Ops:
  11.3 52.2 %all-gather.14.cloned.1.call-done = bf16[1152,1024]{1,0:T(8,128)(2,1)} async-done(((bf16[288,1024]{1,0:T(8,128)(2,1)}), bf16[1152,1024]{1,0:T(8,128)(2,1)}) %all-gather.14.cloned.1.call-update) | async-done | bytes 2359312 | tf_op jit(solution)/shard_map/all_gather | solution.py:340
  71.3 19.7 %collective-permute-done.3 = bf16[4,128,1024]{2,1,0:T(8,128)(2,1)} collective-permute-done((bf16[4,128,1024]{2,1,0:T(8,128)(2,1)}, bf16[4,128,1024]{2,1,0:T(8,128)(2,1)}, u32[]{:S(2)}, u32[]{:S(2)}) %collective-permute-start.3) | collective-permute-done | bytes 1048608 | tf_op jit(solution)/shard_map/ppermute | solution.py:43
  104.2 41.0 %collective-permute-done.4 = bf16[2,4,128,1024]{3,2,1,0:T(8,128)(2,1)S(1)} collective-permute-done((bf16[2,4,128,1024]{3,2,1,0:T(8,128)(2,1)S(1)}, bf16[2,4,128,1024]{3,2,1,0:T(8,128)(2,1)S(1)}, u32[]{:S(2)}, u32[]{:S(2)}) %collective-permute-start.4) | collective-permute-done | bytes 2097184 | tf_op jit(solution)/shard_map/ppermute | solution.py:43
  148.7 10.8 %collective-permute-done.1 = bf16[2,4,160,1024]{3,2,0,1:T(8,128)(2,1)S(1)} collective-permute-done((bf16[2,4,160,1024]{3,2,0,1:T(8,128)(2,1)S(1)}, bf16[2,4,160,1024]{3,2,0,1:T(8,128)(2,1)S(1)}, u32[]{:S(2)}, u32[]{:S(2)}) %collective-permute-start.1) | collective-permute-done | bytes 2621472 | tf_op jit(solution)/shard_map/ppermute | solution.py:43
  168.4 68.0 %all-gather.5 = bf16[32,1,384]{2,1,0:T(2,128)(2,1)S(1)} all-gather(bf16[1,1,384]{2,1,0:T(2,128)(2,1)S(1)} %reshape.432), channel_id=3, replica_groups=mesh['z'=4,'core'=2,'fy'=2,'fx'=2] {'z','core','fy','fx'}, dimensions={0}, use_global_device_ids=true | all-gather | bytes 25344 | tf_op jit(solution)/shard_map/all_gather | solution.py:352
  237.5 9.9 %all-gather.2 = bf16[8,128,384]{2,1,0:T(8,128)(2,1)S(1)} all-gather(bf16[8,32,384]{2,1,0:T(8,128)(2,1)S(1)} %all-to-all-done), channel_id=4, replica_groups=mesh['z'=4,'core'=2,'fy'=2,'fx'=2] {'fy','fx'}, dimensions={1}, use_global_device_ids=true | all-gather | bytes 983040 | tf_op jit(solution)/shard_map/all_gather | solution.py:363
  255.8 14.8 %attend.3 = (bf16[2048,128]{1,0:T(8,128)(2,1)S(1)}, f32[2,1,2048]{2,1,0:T(1,128)S(1)}) custom-call(f32[2]{0:T(128)S(1)} %dynamic_slice.70.slope_ref, bf16[2048,128]{1,0:T(8,128)(2,1)S(1)} %get-tuple-element.40.q_ref, bf16[2048,128]{1,0:T(8,128)(2,1)S(1)} %get-tuple-element.41.k_ref, bf16[128,2048]{1,0:T(8,128)(2,1)S(1)} %get-tuple-element.42.vt_ref), custom_call_target="tpu_custom_call" | custom-call | flops 4294967296 | bytes 2097152 | tf_op jit(solution)/shard_map/attend/pallas_call | solution.py:174
  283.8 14.8 %attend.2 = (bf16[2048,128]{1,0:T(8,128)(2,1)S(1)}, f32[2,1,2048]{2,1,0:T(1,128)S(1)}) custom-call(f32[2]{0:T(128)S(1)} %dynamic_slice.70.slope_ref, bf16[2048,128]{1,0:T(8,128)(2,1)S(1)} %get-tuple-element.36.q_ref, bf16[2048,128]{1,0:T(8,128)(2,1)S(1)} %get-tuple-element.37.k_ref, bf16[128,2048]{1,0:T(8,128)(2,1)S(1)} %get-tuple-element.38.vt_ref), custom_call_target="tpu_custom_call" | custom-call | flops 4294967296 | bytes 2097152 | tf_op jit(solution)/shard_map/attend/pallas_call | solution.py:174
  305.5 15.0 %all-to-all-done.1 = bf16[8,256,128]{1,2,0:T(8,128)(2,1)S(1)} async-done(((bf16[8,256,128]{1,2,0:T(8,128)(2,1)}), bf16[8,256,128]{1,2,0:T(8,128)(2,1)S(1)}, u32[]{:S(2)}, u32[]{:S(2)}) %all-to-all-start.1) | async-done | bytes 524320 | tf_op jit(solution)/shard_map/all_to_all | solution.py:376
  342.1 12.4 %copy.133 = bf16[128,8,4,1024]{3,1,2,0:T(8,128)(2,1)} copy(bf16[128,8,4,1024]{3,2,1,0:T(4,128)(2,1)} %bitcast.260) | data formatting | bytes 16777216
  362.0 9.0 %maximum_bitcast_fusion = bf16[4,2,2,2,160,1024]{5,4,3,2,1,0:T(8,128)(2,1)} fusion(bf16[1,2,2,4,160,1024]{5,4,1,2,0,3:T(8,128)(2,1)} %get-tuple-element.73, bf16[1,2,2,4,160,1024]{5,4,1,2,0,3:T(8,128)(2,1)} %get-tuple-element.72), kind=kLoop, calls=%fused_computation.4 | loop fusion | flops 5242880 | bytes 20971520 | tf_op jit(solution)/shard_map/transpose | solution.py:347
  372.8 8.3 %slice.147 = bf16[4,2,2,2,128,1024]{5,4,3,2,1,0:T(8,128)(2,1)} slice(bf16[4,2,2,2,160,1024]{5,4,3,2,1,0:T(8,128)(2,1)} %maximum_bitcast_fusion), slice={[0:4], [0:2], [0:2], [0:2], [32:160], [0:1024]} | slice | bytes 16777216 | tf_op jit(solution)/shard_map/slice | solution.py:349
  392.3 16.8 %convert_reduce_fusion = (f32[4096]{0:T(1024)S(1)}, bf16[512,4096]{1,0:T(8,128)(2,1)}, f32[512,4096]{1,0:T(8,128)}) fusion(f32[4096]{0:T(1024)S(1)} %fusion.35, f32[4096,512]{0,1:T(8,128)} %fusion.51, bf16[1024,4096]{1,0:T(8,128)(2,1)S(1)} %bitcast.275, f32[512,1024]{1,0:T(8,128)S(1)} %get-tuple-element.116, f32[1024]{0:T(1024)S(1)} %reshape.412, ...), kind=kOutput, calls=%fused_computation.22 | convolution fusion | flops 4354207744 | bytes 31502336 | tf_op jit(solution)/shard_map/dot_general | solution.py:384
  424.1 14.4 %all-to-all-done.4 = bf16[256,8,128]{2,0,1:T(8,128)(2,1)S(1)} async-done(((bf16[256,8,128]{2,0,1:T(8,128)(2,1)}), bf16[256,8,128]{2,0,1:T(8,128)(2,1)S(1)}, u32[]{:S(2)}, u32[]{:S(2)}) %all-to-all-start.4) | async-done | bytes 524320 | tf_op jit(solution)/shard_map/all_to_all | solution.py:402
  445.1 22.4 %attend_back.3 = (bf16[2048,128]{1,0:T(8,128)(2,1)S(1)}, bf16[2048,128]{1,0:T(8,128)(2,1)S(1)}, bf16[2048,128]{1,0:T(8,128)(2,1)S(1)}) custom-call(f32[2]{0:T(128)S(1)} %dynamic_slice.70.slope_ref, bf16[2048,128]{1,0:T(8,128)(2,1)S(1)} %get-tuple-element.40.q_ref, bf16[2048,128]{1,0:T(8,128)(2,1)S(1)} %copy-done.1, bf16[128,2048]{1,0:T(8,128)(2,1)S(1)} %copy-done.5, ...), custom_call_target="tpu_custom_call" | custom-call | flops 10737418240 | bytes 4194304 | tf_op jit(solution)/shard_map/attend_back/pallas_call | solution.py:269
  472.6 22.4 %attend_back.2 = (bf16[2048,128]{1,0:T(8,128)(2,1)S(1)}, bf16[2048,128]{1,0:T(8,128)(2,1)S(1)}, bf16[2048,128]{1,0:T(8,128)(2,1)S(1)}) custom-call(f32[2]{0:T(128)S(1)} %dynamic_slice.70.slope_ref, bf16[2048,128]{1,0:T(8,128)(2,1)S(1)} %copy-done.7, bf16[2048,128]{1,0:T(8,128)(2,1)S(1)} %copy-done.9, bf16[128,2048]{1,0:T(8,128)(2,1)S(1)} %copy-done.13, ...), custom_call_target="tpu_custom_call" | custom-call | flops 10737418240 | bytes 4194304 | tf_op jit(solution)/shard_map/attend_back/pallas_call | solution.py:269
  510.1 7.8 %convolution_convert_fusion = bf16[1024,4096]{1,0:T(8,128)(2,1)S(1)} fusion(bf16[512,4096]{1,0:T(8,128)(2,1)} %get-tuple-element.67, f32[512,1024]{1,0:T(8,128)} %copy-done.30, f32[1024]{0:T(1024)S(1)} %reshape.412, f32[1024]{0:T(1024)S(1)} %reshape.411, f32[512]{0:T(512)S(1)} %fusion.36, f32[512]{0:T(512)S(1)} %broadcast_multiply_fusion.1), kind=kOutput, calls=%fused_computation.24 | convolution fusion | flops 4301783040 | bytes 14692352 | tf_op jit(solution)/shard_map/dot_general | solution.py:35
  522.9 13.4 %convolution_convert_fusion.1 = bf16[4096,1024]{1,0:T(8,128)(2,1)} fusion(bf16[512,1024]{1,0:T(8,128)(2,1)S(1)} %bitcast.268, f32[512,4096]{1,0:T(8,128)} %get-tuple-element.117, f32[4096]{0:T(1024)S(1)} %fusion.35), kind=kOutput, calls=%fused_computation.25 | convolution fusion | flops 4320133120 | bytes 17842176 | tf_op jit(solution)/shard_map/dot_general | solution.py:35
  583.4 24.3 %collective-permute-done.13 = bf16[4,2,32,4096]{3,2,1,0:T(8,128)(2,1)} collective-permute-done((bf16[4,2,32,4096]{3,2,1,0:T(8,128)(2,1)}, bf16[4,2,32,4096]{3,2,1,0:T(8,128)(2,1)}, u32[]{:S(2)}, u32[]{:S(2)}) %collective-permute-start.13) | collective-permute-done | bytes 2097184 | tf_op jit(solution)/shard_map/ppermute | solution.py:43
  611.8 26.5 %collective-permute-done.7 = bf16[4,2,32,1024]{3,2,0,1:T(8,128)(2,1)S(1)} collective-permute-done((bf16[4,2,32,1024]{3,2,0,1:T(8,128)(2,1)S(1)}, bf16[4,2,32,1024]{3,2,0,1:T(8,128)(2,1)S(1)}, u32[]{:S(2)}, u32[]{:S(2)}) %collective-permute-start.7) | collective-permute-done | bytes 524320 | tf_op jit(solution)/shard_map/ppermute | solution.py:43
  647.9 12.2 %collective-permute-done.14 = bf16[4,32,4096]{2,1,0:T(8,128)(2,1)S(1)} collective-permute-done((bf16[4,32,4096]{2,1,0:T(8,128)(2,1)S(1)}, bf16[4,32,4096]{2,1,0:T(8,128)(2,1)S(1)}, u32[]{:S(2)}, u32[]{:S(2)}) %collective-permute-start.14) | collective-permute-done | bytes 1048608 | tf_op jit(solution)/shard_map/ppermute | solution.py:43
  660.4 7.7 %collective-permute-done.11 = bf16[4,128,1024]{2,1,0:T(8,128)(2,1)S(1)} collective-permute-done((bf16[4,128,1024]{2,1,0:T(8,128)(2,1)S(1)}, bf16[4,128,1024]{2,1,0:T(8,128)(2,1)S(1)}, u32[]{:S(2)}, u32[]{:S(2)}) %collective-permute-start.11) | collective-permute-done | bytes 1048608 | tf_op jit(solution)/shard_map/ppermute | solution.py:43
  671.9 12.3 %add_convert_fusion = bf16[512,1024]{1,0:T(8,128)(2,1)} fusion(f32[512,1024]{1,0:T(8,128)S(1)} %copy-done.31, bf16[4096,1024]{1,0:T(8,128)(2,1)} %bitcast.269, f32[1024]{0:T(1024)S(1)} %reshape.414, f32[512,4096]{1,0:T(8,128)} %get-tuple-element.117, f32[4096]{0:T(1024)S(1)} %fusion.35), kind=kOutput, calls=%fused_computation.83 | convolution fusion | flops 4317511680 | bytes 19943424 | tf_op jit(solution)/shard_map/dot_general | solution.py:387
  692.4 21.0 %all-to-all-done.6 = f32[8,32,384]{2,1,0:T(8,128)S(1)} async-done(((f32[8,32,384]{2,1,0:T(8,128)}), f32[8,32,384]{2,1,0:T(8,128)S(1)}, u32[]{:S(2)}, u32[]{:S(2)}) %all-to-all-start.6) | async-done | bytes 393248 | tf_op jit(solution)/shard_map/all_to_all | solution.py:455
  (318 shorter events, 250.6 us)
Async XLA Ops:
  7.2 56.3 %all-gather.14.cloned.1.call-start = ((), (), s32[]{:S(2)}) async-start(), calls=%async_computation.17 | async-start | bytes 2949120 | tf_op jit(solution)/shard_map/all_gather | solution.py:340
  10.1 237.3 %all-gather.12.cloned.1.call-start = ((), (), s32[]{:S(2)}) async-start(), calls=%async_computation.16 | async-start | bytes 4718592 | tf_op jit(solution)/shard_map/all_gather | solution.py:371
  11.2 264.2 %all-gather.10.cloned.1.call-start = ((), (), s32[]{:S(2)}) async-start(), calls=%async_computation.15 | async-start | bytes 4718592 | tf_op jit(solution)/shard_map/all_gather | solution.py:371
  69.8 32.0 %collective-permute-start = (bf16[4,160,1024]{2,1,0:T(8,128)(2,1)}, bf16[4,160,1024]{2,1,0:T(8,128)(2,1)}, u32[]{:S(2)}, u32[]{:S(2)}) collective-permute-start(bf16[4,160,1024]{2,1,0:T(8,128)(2,1)} %slice.140), channel_id=1, source_target_pairs={{0,2},{2,0},{1,3},{3,1},{4,6},{6,4},{5,7},{7,5},{8,10},{10,8},{9,1... | collective-permute-start | bytes 3932168 | tf_op jit(solution)/shard_map/ppermute | solution.py:43
  92.6 52.5 %collective-permute-start.4 = (bf16[2,4,128,1024]{3,2,1,0:T(8,128)(2,1)S(1)}, bf16[2,4,128,1024]{3,2,1,0:T(8,128)(2,1)S(1)}, u32[]{:S(2)}, u32[]{:S(2)}) collective-permute-start(bf16[2,4,128,1024]{3,2,1,0:T(8,128)(2,1)S(1)} %pad_maximum_fusion.5), channel_id=1, source_target_pairs={{0,2},{2,0},{1,3},{3,1},{4,6},{6,4},{5,7},{7,5},{8,10},{10,8},{9,1... | collective-permute-start | bytes 6291464 | tf_op jit(solution)/shard_map/ppermute | solution.py:43
  103.6 56.0 %collective-permute-start.1 = (bf16[2,4,160,1024]{3,2,0,1:T(8,128)(2,1)S(1)}, bf16[2,4,160,1024]{3,2,0,1:T(8,128)(2,1)S(1)}, u32[]{:S(2)}, u32[]{:S(2)}) collective-permute-start(bf16[2,4,160,1024]{3,2,0,1:T(8,128)(2,1)S(1)} %pad_maximum_fusion.3), channel_id=1, source_target_pairs={{0,1},{1,0},{2,3},{3,2},{4,5},{5,4},{6,7},{7,6},{8,9},{9,8},{10,11... | collective-permute-start | bytes 7864328 | tf_op jit(solution)/shard_map/ppermute | solution.py:43
  148.7 175.2 %collective-permute-start.5 = (bf16[2,2,4,128,1024]{4,3,2,1,0:T(8,128)(2,1)}, bf16[2,2,4,128,1024]{4,3,2,1,0:T(8,128)(2,1)}, u32[]{:S(2)}, u32[]{:S(2)}) collective-permute-start(bf16[2,2,4,128,1024]{4,3,2,1,0:T(8,128)(2,1)} %pad_maximum_fusion.2), channel_id=1, source_target_pairs={{0,4},{4,0},{1,5},{5,1},{2,6},{6,2},{3,7},{7,3},{8,12},{12,8},{9,1... | collective-permute-start | bytes 12582920 | tf_op jit(solution)/shard_map/ppermute | solution.py:43
  163.8 190.7 %collective-permute-start.2 = (bf16[2,2,4,160,1024]{4,3,0,1,2:T(8,128)(2,1)}, bf16[2,2,4,160,1024]{4,3,0,1,2:T(8,128)(2,1)}, u32[]{:S(2)}, u32[]{:S(2)}) collective-permute-start(bf16[2,2,4,160,1024]{4,3,0,1,2:T(8,128)(2,1)} %pad_maximum_fusion.1), channel_id=1, source_target_pairs={{0,4},{4,0},{1,5},{5,1},{2,6},{6,2},{3,7},{7,3},{8,12},{12,8},{9,1... | collective-permute-start | bytes 15728648 | tf_op jit(solution)/shard_map/ppermute | solution.py:43
  164.8 72.7 %all-to-all-start = ((bf16[8,32,384]{2,1,0:T(8,128)(2,1)}), bf16[8,32,384]{2,1,0:T(8,128)(2,1)S(1)}, u32[]{:S(2)}, u32[]{:S(2)}) async-start(bf16[8,32,384]{2,1,0:T(8,128)(2,1)} %reshape.378), calls=%async_computation | async-start | bytes 393216 | tf_op jit(solution)/shard_map/all_to_all | solution.py:362
  271.7 27.9 %all-to-all-start.2 = ((bf16[8,256,128]{1,2,0:T(8,128)(2,1)}), bf16[8,256,128]{1,2,0:T(8,128)(2,1)S(1)}, u32[]{:S(2)}, u32[]{:S(2)}) async-start(bf16[8,256,128]{1,2,0:T(8,128)(2,1)} %copy.104), calls=%async_computation.2 | async-start | bytes 1048576 | tf_op jit(solution)/shard_map/all_to_all | solution.py:376
  438.5 30.0 %all-to-all-start.3 = ((bf16[256,8,128]{2,0,1:T(8,128)(2,1)}), bf16[256,8,128]{2,0,1:T(8,128)(2,1)S(1)}, u32[]{:S(2)}, u32[]{:S(2)}) async-start(bf16[256,8,128]{2,0,1:T(8,128)(2,1)} %bitcast.247), calls=%async_computation.3 | async-start | bytes 1048576 | tf_op jit(solution)/shard_map/all_to_all | solution.py:402
  442.0 243.5 %reduce-scatter.13.cloned.1.call-start = ((), (), s32[]{:S(2)}) async-start(), calls=%async_computation.18 | async-start | bytes 1966080
  504.6 210.0 %reduce-scatter.7.cloned.1.call-start = ((), (), s32[]{:S(2)}) async-start(), calls=%async_computation.12 | async-start | bytes 4718592 | tf_op jit(solution)/shard_map/reduce_scatter | solution.py:445
  509.6 205.0 %reduce-scatter.9.cloned.1.call-start = ((), (), s32[]{:S(2)}) async-start(), calls=%async_computation.13 | async-start | bytes 4718592 | tf_op jit(solution)/shard_map/reduce_scatter | solution.py:445
  522.6 28.1 %collective-permute-start.12 = (bf16[4,2,2,32,4096]{4,3,2,1,0:T(8,128)(2,1)}, bf16[4,2,2,32,4096]{4,3,2,1,0:T(8,128)(2,1)}, u32[]{:S(2)}, u32[]{:S(2)}) collective-permute-start(bf16[4,2,2,32,4096]{4,3,2,1,0:T(8,128)(2,1)} %dynamic-slice_bitcast_fusion), channel_id=1, source_target_pairs={{0,4},{4,0},{1,5},{5,1},{2,6},{6,2},{3,7},{7,3},{8,12},{12,8},{9,1... | collective-permute-start | bytes 12582920 | tf_op jit(solution)/shard_map/ppermute | solution.py:43
  546.1 26.5 %collective-permute-start.9 = (bf16[4,2,2,128,1024]{4,3,0,1,2:T(8,128)(2,1)}, bf16[4,2,2,128,1024]{4,3,0,1,2:T(8,128)(2,1)}, u32[]{:S(2)}, u32[]{:S(2)}) collective-permute-start(bf16[4,2,2,128,1024]{4,3,0,1,2:T(8,128)(2,1)} %bitcast.243), channel_id=1, source_target_pairs={{0,4},{4,0},{1,5},{5,1},{2,6},{6,2},{3,7},{7,3},{8,12},{12,8},{9,1... | collective-permute-start | bytes 12582920 | tf_op jit(solution)/shard_map/ppermute | solution.py:43
  559.3 48.4 %collective-permute-start.13 = (bf16[4,2,32,4096]{3,2,1,0:T(8,128)(2,1)}, bf16[4,2,32,4096]{3,2,1,0:T(8,128)(2,1)}, u32[]{:S(2)}, u32[]{:S(2)}) collective-permute-start(bf16[4,2,32,4096]{3,2,1,0:T(8,128)(2,1)} %dynamic-slice_bitcast_fusion.1), channel_id=1, source_target_pairs={{0,2},{2,0},{1,3},{3,1},{4,6},{6,4},{5,7},{7,5},{8,10},{10,8},{9,1... | collective-permute-start | bytes 6291464 | tf_op jit(solution)/shard_map/ppermute | solution.py:43
  567.7 116.5 %all-to-all-start.7 = ((f32[32,1,256]{2,1,0:T(1,128)}), f32[32,1,256]{2,1,0:T(1,128)S(1)}, u32[]{:S(2)}, u32[]{:S(2)}) async-start(f32[32,1,256]{2,1,0:T(1,128)} %all_to_all.88), calls=%async_computation.10 | async-start | bytes 65536 | tf_op jit(solution)/shard_map/all_to_all | solution.py:435
  572.5 160.2 %reduce-scatter.11.cloned.1.call-start = ((), (), s32[]{:S(2)}) async-start(), calls=%async_computation.14 | async-start | bytes 2949120 | tf_op jit(solution)/shard_map/reduce_scatter | solution.py:419
  578.5 61.9 %collective-permute-start.10 = (bf16[4,2,128,1024]{3,2,0,1:T(8,128)(2,1)S(1)}, bf16[4,2,128,1024]{3,2,0,1:T(8,128)(2,1)S(1)}, u32[]{:S(2)}, u32[]{:S(2)}) collective-permute-start(bf16[4,2,128,1024]{3,2,0,1:T(8,128)(2,1)S(1)} %dynamic-slice_bitcast_fusion.2), channel_id=1, source_target_pairs={{0,1},{1,0},{2,3},{3,2},{4,5},{5,4},{6,7},{7,6},{8,9},{9,8},{10,11... | collective-permute-start | bytes 6291464 | tf_op jit(solution)/shard_map/ppermute | solution.py:43
  582.0 56.2 %collective-permute-start.7 = (bf16[4,2,32,1024]{3,2,0,1:T(8,128)(2,1)S(1)}, bf16[4,2,32,1024]{3,2,0,1:T(8,128)(2,1)S(1)}, u32[]{:S(2)}, u32[]{:S(2)}) collective-permute-start(bf16[4,2,32,1024]{3,2,0,1:T(8,128)(2,1)S(1)} %dynamic-slice_bitcast_fusion.5), channel_id=1, source_target_pairs={{0,1},{1,0},{2,3},{3,2},{4,5},{5,4},{6,7},{7,6},{8,9},{9,8},{10,11... | collective-permute-start | bytes 1572872 | tf_op jit(solution)/shard_map/ppermute | solution.py:43
  610.3 49.8 %collective-permute-start.14 = (bf16[4,32,4096]{2,1,0:T(8,128)(2,1)S(1)}, bf16[4,32,4096]{2,1,0:T(8,128)(2,1)S(1)}, u32[]{:S(2)}, u32[]{:S(2)}) collective-permute-start(bf16[4,32,4096]{2,1,0:T(8,128)(2,1)S(1)} %dynamic-slice_bitcast_fusion.3), channel_id=1, source_target_pairs={{0,1},{1,0},{2,3},{3,2},{4,5},{5,4},{6,7},{7,6},{8,9},{9,8},{10,11... | collective-permute-start | bytes 3145736 | tf_op jit(solution)/shard_map/ppermute | solution.py:43
  641.5 26.6 %collective-permute-start.11 = (bf16[4,128,1024]{2,1,0:T(8,128)(2,1)S(1)}, bf16[4,128,1024]{2,1,0:T(8,128)(2,1)S(1)}, u32[]{:S(2)}, u32[]{:S(2)}) collective-permute-start(bf16[4,128,1024]{2,1,0:T(8,128)(2,1)S(1)} %dynamic-slice_bitcast_fusion.4), channel_id=1, source_target_pairs={{0,2},{2,0},{1,3},{3,1},{4,6},{6,4},{5,7},{7,5},{8,10},{10,8},{9,1... | collective-permute-start | bytes 3145736 | tf_op jit(solution)/shard_map/ppermute | solution.py:43
  685.4 28.0 %all-to-all-start.6 = ((f32[8,32,384]{2,1,0:T(8,128)}), f32[8,32,384]{2,1,0:T(8,128)S(1)}, u32[]{:S(2)}, u32[]{:S(2)}) async-start(f32[8,32,384]{2,1,0:T(8,128)} %bitcast.302), calls=%async_computation.8 | async-start | bytes 786432 | tf_op jit(solution)/shard_map/all_to_all | solution.py:455
  (67 other events, 602.5 us)
Sparse Core Ops, SparseCore 0:
  10.2 53.1 all-gather.13
  65.6 45.9 all-gather.11
  113.8 45.8 all-gather.9
  504.7 31.4 reduce-scatter.12
  538.4 50.5 reduce-scatter.6
  591.1 48.1 reduce-scatter.8
  670.4 55.1 reduce-scatter.10

commit v2 on v1

--- a/solution.py
+++ b/solution.py
@@ -43,21 +43,143 @@
     return lax.ppermute(values, axis, [(0, 1), (1, 0)])
 
 
-def gather_axis(values, axis):
+def after(values, *earlier):
+    return lax.optimization_barrier((values, *earlier))[0]
+
+
+def merge_pair(mine, other, axis, position):
+    shape = [1] * (mine.ndim + 1)
+    shape[position] = 2
+    slot = jnp.arange(2).reshape(shape)
+    return jnp.where(
+        slot == lax.axis_index(axis), jnp.expand_dims(mine, position), jnp.expand_dims(other, position)
+    )
+
+
+def send_axis(values, axis, position):
     if lax.axis_size(axis) != 2:
-        return lax.all_gather(values, axis, axis=0, tiled=False)
-    other = swap(values, axis)
-    first = lax.axis_index(axis) == 0
-    return jnp.stack([jnp.where(first, values, other), jnp.where(first, other, values)])
-
-
-def reduce_axis(values, axis, position):
+        return lax.all_gather(values, axis, axis=position, tiled=False)
+    return swap(values, axis)
+
+
+def join_axis(values, other, axis, position):
     if lax.axis_size(axis) != 2:
-        return lax.psum_scatter(values, axis, scatter_dimension=position, tiled=False)
+        return other
+    return merge_pair(values, other, axis, position)
+
+
+def at_index(values, index, position):
+    return lax.dynamic_index_in_dim(values, index, position, keepdims=False)
+
+
+def total_of(terms):
+    total = terms[0].astype(F32)
+    for term in terms[1:]:
+        total = total + term.astype(F32)
+    return total
+
+
+def reduce_axis(terms, axis, position):
+    if lax.axis_size(axis) != 2:
+        whole = total_of(terms).astype(BF)
+        return [lax.psum_scatter(whole, axis, scatter_dimension=position, tiled=False)]
     me = lax.axis_index(axis)
-    give = lax.dynamic_index_in_dim(values, 1 - me, position, keepdims=False)
-    keep = lax.dynamic_index_in_dim(values, me, position, keepdims=False)
-    return (keep.astype(F32) + swap(give, axis).astype(F32)).astype(BF)
+    give = total_of([at_index(term, 1 - me, position) for term in terms]).astype(BF)
+    return [at_index(term, me, position) for term in terms] + [swap(give, axis)]
+
+
+def feed_kernel(
+    me_ref, own_ref, oth_ref, cot_ref, up_own_ref, up_oth_ref, down_own_ref, down_oth_ref, bias_ref,
+    y_ref, gs_own_ref, gs_oth_ref, gd_own_ref, gd_oth_ref, gu_own_ref, gu_oth_ref, gb_ref,
+    own_t, oth_t,
+):
+    step = pl.program_id(0)
+    half = pl.num_programs(0) // 2
+
+    @pl.when(step == 0)
+    def _():
+        own_t[...] = own_ref[...].astype(F32).T.astype(BF)
+        oth_t[...] = oth_ref[...].astype(F32).T.astype(BF)
+        y_ref[...] = jnp.zeros_like(y_ref)
+        gs_own_ref[...] = jnp.zeros_like(gs_own_ref)
+        gs_oth_ref[...] = jnp.zeros_like(gs_oth_ref)
+
+    def one(down_ref, gd_ref):
+        down = down_ref[0]
+        pre = jnp.dot(own_ref[...], up_own_ref[...], preferred_element_type=F32)
+        pre = pre + jnp.dot(oth_ref[...], up_oth_ref[...], preferred_element_type=F32)
+        pre = pre + bias_ref[...]
+        square = pre * pre
+        tanh = jnp.tanh(0.7978845608 * (pre + 0.044715 * pre * square))
+        near = 0.5 * (1.0 + tanh)
+        active = (pre * near).astype(BF)
+        slope = near + 0.5 * pre * (1.0 - tanh * tanh) * (
+            0.7978845608 * (1.0 + 3.0 * 0.044715 * square)
+        )
+        grad = lax.dot_general(cot_ref[...], down, NT, preferred_element_type=F32) * slope
+        grad = grad.astype(BF)
+        y_ref[...] = y_ref[...] + jnp.dot(active, down, preferred_element_type=F32)
+        gd_ref[0] = outer_sum(active, cot_ref[...]).astype(BF)
+        gu_own_ref[...] = jnp.dot(own_t[...], grad, preferred_element_type=F32).astype(BF)
+        gu_oth_ref[...] = jnp.dot(oth_t[...], grad, preferred_element_type=F32).astype(BF)
+        gb_ref[...] = jnp.sum(grad.astype(F32), 0, keepdims=True)
+        gs_own_ref[...] = gs_own_ref[...] + times_rows(grad, up_own_ref[...])
+        gs_oth_ref[...] = gs_oth_ref[...] + times_rows(grad, up_oth_ref[...])
+
+    @pl.when(step < half)
+    def _():
+        one(down_own_ref, gd_own_ref)
+
+    @pl.when(step >= half)
+    def _():
+        one(down_oth_ref, gd_oth_ref)
+
+
+def feed(me, own, oth, cot, up_own, up_oth, down_own, down_oth, bias):
+    tokens, half_width = own.shape
+    model_width = cot.shape[1]
+    ff_width = up_own.shape[1]
+    z_size, block, _ = down_own.shape
+
+    def column(j, me_ref):
+        mine = me_ref[0]
+        return (0, (j % z_size) * 2 + jnp.where(j < z_size, mine, 1 - mine))
+
+    whole = lambda j, me_ref: (0, 0)
+    first = lambda j, me_ref: (jnp.minimum(j, z_size - 1), 0, 0)
+    second = lambda j, me_ref: (jnp.maximum(j - z_size, 0), 0, 0)
+    halves = [pl.BlockSpec((tokens, half_width), whole)] * 2
+    columns = [pl.BlockSpec((half_width, block), column)] * 2
+    downs = [pl.BlockSpec((1, block, model_width), first), pl.BlockSpec((1, block, model_width), second)]
+    line = pl.BlockSpec((1, block), column)
+    all_rows = pl.BlockSpec((tokens, model_width), whole)
+    return pl.pallas_call(
+        feed_kernel,
+        grid_spec=pltpu.PrefetchScalarGridSpec(
+            num_scalar_prefetch=1,
+            grid=(2 * z_size,),
+            in_specs=[*halves, all_rows, *columns, *downs, line],
+            out_specs=[all_rows, *halves, *downs, *columns, line],
+            scratch_shapes=[pltpu.VMEM((half_width, tokens), BF)] * 2,
+        ),
+        out_shape=[
+            jax.ShapeDtypeStruct((tokens, model_width), F32),
+            jax.ShapeDtypeStruct((tokens, half_width), F32),
+            jax.ShapeDtypeStruct((tokens, half_width), F32),
+            jax.ShapeDtypeStruct(down_own.shape, BF),
+            jax.ShapeDtypeStruct(down_own.shape, BF),
+            jax.ShapeDtypeStruct(up_own.shape, BF),
+            jax.ShapeDtypeStruct(up_own.shape, BF),
+            jax.ShapeDtypeStruct((1, ff_width), F32),
+        ],
+        compiler_params=pltpu.CompilerParams(vmem_limit_bytes=VMEM_BYTES),
+        cost_estimate=pl.CostEstimate(
+            flops=12 * tokens * model_width * ff_width,
+            bytes_accessed=8 * model_width * ff_width + 12 * tokens * model_width,
+            transcendentals=tokens * ff_width,
+        ),
+        name="feed",
+    )(me, own, oth, cot, up_own, up_oth, down_own, down_oth, bias)
 
 
 def project_kernel(x_ref, gain_ref, shift_ref, w_ref, bias_ref, low_ref, q_ref, k_ref, v_ref, kt_ref, vt_ref):
@@ -329,27 +451,27 @@
     ff_width = up_weight.shape[1]
     rows_each = qkv_weight.shape[0]
     ff_each = down_weight.shape[0]
-    up_blocks = ff_width // model_width
     place = lax.axis_index(SEQ)
     slopes = lax.dynamic_slice_in_dim(alibi_slopes, place * heads_local, heads_local)
 
-    up_stack = up_weight.reshape(rows_each, up_blocks, model_width).transpose(1, 0, 2)
-    stacked = jnp.concatenate(
-        [out_weight, down_weight, up_stack.reshape(up_blocks * rows_each, model_width)], 0
+    me = lax.axis_index("core")
+
+    def split(values):
+        values = values.reshape(tokens, z_size, 2, -1)
+        return (
+            at_index(values, me, 2).reshape(tokens, -1),
+            at_index(values, 1 - me, 2).reshape(tokens, -1),
+        )
+
+    def unsplit(own, oth):
+        own, oth = own.reshape(tokens, z_size, -1), oth.reshape(tokens, z_size, -1)
+        return merge_pair(own, oth, "core", 2).reshape(tokens, -1)
+
+    small_parts = (norm1_gain, norm1_bias, qv_bias, out_bias, norm2_gain, norm2_bias, up_bias, down_bias)
+    small_here = jnp.concatenate(small_parts)
+    small_all = lax.all_to_all(
+        jnp.broadcast_to(small_here, (devices, small_here.shape[0])), ALL, split_axis=0, concat_axis=0, tiled=True
     )
-    along_z = lax.all_gather(stacked, "z", axis=0, tiled=False)
-    cut = rows_each + ff_each
-    low_part, up_part = along_z[:, :cut], along_z[:, cut:]
-    up_part = gather_axis(gather_axis(gather_axis(up_part, "fx"), "fy"), "core")
-    low_part = gather_axis(gather_axis(gather_axis(low_part, "fy"), "fx"), "core")
-    up_part = up_part.reshape(2, y_size, x_size, z_size, up_blocks, rows_each, model_width)
-    w_up = up_part.transpose(3, 0, 1, 2, 5, 4, 6).reshape(model_width, ff_width)
-    low_part = low_part.transpose(3, 0, 2, 1, 4, 5)
-    w_out = low_part[:, :, :, :, :rows_each].reshape(model_width, model_width)
-    w_down = low_part[:, :, :, :, rows_each:].reshape(ff_width, model_width)
-
-    small_parts = (norm1_gain, norm1_bias, qv_bias, out_bias, norm2_gain, norm2_bias, up_bias, down_bias)
-    small_all = lax.all_gather(jnp.concatenate(small_parts), ALL, axis=0, tiled=False)
     full, start = [], 0
     for part in small_parts:
         size = part.shape[0]
@@ -365,10 +487,27 @@
     bias_mine = lax.dynamic_index_in_dim(bias_parts, place, 1, keepdims=False)
     bias_heads = jnp.concatenate([bias_mine[0], jnp.zeros((width,), F32), bias_mine[1]])
 
+    orders = (("fx", "fy"), ("fy", "fx"), ("fy", "fx"))
+    along_z = [
+        lax.all_gather(weight, "z", axis=0, tiled=False) for weight in (up_weight, down_weight, out_weight)
+    ]
+    along_z = [after(weight, w_heads, small_all) for weight in along_z]
+    sent = [send_axis(w, order[0], 1) for w, order in zip(along_z, orders)]
+    pairs = [join_axis(w, o, order[0], 1) for w, o, order in zip(along_z, sent, orders)]
+    second_place = [1 if order[1] == "fy" else 2 for order in orders]
+    sent = [send_axis(w, order[1], at) for w, order, at in zip(pairs, orders, second_place)]
+
     kept = []
     returned = []
     for n in range(sequences):
         rows = lax.all_gather(hidden_in[n], SEQ, axis=0, tiled=True)
+        if n == sequences - 1:
+            sent = [after(o, kept[0][-1]) if kept else o for o in sent]
+            mine = [
+                join_axis(w, o, order[1], at)
+                for w, o, order, at in zip(pairs, sent, orders, second_place)
+            ]
+            theirs = [swap(w, "core") for w in mine]
         first_low, q, k, v, kt, vt = project(
             rows, first_gain[None], first_shift[None], w_heads, bias_heads[None]
         )
@@ -376,59 +515,58 @@
         returned.append(lax.all_to_all(attended, SEQ, split_axis=0, concat_axis=1, tiled=True))
         kept.append((first_low, q, k, v, kt, lse))
     attended_low = jnp.stack(returned).reshape(tokens, model_width)
+    half_width = model_width // 2
+    up_own, up_oth = (w.reshape(half_width, ff_width) for w in (mine[0], theirs[0]))
+    down_own, down_oth = (w.reshape(z_size, -1, model_width) for w in (mine[1], theirs[1]))
+    out_own, out_oth = (w.reshape(half_width, model_width) for w in (mine[2], theirs[2]))
 
     flat_in = hidden_in.reshape(tokens, model_width).astype(F32)
-    middle = flat_in + jnp.dot(attended_low, w_out, preferred_element_type=F32) + b_out
+    att_own, att_oth = split(attended_low)
+    middle = (
+        flat_in
+        + jnp.dot(att_own, out_own, preferred_element_type=F32)
+        + jnp.dot(att_oth, out_oth, preferred_element_type=F32)
+        + b_out
+    )
     second_norm, second_back = jax.vjp(layer_norm, middle, second_gain, second_shift)
-    second_low = second_norm.astype(BF)
-    hidden_pre = jnp.dot(second_low, w_up, preferred_element_type=F32) + b_up
-    activated, gelu_back = jax.vjp(gelu_tanh, hidden_pre)
-    activated_low = activated.astype(BF)
-    result = middle + jnp.dot(activated_low, w_down, preferred_element_type=F32) + b_down
-    block_out = result.astype(BF).reshape(sequences, local_len, model_width)
-
+    second_own, second_oth = split(second_norm.astype(BF))
     cot_low = out_grad.reshape(tokens, model_width)
     cotangent = cot_low.astype(F32)
-    grad_act = times_rows(cot_low, w_down)
-    (grad_pre,) = gelu_back(grad_act)
-    grad_hidden = grad_pre.astype(BF)
-    grad_second = times_rows(grad_hidden, w_up)
+    y, gs_own, gs_oth, gd_own, gd_oth, gu_own, gu_oth, grad_up_bias = feed(
+        me.reshape(1), second_own, second_oth, cot_low, up_own, up_oth, down_own, down_oth, b_up[None]
+    )
+    block_out = (middle + y + b_down).astype(BF).reshape(sequences, local_len, model_width)
+
+    cells = (z_size, y_size, x_size)
+    to_up = gu_own.reshape(*cells, rows_each, ff_width)
+    to_down = gd_own.reshape(*cells, ff_each, model_width)
+    sum_up = [to_up, swap(gu_oth, "core").reshape(to_up.shape)]
+    sum_down = [to_down, swap(gd_oth, "core").reshape(to_down.shape)]
+
+    grad_second = unsplit(gs_own, gs_oth)
     grad_mid_norm, grad_gain_two, grad_shift_two = second_back(grad_second)
     grad_middle = cotangent + grad_mid_norm
     grad_branch = grad_middle.astype(BF)
-    grad_attended = times_rows(grad_branch, w_out).astype(BF)
+    grad_attended = unsplit(
+        times_rows(grad_branch, out_own).astype(BF), times_rows(grad_branch, out_oth).astype(BF)
+    )
     grad_attended = grad_attended.reshape(sequences, local_len, model_width)
     grad_heads = [
         lax.all_to_all(grad_attended[n], SEQ, split_axis=1, concat_axis=0, tiled=True)
         for n in range(sequences)
     ]
-
-    grad_down = outer_sum(activated_low, cot_low).astype(BF)
-    grad_up = outer_sum(second_low, grad_hidden).astype(BF)
-    grad_outw = outer_sum(attended_low, grad_branch).astype(BF)
-
-    split = (z_size, 2, y_size, x_size)
-    sum_down = grad_down.reshape(*split, ff_each, model_width)
-    sum_down = reduce_axis(reduce_axis(reduce_axis(sum_down, "core", 1), "fx", 2), "fy", 1)
-    sum_up = grad_up.reshape(*split, rows_each, ff_width)
-    sum_up = reduce_axis(reduce_axis(reduce_axis(sum_up, "core", 1), "fy", 1), "fx", 1)
-    sum_out = grad_outw.reshape(*split, rows_each, model_width)
-    sum_out = reduce_axis(reduce_axis(reduce_axis(sum_out, "core", 1), "fx", 2), "fy", 1)
-    sum_up = sum_up.reshape(z_size, rows_each, up_blocks, model_width).transpose(0, 2, 1, 3)
-    sum_up = sum_up.reshape(z_size, up_blocks * rows_each, model_width)
-    sums = lax.psum_scatter(
-        jnp.concatenate([sum_out, sum_down, sum_up], 1), "z", scatter_dimension=0, tiled=False
-    ).astype(F32)
-    out_outw = sums[:rows_each]
-    out_down = sums[rows_each:cut]
-    out_up = sums[cut:].reshape(up_blocks, rows_each, model_width).transpose(1, 0, 2)
-    out_up = out_up.reshape(rows_each, ff_width)
+    go_own = outer_sum(att_own, grad_branch).astype(BF).reshape(*cells, rows_each, model_width)
+    go_oth = outer_sum(att_oth, grad_branch).astype(BF)
+    sum_out = [go_own, swap(go_oth, "core").reshape(go_own.shape)]
+    sum_up = reduce_axis(sum_up, "fy", 1)
+    sum_down = reduce_axis(sum_down, "fx", 2)
+    sum_out = reduce_axis(sum_out, "fx", 2)
 
     rear = [
         jnp.sum(grad_branch.astype(F32), 0),
         grad_gain_two,
         grad_shift_two,
-        jnp.sum(grad_hidden.astype(F32), 0),
+        grad_up_bias,
         jnp.sum(cotangent, 0),
     ]
     rear_wide = jnp.concatenate([part.reshape(devices, -1) for part in rear], 1)
@@ -440,21 +578,35 @@
     for n in range(sequences):
         first_low, q, k, v, kt, lse = kept[n]
         dq, dk, dv = attend_back(slopes, q, k, kt, v, grad_heads[n], lse)
+        if n == sequences - 1:
+            sum_up, sum_down, sum_out = (
+                terms[:-1] + [after(terms[-1], dq)] for terms in (sum_up, sum_down, sum_out)
+            )
+            sum_up = reduce_axis(sum_up, "fx", 1)
+            sum_down = reduce_axis(sum_down, "fy", 1)
+            sum_out = reduce_axis(sum_out, "fy", 1)
         grad_projected = jnp.concatenate([dq, dk, dv], 1)
         partial = times_rows(grad_projected, w_heads).astype(BF)
         grad_first.append(lax.psum_scatter(partial, SEQ, scatter_dimension=0, tiled=True))
         grad_qkvw = grad_qkvw + outer_sum(first_low, grad_projected)
         column_sums = column_sums + jnp.sum(grad_projected.astype(F32), 0)
+
+    wide = [grad_qkvw.reshape(seq_devices, y_size, x_size, rows_each, 3 * width)]
+    wide = total_of(reduce_axis(reduce_axis(wide, "fy", 1), "fx", 1))
+    wide = lax.all_to_all(wide, SEQ, split_axis=0, concat_axis=0, tiled=True)
+    wide = wide.reshape(seq_devices, rows_each, 3, width).transpose(1, 2, 0, 3)
+    out_qkvw = wide.reshape(rows_each, 3 * model_width)
+
+    low_sum = jnp.concatenate([total_of(sum_out).astype(BF), total_of(sum_down).astype(BF)], 1)
+    low_sum = lax.psum_scatter(low_sum, "z", scatter_dimension=0, tiled=False).astype(F32)
+    out_outw, out_down = low_sum[:rows_each], low_sum[rows_each:]
+    out_up = total_of(sum_up).astype(BF)
+    out_up = lax.psum_scatter(out_up, "z", scatter_dimension=0, tiled=False).astype(F32)
+
     grad_first = jnp.stack(grad_first).reshape(tokens, model_width).astype(F32)
     _, first_back = jax.vjp(layer_norm, flat_in, first_gain, first_shift)
     grad_in_norm, grad_gain_one, grad_shift_one = first_back(grad_first)
     input_grad = (grad_middle + grad_in_norm).reshape(sequences, local_len, model_width)
-
-    wide = grad_qkvw.reshape(seq_devices, fsdp_devices, rows_each, 3 * width)
-    wide = lax.psum_scatter(wide, FSDP, scatter_dimension=1, tiled=False)
-    wide = lax.all_to_all(wide, SEQ, split_axis=0, concat_axis=0, tiled=True)
-    wide = wide.reshape(seq_devices, rows_each, 3, width).transpose(1, 2, 0, 3)
-    out_qkvw = wide.reshape(rows_each, 3 * model_width)
 
     qv_here = jnp.zeros((2, seq_devices, width), F32)
     qv_mine = jnp.stack([column_sums[:width], column_sums[2 * width :]])

time: 753 us -> 648 us (0.86)
  matrix products: 83.1 us -> 28.3 us
  waiting for transfers between devices: 262 us -> 220 us
  Pallas kernels: 89.6 us -> 124 us
  blocking collectives: 77.9 us -> 45.5 us
  local copies, waits for them, and re-layouts: 93.3 us -> 76.3 us
    ppermute x15 -> x20, waiting for transfers between devices: 156 us -> 87.1 us  [swap(): return lax.ppermute(values, axis, [(0, 1), (1, 0)])]
    all_gather x1, blocking collectives: 68 us -> 16.1 us  [body(): lax.all_gather(weight, 'z', axis=0, tiled=False)]
    all_gather x1 -> x2, waiting for transfers between devices: 52.2 us -> 16.5 us  [body(): lax.all_gather(weight, 'z', axis=0, tiled=False)]
    pallas_call x0 -> x1, Pallas kernels: none -> 35.2 us  [feed(): pl.pallas_call(feed_kernel, grid_spec=pltpu.PrefetchScalarGridSpec(num_sc...]
    all_to_all x1, waiting for transfers between devices: 0.01 us -> 35.1 us  [body(): lax.all_to_all(rear_wide, ALL, split_axis=0, concat_axis=0, tiled=True)]
    dot_general x3 -> x2, matrix products: 30.6 us -> 2.89 us  [the longest x1 2.14 us: body(): jnp.dot(att_oth, out_oth, preferred_element_type=F32)]
    another operation x10 -> x0, other arithmetic: 24.1 us -> none  [gather_axis(): jnp.stack([jnp.where(first, values, other), jnp.where(first, other, value...]
    select_n x1 -> x10, other arithmetic: 3.69 us -> 26.3 us  [merge_pair(): jnp.where(slot == lax.axis_index(axis), jnp.expand_dims(mine, position),...]
  transfers between devices with their start and end apart: 30 -> 36, of which waited for: 14 -> 16; matrix products, arithmetic and copies ran while one was open for 20% -> 20% of each run, Pallas kernels for 9% -> 10%
where the time goes in v2:
time: 648 us; the launch traced here: 639 us
  waiting for transfers between devices  220 us (34%)
  Pallas kernels  124 us (19%)
  other arithmetic  79.6 us (12%)
  local copies, waits for them, and re-layouts  76.3 us (12%)
  starting transfers between devices  48.7 us (8%)
  blocking collectives  45.5 us (7%)
  matrix products  28.3 us (4%)
  between operations  15.7 us (2%)
    ppermute x20, waiting for transfers between devices, swap(): return lax.ppermute(values, axis, [(0, 1), (1, 0)])  87.1 us
    pallas_call x2, Pallas kernels, attend_back(): pl.pallas_call(attend_back_kernel, grid=(length // block, heads), in_spec...  44.3 us
    pallas_call x1, Pallas kernels, feed(): pl.pallas_call(feed_kernel, grid_spec=pltpu.PrefetchScalarGridSpec(num_sc...  35.2 us
    all_to_all x1, waiting for transfers between devices, body(): lax.all_to_all(rear_wide, ALL, split_axis=0, concat_axis=0, tiled=True)  35.1 us
    pallas_call x2, Pallas kernels, attend(): pl.pallas_call(attend_kernel, grid=(length // block, heads), in_specs=[pl...  29.7 us
    select_n x10, other arithmetic, merge_pair(): jnp.where(slot == lax.axis_index(axis), jnp.expand_dims(mine, position),...  26.3 us
    all_to_all x1, waiting for transfers between devices, body(): lax.all_to_all(grad_attended[n], SEQ, split_axis=1, concat_axis=0, tiled=...  23.5 us
    unnamed x147, local copies, waits for them, and re-layouts  21.5 us
  transfers between devices with their start and end apart: 36, of which 16 were waited for; matrix products, arithmetic and copies ran while one was open for 20% of the time, Pallas kernels for 10%

profile of v2, /device:TPU:0, one launch (start us, length us, event | category | flops | bytes accessed | tf_op | source)
XLA Modules:
  0.0 638.8 jit_solution(2584840114685416183)
XLA Ops:
  13.9 7.3 %all-to-all-start = ((bf16[32,2,192]{2,1,0:T(2,128)(2,1)}), bf16[32,2,192]{2,1,0:T(2,128)(2,1)S(1)}, u32[]{:S(2)}, u32[]{:S(2)}) async-start(bf16[32,2,192]{2,1,0:T(2,128)(2,1)} %reshape.612), calls=%async_computation | async-start | bytes 65536 | tf_op jit(solution)/shard_map/all_to_all | solution.py:472
  22.2 6.7 %all-to-all-done = bf16[32,2,192]{2,1,0:T(2,128)(2,1)S(1)} async-done(((bf16[32,2,192]{2,1,0:T(2,128)(2,1)}), bf16[32,2,192]{2,1,0:T(2,128)(2,1)S(1)}, u32[]{:S(2)}, u32[]{:S(2)}) %all-to-all-start) | async-done | bytes 24608 | tf_op jit(solution)/shard_map/all_to_all | solution.py:472
  32.4 12.9 %all-to-all-done.1 = bf16[8,32,384]{2,1,0:T(8,128)(2,1)S(1)} async-done(((bf16[8,32,384]{2,1,0:T(8,128)(2,1)}), bf16[8,32,384]{2,1,0:T(8,128)(2,1)S(1)}, u32[]{:S(2)}, u32[]{:S(2)}) %all-to-all-start.1) | async-done | bytes 196640 | tf_op jit(solution)/shard_map/all_to_all | solution.py:484
  45.3 11.2 %all-gather.1 = bf16[8,128,384]{2,1,0:T(8,128)(2,1)S(1)} all-gather(bf16[8,32,384]{2,1,0:T(8,128)(2,1)S(1)} %all-to-all-done.1), channel_id=3, replica_groups=mesh['z'=4,'core'=2,'fy'=2,'fx'=2] {'fy','fx'}, dimensions={1}, use_global_device_ids=true | all-gather | bytes 983040 | tf_op jit(solution)/shard_map/all_gather | solution.py:485
  57.7 16.5 %all-gather.15.cloned.1.call-done = bf16[128,4096]{1,0:T(8,128)(2,1)} async-done(((bf16[32,4096]{1,0:T(8,128)(2,1)}), bf16[128,4096]{1,0:T(8,128)(2,1)}) %all-gather.15.cloned.1.call-update) | async-done | bytes 1048592 | tf_op jit(solution)/shard_map/all_gather | solution.py:492
  84.2 16.3 %collective-permute-done.3 = bf16[4,32,4096]{2,1,0:T(8,128)(2,1)S(1)} collective-permute-done((bf16[4,32,4096]{2,1,0:T(8,128)(2,1)}, bf16[4,32,4096]{2,1,0:T(8,128)(2,1)S(1)}, u32[]{:S(2)}, u32[]{:S(2)}) %collective-permute-start.3) | collective-permute-done | bytes 1048608 | tf_op jit(solution)/shard_map/ppermute | solution.py:43
  104.0 19.0 %all-gather.11.cloned.1.call-done = bf16[1,2048,1024]{2,1,0:T(8,128)(2,1)} async-done(((bf16[1,256,1024]{2,1,0:T(8,128)(2,1)}), bf16[1,2048,1024]{2,1,0:T(8,128)(2,1)}) %all-gather.11.cloned.1.call-update) | async-done | bytes 4194320 | tf_op jit(solution)/shard_map/all_gather | solution.py:503
  123.1 7.5 %project.2 = (bf16[2048,1024]{1,0:T(8,128)(2,1)}, bf16[2048,128]{1,0:T(8,128)(2,1)S(1)}, bf16[2048,128]{1,0:T(8,128)(2,1)S(1)}, bf16[2048,128]{1,0:T(8,128)(2,1)...) custom-call(bf16[2048,1024]{1,0:T(8,128)(2,1)} %bitcast.284, f32[1,1024]{1,0:T(1,128)S(1)} %reshape.586.gain_ref, ...), custom_call_target="tpu_custom_call" | custom-call | flops 1610612736 | bytes 11010048 | tf_op jit(solution)/shard_map/project/pallas_call | solution.py:206
  132.2 14.8 %attend.2 = (bf16[2048,128]{1,0:T(8,128)(2,1)S(1)}, f32[2,1,2048]{2,1,0:T(1,128)S(1)}) custom-call(f32[2]{0:T(128)S(1)} %dynamic_slice.123.slope_ref, bf16[2048,128]{1,0:T(8,128)(2,1)S(1)} %get-tuple-element.53.q_ref, bf16[2048,128]{1,0:T(8,128)(2,1)S(1)} %get-tuple-element.54.k_ref, bf16[128,2048]{1,0:T(8,128)(2,1)S(1)} %get-tuple-element.55.vt_ref), custom_call_target="tpu_custom_call" | custom-call | flops 4294967296 | bytes 2097152 | tf_op jit(solution)/shard_map/attend/pallas_call | solution.py:296
  157.0 16.1 %all-gather.3 = bf16[128,1024]{1,0:T(8,128)(2,1)S(1)} all-gather(bf16[32,1024]{1,0:T(8,128)(2,1)S(1)} %copy-done.51), channel_id=5, replica_groups=mesh['z'=4,'core'=2,'fy'=2,'fx'=2] {'z'}, dimensions={0}, use_global_device_ids=true | all-gather | bytes 327680 | tf_op jit(solution)/shard_map/all_gather | solution.py:492
  181.1 7.6 %project.3 = (bf16[2048,1024]{1,0:T(8,128)(2,1)}, bf16[2048,128]{1,0:T(8,128)(2,1)S(1)}, bf16[2048,128]{1,0:T(8,128)(2,1)S(1)}, bf16[2048,128]{1,0:T(8,128)(2,1)...) custom-call(bf16[2048,1024]{1,0:T(8,128)(2,1)} %bitcast.283, f32[1,1024]{1,0:T(1,128)S(1)} %reshape.586.gain_ref, ...), custom_call_target="tpu_custom_call" | custom-call | flops 1610612736 | bytes 11010048 | tf_op jit(solution)/shard_map/project/pallas_call | solution.py:206
  189.5 14.8 %attend.3 = (bf16[2048,128]{1,0:T(8,128)(2,1)S(1)}, f32[2,1,2048]{2,1,0:T(1,128)S(1)}) custom-call(f32[2]{0:T(128)S(1)} %dynamic_slice.123.slope_ref, bf16[2048,128]{1,0:T(8,128)(2,1)S(1)} %get-tuple-element.57.q_ref, bf16[2048,128]{1,0:T(8,128)(2,1)S(1)} %get-tuple-element.58.k_ref, bf16[128,2048]{1,0:T(8,128)(2,1)S(1)} %get-tuple-element.59.vt_ref), custom_call_target="tpu_custom_call" | custom-call | flops 4294967296 | bytes 2097152 | tf_op jit(solution)/shard_map/attend/pallas_call | solution.py:296
  205.4 4.9 all-to-all-start.3
  256.1 35.2 %feed.1 = (f32[512,1024]{1,0:T(8,128)}, f32[512,512]{1,0:T(8,128)S(1)}, f32[512,512]{1,0:T(8,128)S(1)}, bf16[4,512,1024]{2,1,0:T(8,128)(2,1)}, bf16[4,512,1024]{...) custom-call(s32[1]{0:T(128)} %bitcast.18.me_ref, ...), custom_call_target="tpu_custom_call" | custom-call | flops 25769803776 | bytes 39845888 | tf_op jit(solution)/shard_map/feed/pallas_call | solution.py:156
  326.0 18.2 %all_to_all.107 = bf16[256,8,128]{2,0,1:T(8,128)(2,1)S(1)} all-to-all(bf16[256,8,128]{2,0,1:T(8,128)(2,1)S(1)} %bitcast.249), channel_id=1, replica_groups=mesh['z'=4,'core'=2,'fy'=2,'fx'=2] {'z','core'}, dimensions={1} | all-to-all | bytes 1048576 | tf_op jit(solution)/shard_map/all_to_all | solution.py:555
  344.2 22.1 %attend_back.2 = (bf16[2048,128]{1,0:T(8,128)(2,1)S(1)}, bf16[2048,128]{1,0:T(8,128)(2,1)S(1)}, bf16[2048,128]{1,0:T(8,128)(2,1)S(1)}) custom-call(f32[2]{0:T(128)S(1)} %dynamic_slice.123.slope_ref, bf16[2048,128]{1,0:T(8,128)(2,1)S(1)} %copy-done.6, bf16[2048,128]{1,0:T(8,128)(2,1)S(1)} %copy-done.8, bf16[128,2048]{1,0:T(8,128)(2,1)S(1)} %copy-done.12, ...), custom_call_target="tpu_custom_call" | custom-call | flops 10737418240 | bytes 4194304 | tf_op jit(solution)/shard_map/attend_back/pallas_call | solution.py:391
  378.0 23.5 %all-to-all-done.5 = bf16[256,8,128]{2,0,1:T(8,128)(2,1)S(1)} async-done(((bf16[256,8,128]{2,0,1:T(8,128)(2,1)}), bf16[256,8,128]{2,0,1:T(8,128)(2,1)S(1)}, u32[]{:S(2)}, u32[]{:S(2)}) %all-to-all-start.5) | async-done | bytes 524320 | tf_op jit(solution)/shard_map/all_to_all | solution.py:555
  404.6 22.2 %attend_back.3 = (bf16[2048,128]{1,0:T(8,128)(2,1)S(1)}, bf16[2048,128]{1,0:T(8,128)(2,1)S(1)}, bf16[2048,128]{1,0:T(8,128)(2,1)S(1)}) custom-call(f32[2]{0:T(128)S(1)} %dynamic_slice.123.slope_ref, bf16[2048,128]{1,0:T(8,128)(2,1)S(1)} %copy-done.14, bf16[2048,128]{1,0:T(8,128)(2,1)S(1)} %copy-done.16, bf16[128,2048]{1,0:T(8,128)(2,1)S(1)} %copy-done.20, ...), custom_call_target="tpu_custom_call" | custom-call | flops 10737418240 | bytes 4194304 | tf_op jit(solution)/shard_map/attend_back/pallas_call | solution.py:391
  450.9 35.1 %all-to-all-done.8 = f32[32,1,256]{2,1,0:T(1,128)S(1)} async-done(((f32[32,1,256]{2,1,0:T(1,128)}), f32[32,1,256]{2,1,0:T(1,128)S(1)}, u32[]{:S(2)}, u32[]{:S(2)}) %all-to-all-start.8) | async-done | bytes 32800 | tf_op jit(solution)/shard_map/all_to_all | solution.py:573
  504.9 10.8 %collective-permute-done.19 = bf16[4,32,4096]{2,1,0:T(8,128)(2,1)S(1)} collective-permute-done((bf16[4,32,4096]{2,1,0:T(8,128)(2,1)S(1)}, bf16[4,32,4096]{2,1,0:T(8,128)(2,1)S(1)}, u32[]{:S(2)}, u32[]{:S(2)}) %collective-permute-start.19) | collective-permute-done | bytes 1048608 | tf_op jit(solution)/shard_map/ppermute | solution.py:43
  525.3 35.5 %collective-permute-done.15 = bf16[4,2,128,1024]{3,2,0,1:T(8,128)(2,1)} collective-permute-done((bf16[4,2,128,1024]{3,2,0,1:T(8,128)(2,1)}, bf16[4,2,128,1024]{3,2,0,1:T(8,128)(2,1)}, u32[]{:S(2)}, u32[]{:S(2)}) %collective-permute-start.15) | collective-permute-done | bytes 2097184 | tf_op jit(solution)/shard_map/ppermute | solution.py:43
  565.7 9.6 %collective-permute-done.10 = bf16[8,32,384]{2,1,0:T(8,128)(2,1)S(1)} collective-permute-done((bf16[8,32,384]{2,1,0:T(8,128)(2,1)S(1)}, bf16[8,32,384]{2,1,0:T(8,128)(2,1)S(1)}, u32[]{:S(2)}, u32[]{:S(2)}) %collective-permute-start.10) | collective-permute-done | bytes 196640 | tf_op jit(solution)/shard_map/ppermute | solution.py:43
  583.6 10.0 %collective-permute-done.13 = bf16[4,32,1024]{2,1,0:T(8,128)(2,1)S(1)} collective-permute-done((bf16[4,32,1024]{2,1,0:T(8,128)(2,1)S(1)}, bf16[4,32,1024]{2,1,0:T(8,128)(2,1)S(1)}, u32[]{:S(2)}, u32[]{:S(2)}) %collective-permute-start.13) | collective-permute-done | bytes 262176 | tf_op jit(solution)/shard_map/ppermute | solution.py:43
  617.6 11.4 %reduce-scatter.9.cloned.1.call-done = bf16[1,160,1024]{2,1,0:T(8,128)(2,1)} async-done(((bf16[4,160,1024]{2,1,0:T(8,128)(2,1)}), bf16[1,160,1024]{2,1,0:T(8,128)(2,1)}) %reduce-scatter.9.cloned.1.call-update) | async-done | bytes 327696 | tf_op jit(solution)/shard_map/reduce_scatter | solution.py:601
  (353 shorter events, 233.7 us)
Async XLA Ops:
  7.3 49.2 %all-gather.17.cloned.1.call-start = ((), (), s32[]{:S(2)}) async-start(), calls=%async_computation.20 | async-start | bytes 1310720 | tf_op jit(solution)/shard_map/all_gather | solution.py:492
  8.0 66.2 %all-gather.15.cloned.1.call-start = ((), (), s32[]{:S(2)}) async-start(), calls=%async_computation.19 | async-start | bytes 1310720 | tf_op jit(solution)/shard_map/all_gather | solution.py:492
  8.8 114.3 %all-gather.11.cloned.1.call-start = ((), (), s32[]{:S(2)}) async-start(), calls=%async_computation.17 | async-start | bytes 4718592 | tf_op jit(solution)/shard_map/all_gather | solution.py:503
  11.1 170.1 %all-gather.13.cloned.1.call-start = ((), (), s32[]{:S(2)}) async-start(), calls=%async_computation.18 | async-start | bytes 4718592 | tf_op jit(solution)/shard_map/all_gather | solution.py:503
  83.2 63.9 %collective-permute-start.7 = (bf16[4,2,128,1024]{3,2,1,0:T(8,128)(2,1)}, bf16[4,2,128,1024]{3,2,1,0:T(8,128)(2,1)}, u32[]{:S(2)}, u32[]{:S(2)}) collective-permute-start(bf16[4,2,128,1024]{3,2,1,0:T(8,128)(2,1)} %broadcast_select_fusion.2), channel_id=1, source_target_pairs={{0,1},{1,0},{2,3},{3,2},{4,5},{5,4},{6,7},{7,6},{8,9},{9,8},{10,11... | collective-permute-start | bytes 6291464 | tf_op jit(solution)/shard_map/ppermute | solution.py:43
  102.0 49.9 %collective-permute-start.4 = (bf16[4,2,32,4096]{3,2,1,0:T(8,128)(2,1)}, bf16[4,2,32,4096]{3,2,1,0:T(8,128)(2,1)}, u32[]{:S(2)}, u32[]{:S(2)}) collective-permute-start(bf16[4,2,32,4096]{3,2,1,0:T(8,128)(2,1)} %broadcast_select_fusion.3), channel_id=1, source_target_pairs={{0,2},{2,0},{1,3},{3,1},{4,6},{6,4},{5,7},{7,5},{8,10},{10,8},{9,1... | collective-permute-start | bytes 6291464 | tf_op jit(solution)/shard_map/ppermute | solution.py:43
  151.7 102.3 %collective-permute-start.8 = (bf16[4,2,2,128,1024]{4,3,2,1,0:T(8,128)(2,1)}, bf16[4,2,2,128,1024]{4,3,2,1,0:T(8,128)(2,1)}, u32[]{:S(2)}, u32[]{:S(2)}) collective-permute-start(bf16[4,2,2,128,1024]{4,3,2,1,0:T(8,128)(2,1)} %broadcast_select_fusion), channel_id=1, source_target_pairs={{0,4},{4,0},{1,5},{5,1},{2,6},{6,2},{3,7},{7,3},{8,12},{12,8},{9,1... | collective-permute-start | bytes 12582920 | tf_op jit(solution)/shard_map/ppermute | solution.py:43
  156.5 97.5 %collective-permute-start.5 = (bf16[4,2,2,32,4096]{4,3,2,1,0:T(8,128)(2,1)}, bf16[4,2,2,32,4096]{4,3,2,1,0:T(8,128)(2,1)}, u32[]{:S(2)}, u32[]{:S(2)}) collective-permute-start(bf16[4,2,2,32,4096]{4,3,2,1,0:T(8,128)(2,1)} %broadcast_select_fusion.1), channel_id=1, source_target_pairs={{0,4},{4,0},{1,5},{5,1},{2,6},{6,2},{3,7},{7,3},{8,12},{12,8},{9,1... | collective-permute-start | bytes 12582920 | tf_op jit(solution)/shard_map/ppermute | solution.py:43
  175.6 29.8 %all-to-all-start.2 = ((bf16[8,256,128]{1,2,0:T(8,128)(2,1)}), bf16[8,256,128]{1,2,0:T(8,128)(2,1)S(1)}, u32[]{:S(2)}, u32[]{:S(2)}) async-start(bf16[8,256,128]{1,2,0:T(8,128)(2,1)} %copy.157), calls=%async_computation.2 | async-start | bytes 1048576 | tf_op jit(solution)/shard_map/all_to_all | solution.py:515
  179.6 31.2 %collective-permute-start.1 = (bf16[4,2,32,1024]{3,2,1,0:T(8,128)(2,1)S(1)}, bf16[4,2,32,1024]{3,2,1,0:T(8,128)(2,1)}, u32[]{:S(2)}, u32[]{:S(2)}) collective-permute-start(bf16[4,2,32,1024]{3,2,1,0:T(8,128)(2,1)S(1)} %broadcast_select_fusion.7), channel_id=1, source_target_pairs={{0,1},{1,0},{2,3},{3,2},{4,5},{5,4},{6,7},{7,6},{8,9},{9,8},{10,11... | collective-permute-start | bytes 1572872 | tf_op jit(solution)/shard_map/ppermute | solution.py:43
  210.3 390.0 %reduce-scatter.5.cloned.1.call-start = ((), (), s32[]{:S(2)}) async-start(), calls=%async_computation.13 | async-start | bytes 4718592 | tf_op jit(solution)/shard_map/reduce_scatter | solution.py:590
  212.0 27.9 %collective-permute-start.2 = (bf16[4,2,2,32,1024]{4,3,2,1,0:T(8,128)(2,1)S(1)}, bf16[4,2,2,32,1024]{4,3,2,1,0:T(8,128)(2,1)}, u32[]{:S(2)}, u32[]{:S(2)}) collective-permute-start(bf16[4,2,2,32,1024]{4,3,2,1,0:T(8,128)(2,1)S(1)} %broadcast_select_fusion.5), channel_id=1, source_target_pairs={{0,4},{4,0},{1,5},{5,1},{2,6},{6,2},{3,7},{7,3},{8,12},{12,8},{9,1... | collective-permute-start | bytes 3145736 | tf_op jit(solution)/shard_map/ppermute | solution.py:43
  377.5 222.8 %reduce-scatter.7.cloned.1.call-start = ((), (), s32[]{:S(2)}) async-start(), calls=%async_computation.14 | async-start | bytes 4718592 | tf_op jit(solution)/shard_map/reduce_scatter | solution.py:590
  377.6 55.2 %collective-permute-start.17 = (bf16[512,4096]{1,0:T(8,128)(2,1)}, bf16[512,4096]{1,0:T(8,128)(2,1)}, u32[]{:S(2)}, u32[]{:S(2)}) collective-permute-start(bf16[512,4096]{1,0:T(8,128)(2,1)} %get-tuple-element.90), channel_id=1, source_target_pairs={{0,4},{4,0},{1,5},{5,1},{2,6},{6,2},{3,7},{7,3},{8,12},{12,8},{9,1... | collective-permute-start | bytes 12582920 | tf_op jit(solution)/shard_map/ppermute | solution.py:43
  432.7 62.3 %collective-permute-start.14 = (bf16[4,512,1024]{2,1,0:T(8,128)(2,1)}, bf16[4,512,1024]{2,1,0:T(8,128)(2,1)}, u32[]{:S(2)}, u32[]{:S(2)}) collective-permute-start(bf16[4,512,1024]{2,1,0:T(8,128)(2,1)} %get-tuple-element.86), channel_id=1, source_target_pairs={{0,4},{4,0},{1,5},{5,1},{2,6},{6,2},{3,7},{7,3},{8,12},{12,8},{9,1... | collective-permute-start | bytes 12582920 | tf_op jit(solution)/shard_map/ppermute | solution.py:43
  437.3 49.9 %collective-permute-start.18 = (bf16[4,2,32,4096]{3,2,0,1:T(8,128)(2,1)}, bf16[4,2,32,4096]{3,2,0,1:T(8,128)(2,1)}, u32[]{:S(2)}, u32[]{:S(2)}) collective-permute-start(bf16[4,2,32,4096]{3,2,0,1:T(8,128)(2,1)} %fusion.4), channel_id=1, source_target_pairs={{0,2},{2,0},{1,3},{3,1},{4,6},{6,4},{5,7},{7,5},{8,10},{10,8},{9,1... | collective-permute-start | bytes 6291464 | tf_op jit(solution)/shard_map/ppermute | solution.py:43
  442.9 43.1 %all-to-all-start.8 = ((f32[32,1,256]{2,1,0:T(1,128)}), f32[32,1,256]{2,1,0:T(1,128)S(1)}, u32[]{:S(2)}, u32[]{:S(2)}) async-start(f32[32,1,256]{2,1,0:T(1,128)} %all_to_all.96), calls=%async_computation.11 | async-start | bytes 65536 | tf_op jit(solution)/shard_map/all_to_all | solution.py:573
  445.4 170.4 %reduce-scatter.11.cloned.1.call-start = ((), (), s32[]{:S(2)}) async-start(), calls=%async_computation.16 | async-start | bytes 1310720 | tf_op jit(solution)/shard_map/reduce_scatter | solution.py:604
  450.6 70.5 %collective-permute-start.11 = (bf16[512,1024]{1,0:T(8,128)(2,1)}, bf16[512,1024]{1,0:T(8,128)(2,1)}, u32[]{:S(2)}, u32[]{:S(2)}) collective-permute-start(bf16[512,1024]{1,0:T(8,128)(2,1)} %convolution_convert_fusion.2), channel_id=1, source_target_pairs={{0,4},{4,0},{1,5},{5,1},{2,6},{6,2},{3,7},{7,3},{8,12},{12,8},{9,1... | collective-permute-start | bytes 3145736 | tf_op jit(solution)/shard_map/ppermute | solution.py:43
  499.1 61.6 %collective-permute-start.15 = (bf16[4,2,128,1024]{3,2,0,1:T(8,128)(2,1)}, bf16[4,2,128,1024]{3,2,0,1:T(8,128)(2,1)}, u32[]{:S(2)}, u32[]{:S(2)}) collective-permute-start(bf16[4,2,128,1024]{3,2,0,1:T(8,128)(2,1)} %fusion.3), channel_id=1, source_target_pairs={{0,1},{1,0},{2,3},{3,2},{4,5},{5,4},{6,7},{7,6},{8,9},{9,8},{10,11... | collective-permute-start | bytes 6291464 | tf_op jit(solution)/shard_map/ppermute | solution.py:43
  523.2 56.5 %collective-permute-start.12 = (bf16[4,2,32,1024]{3,2,0,1:T(8,128)(2,1)}, bf16[4,2,32,1024]{3,2,0,1:T(8,128)(2,1)S(1)}, u32[]{:S(2)}, u32[]{:S(2)}) collective-permute-start(bf16[4,2,32,1024]{3,2,0,1:T(8,128)(2,1)} %fusion.24), channel_id=1, source_target_pairs={{0,1},{1,0},{2,3},{3,2},{4,5},{5,4},{6,7},{7,6},{8,9},{9,8},{10,11... | collective-permute-start | bytes 1572872 | tf_op jit(solution)/shard_map/ppermute | solution.py:43
  523.8 51.5 %collective-permute-start.10 = (bf16[8,32,384]{2,1,0:T(8,128)(2,1)S(1)}, bf16[8,32,384]{2,1,0:T(8,128)(2,1)S(1)}, u32[]{:S(2)}, u32[]{:S(2)}) collective-permute-start(bf16[8,32,384]{2,1,0:T(8,128)(2,1)S(1)} %fusion.29), channel_id=1, source_target_pairs={{0,1},{1,0},{2,3},{3,2},{4,5},{5,4},{6,7},{7,6},{8,9},{9,8},{10,11... | collective-permute-start | bytes 589832 | tf_op jit(solution)/shard_map/ppermute | solution.py:43
  564.3 31.8 %collective-permute-start.16 = (bf16[4,128,1024]{2,1,0:T(8,128)(2,1)}, bf16[4,128,1024]{2,1,0:T(8,128)(2,1)}, u32[]{:S(2)}, u32[]{:S(2)}) collective-permute-start(bf16[4,128,1024]{2,1,0:T(8,128)(2,1)} %fusion.8), channel_id=1, source_target_pairs={{0,2},{2,0},{1,3},{3,1},{4,6},{6,4},{5,7},{7,5},{8,10},{10,8},{9,1... | collective-permute-start | bytes 3145736 | tf_op jit(solution)/shard_map/ppermute | solution.py:43
  579.6 49.4 %reduce-scatter.9.cloned.1.call-start = ((), (), s32[]{:S(2)}) async-start(), calls=%async_computation.15 | async-start | bytes 1638400 | tf_op jit(solution)/shard_map/reduce_scatter | solution.py:601
  (78 other events, 796.5 us)
Sparse Core Ops, SparseCore 0:
  9.7 36.0 all-gather.16
  47.4 26.7 all-gather.14
  76.4 46.6 all-gather.10
  125.1 50.0 all-gather.12
  372.3 55.4 reduce-scatter.4
  432.9 48.2 reduce-scatter.6
  519.3 24.1 reduce-scatter.10
  600.4 28.4 reduce-scatter.8

commit v3 on v2

--- a/solution.py
+++ b/solution.py
@@ -17,6 +17,7 @@
 F32 = jnp.float32
 NT = (((1,), (1,)), ((), ()))
 VMEM_BYTES = 48 * 1024 * 1024
+LIGHT = pl.CostEstimate(flops=1024, bytes_accessed=1024, transcendentals=0)
 
 
 def layer_norm(values, norm_gain, norm_shift):
@@ -24,11 +25,6 @@
     centered = values - average
     variance = jnp.mean(centered * centered, -1, keepdims=True)
     return centered * lax.rsqrt(variance + 1e-05) * norm_gain + norm_shift
-
-
-def gelu_tanh(values):
-    inside = 0.7978845608 * (values + 0.044715 * values * values * values)
-    return 0.5 * values * (1.0 + jnp.tanh(inside))
 
 
 def outer_sum(left, right):
@@ -56,6 +52,34 @@
     )
 
 
+def line_gather(values, axis, *earlier):
+    size, me = lax.axis_size(axis), lax.axis_index(axis)
+    held = jnp.zeros((3 * size - 2, *values.shape), values.dtype)
+    held = lax.dynamic_update_index_in_dim(held, values, me + size - 1, 0)
+    up = down = values
+    for step in range(1, size):
+        if step == size - 1:
+            up, down = after(up, *earlier), after(down, *earlier)
+        up = lax.ppermute(up, axis, [(i - 1, i) for i in range(step, size)])
+        down = lax.ppermute(down, axis, [(i + 1, i) for i in range(size - step)])
+        held = lax.dynamic_update_index_in_dim(held, up, me - step + size - 1, 0)
+        held = lax.dynamic_update_index_in_dim(held, down, me + step + size - 1, 0)
+    return held[size - 1 : 2 * size - 1]
+
+
+def line_reduce(values, axis):
+    size, me = lax.axis_size(axis), lax.axis_index(axis)
+    up = down = 0.0
+    for step in range(1, size):
+        above = jnp.minimum(me + size - step, size - 1)
+        below = jnp.maximum(me - size + step, 0)
+        up = (at_index(values, above, 0).astype(F32) + up).astype(BF)
+        down = (at_index(values, below, 0).astype(F32) + down).astype(BF)
+        up = lax.ppermute(up, axis, [(i, i + 1) for i in range(step)]).astype(F32)
+        down = lax.ppermute(down, axis, [(i, i - 1) for i in range(size - step, size)]).astype(F32)
+    return at_index(values, me, 0).astype(F32) + up + down
+
+
 def send_axis(values, axis, position):
     if lax.axis_size(axis) != 2:
         return lax.all_gather(values, axis, axis=position, tiled=False)
@@ -79,25 +103,229 @@
     return total
 
 
+def give_part(terms, axis, position):
+    if lax.axis_size(axis) != 2:
+        return total_of(terms).astype(BF)
+    other = 1 - lax.axis_index(axis)
+    return total_of([at_index(term, other, position) for term in terms]).astype(BF)
+
+
+def take_part(terms, given, axis, position):
+    if lax.axis_size(axis) != 2:
+        return [lax.psum_scatter(given, axis, scatter_dimension=position, tiled=False)]
+    me = lax.axis_index(axis)
+    return [at_index(term, me, position) for term in terms] + [swap(given, axis)]
+
+
 def reduce_axis(terms, axis, position):
-    if lax.axis_size(axis) != 2:
-        whole = total_of(terms).astype(BF)
-        return [lax.psum_scatter(whole, axis, scatter_dimension=position, tiled=False)]
-    me = lax.axis_index(axis)
-    give = total_of([at_index(term, 1 - me, position) for term in terms]).astype(BF)
-    return [at_index(term, me, position) for term in terms] + [swap(give, axis)]
-
-
-def feed_kernel(
-    me_ref, own_ref, oth_ref, cot_ref, up_own_ref, up_oth_ref, down_own_ref, down_oth_ref, bias_ref,
-    y_ref, gs_own_ref, gs_oth_ref, gd_own_ref, gd_oth_ref, gu_own_ref, gu_oth_ref, gb_ref,
-    own_t, oth_t,
+    return take_part(terms, give_part(terms, axis, position), axis, position)
+
+
+def normalize(values):
+    average = jnp.mean(values, -1, keepdims=True)
+    centered = values - average
+    variance = jnp.mean(centered * centered, -1, keepdims=True)
+    scale = lax.rsqrt(variance + 1e-05)
+    return centered * scale, scale
+
+
+def norm_back(grad, normal, scale, gain):
+    scaled = grad * gain
+    inner = jnp.mean(scaled * normal, -1, keepdims=True)
+    return scale * (scaled - jnp.mean(scaled, -1, keepdims=True) - normal * inner)
+
+
+def branch_kernel(
+    me_ref, att_ref, x_ref, w_own_ref, w_oth_ref, bias_ref, gain_ref, shift_ref, middle_ref, own_ref, oth_ref
 ):
+    me = me_ref[0]
+    z_size, block, _ = w_own_ref.shape
+    middle = x_ref[...].astype(F32) + bias_ref[...]
+    for z in range(z_size):
+        middle = middle + jnp.dot(att_ref[2 * z + me], w_own_ref[z], preferred_element_type=F32)
+        middle = middle + jnp.dot(att_ref[2 * z + 1 - me], w_oth_ref[z], preferred_element_type=F32)
+    middle_ref[...] = middle
+    normal, _ = normalize(middle)
+    normal = normal * gain_ref[...] + shift_ref[...]
+    for z in range(z_size):
+        even = normal[:, 2 * z * block : (2 * z + 1) * block]
+        odd = normal[:, (2 * z + 1) * block : (2 * z + 2) * block]
+        own_ref[:, z * block : (z + 1) * block] = jnp.where(me == 0, even, odd).astype(BF)
+        oth_ref[:, z * block : (z + 1) * block] = jnp.where(me == 0, odd, even).astype(BF)
+
+
+def branch(me, att, rows, w_own, w_oth, bias, gain, shift):
+    length, model_width = rows.shape
+    vmem = pl.BlockSpec(memory_space=pltpu.VMEM)
+    return pl.pallas_call(
+        branch_kernel,
+        in_specs=[pl.BlockSpec(memory_space=pltpu.SMEM)] + [vmem] * 7,
+        out_specs=[vmem] * 3,
+        out_shape=[
+            jax.ShapeDtypeStruct((length, model_width), F32),
+            jax.ShapeDtypeStruct((length, model_width // 2), BF),
+            jax.ShapeDtypeStruct((length, model_width // 2), BF),
+        ],
+        compiler_params=pltpu.CompilerParams(vmem_limit_bytes=VMEM_BYTES),
+        cost_estimate=LIGHT,
+        name="branch",
+    )(me, att, rows, w_own, w_oth, bias, gain, shift)
+
+
+def middle_back_kernel(
+    me_ref, gs_own_ref, gs_oth_ref, middle_ref, cot_ref, y_ref, bias_ref, gain_ref, w_own_ref, w_oth_ref, *rest
+):
+    gm_ref, gb_ref, ga_ref, sums_ref, out_ref, grad_scr = rest[-6:]
+    me = me_ref[0]
+    z_size, block, _ = w_own_ref.shape
+    for z in range(z_size):
+        own = gs_own_ref[:, z * block : (z + 1) * block]
+        oth = gs_oth_ref[:, z * block : (z + 1) * block]
+        grad_scr[:, 2 * z * block : (2 * z + 1) * block] = jnp.where(me == 0, own, oth)
+        grad_scr[:, (2 * z + 1) * block : (2 * z + 2) * block] = jnp.where(me == 0, oth, own)
+    middle = middle_ref[...]
+    out_ref[0] = (middle + y_ref[...] + bias_ref[...]).astype(BF)
+    normal, scale = normalize(middle)
+    grad = grad_scr[...]
+    cot = cot_ref[...].astype(F32)
+    grad_middle = cot + norm_back(grad, normal, scale, gain_ref[...])
+    gm_ref[...] = grad_middle
+    low = grad_middle.astype(BF)
+    gb_ref[...] = low
+    for z in range(z_size):
+        ga_ref[2 * z + me] = times_rows(low, w_own_ref[z]).astype(BF)
+        ga_ref[2 * z + 1 - me] = times_rows(low, w_oth_ref[z]).astype(BF)
+    sums_ref[0:1, :] = jnp.sum(low.astype(F32), 0, keepdims=True)
+    sums_ref[1:2, :] = jnp.sum(grad * normal, 0, keepdims=True)
+    sums_ref[2:3, :] = jnp.sum(grad, 0, keepdims=True)
+    sums_ref[3:4, :] = jnp.sum(cot, 0, keepdims=True)
+
+
+def middle_back(n, sequences, me, gs_own, gs_oth, middle, cot, y, bias, gain, w_own, w_oth, filled):
+    length, model_width = middle.shape
+    z_size, block, _ = w_own.shape
+    whole = lambda i: (0, 0)
+    part = lambda i: (n, 0)
+    cube = lambda i: (0, 0, 0)
+    half = pl.BlockSpec((length, model_width // 2), part)
+    line = pl.BlockSpec((1, model_width), whole)
+    matrix = pl.BlockSpec(w_own.shape, cube)
+    full = pl.BlockSpec((length, model_width), whole)
+    extra = [] if filled is None else [filled]
+    return pl.pallas_call(
+        middle_back_kernel,
+        grid=(1,),
+        in_specs=[
+            pl.BlockSpec(memory_space=pltpu.SMEM), half, half, full, full,
+            pl.BlockSpec((length, model_width), part), line, line, matrix, matrix,
+        ]
+        + [pl.BlockSpec(memory_space=pl.ANY)] * len(extra),
+        out_specs=[
+            full,
+            full,
+            pl.BlockSpec((2 * z_size, length, block), cube),
+            pl.BlockSpec((8, model_width), whole),
+            pl.BlockSpec((1, length, model_width), lambda i: (n, 0, 0)),
+        ],
+        out_shape=[
+            jax.ShapeDtypeStruct((length, model_width), F32),
+            jax.ShapeDtypeStruct((length, model_width), BF),
+            jax.ShapeDtypeStruct((2 * z_size, length, block), BF),
+            jax.ShapeDtypeStruct((8, model_width), F32),
+            jax.ShapeDtypeStruct((sequences, length, model_width), BF),
+        ],
+        scratch_shapes=[pltpu.VMEM((length, model_width), F32)],
+        input_output_aliases={10: 4} if extra else {},
+        compiler_params=pltpu.CompilerParams(vmem_limit_bytes=VMEM_BYTES),
+        cost_estimate=LIGHT,
+        name="middle_back",
+    )(me, gs_own, gs_oth, middle, cot, y, bias, gain, w_own, w_oth, *extra)
+
+
+def out_weight_kernel(sequences, me_ref, *refs):
+    own_refs, oth_refs = refs[:sequences], refs[sequences : 2 * sequences]
+    grad_refs = refs[2 * sequences : 3 * sequences]
+    go_own_ref, go_oth_ref = refs[3 * sequences :]
+    for att_refs, out_ref in ((own_refs, go_own_ref), (oth_refs, go_oth_ref)):
+        total = outer_sum(att_refs[0][0], grad_refs[0][...])
+        for att_ref, grad_ref in zip(att_refs[1:], grad_refs[1:]):
+            total = total + outer_sum(att_ref[0], grad_ref[...])
+        out_ref[0] = total.astype(BF)
+
+
+def out_weight_grad(me, atts, grads):
+    sequences = len(atts)
+    devices, length, block = atts[0].shape
+    model_width = grads[0].shape[1]
+    z_size = devices // 2
+    own = pl.BlockSpec((1, length, block), lambda z, me_ref: (2 * z + me_ref[0], 0, 0))
+    oth = pl.BlockSpec((1, length, block), lambda z, me_ref: (2 * z + 1 - me_ref[0], 0, 0))
+    full = pl.BlockSpec((length, model_width), lambda z, me_ref: (0, 0))
+    out = pl.BlockSpec((1, block, model_width), lambda z, me_ref: (z, 0, 0))
+    shape = jax.ShapeDtypeStruct((z_size, block, model_width), BF)
+    return pl.pallas_call(
+        functools.partial(out_weight_kernel, sequences),
+        grid_spec=pltpu.PrefetchScalarGridSpec(
+            num_scalar_prefetch=1,
+            grid=(z_size,),
+            in_specs=[own] * sequences + [oth] * sequences + [full] * sequences,
+            out_specs=[out, out],
+        ),
+        out_shape=[shape, shape],
+        compiler_params=pltpu.CompilerParams(vmem_limit_bytes=VMEM_BYTES),
+        cost_estimate=LIGHT,
+        name="out_weight_grad",
+    )(me, *atts, *atts, *grads)
+
+
+def first_back_kernel(grad_ref, x_ref, gain_ref, gm_ref, *rest):
+    sums_ref, out_ref = rest[-2:]
+    grad = grad_ref[...].astype(F32)
+    normal, scale = normalize(x_ref[...].astype(F32))
+    out_ref[0] = gm_ref[...] + norm_back(grad, normal, scale, gain_ref[...])
+    sums_ref[0:1, :] = jnp.sum(grad * normal, 0, keepdims=True)
+    sums_ref[1:2, :] = jnp.sum(grad, 0, keepdims=True)
+
+
+def first_back(n, sequences, grad, rows, gain, grad_middle, filled):
+    length, model_width = rows.shape
+    whole = lambda i: (0, 0)
+    full = pl.BlockSpec((length, model_width), whole)
+    extra = [] if filled is None else [filled]
+    return pl.pallas_call(
+        first_back_kernel,
+        grid=(1,),
+        in_specs=[full, full, pl.BlockSpec((1, model_width), whole), full]
+        + [pl.BlockSpec(memory_space=pl.ANY)] * len(extra),
+        out_specs=[
+            pl.BlockSpec((8, model_width), whole),
+            pl.BlockSpec((1, length, model_width), lambda i: (n, 0, 0)),
+        ],
+        out_shape=[
+            jax.ShapeDtypeStruct((8, model_width), F32),
+            jax.ShapeDtypeStruct((sequences, length, model_width), F32),
+        ],
+        input_output_aliases={4: 1} if extra else {},
+        compiler_params=pltpu.CompilerParams(vmem_limit_bytes=VMEM_BYTES),
+        cost_estimate=LIGHT,
+        name="first_back",
+    )(grad, rows, gain, grad_middle, *extra)
+
+
+def feed_kernel(sequences, me_ref, *refs):
+    own_refs, oth_refs, refs = refs[:sequences], refs[sequences : 2 * sequences], refs[2 * sequences :]
+    cot_ref, up_own_ref, up_oth_ref, down_own_ref, down_oth_ref, bias_ref = refs[:6]
+    y_ref, gs_own_ref, gs_oth_ref, gd_own_ref, gd_oth_ref, gu_own_ref, gu_oth_ref, gb_ref = refs[6:14]
+    own_ref, oth_ref, own_t, oth_t = refs[14:]
     step = pl.program_id(0)
     half = pl.num_programs(0) // 2
+    length = own_refs[0].shape[0]
 
     @pl.when(step == 0)
     def _():
+        for n in range(sequences):
+            own_ref[n * length : (n + 1) * length, :] = own_refs[n][...]
+            oth_ref[n * length : (n + 1) * length, :] = oth_refs[n][...]
         own_t[...] = own_ref[...].astype(F32).T.astype(BF)
         oth_t[...] = oth_ref[...].astype(F32).T.astype(BF)
         y_ref[...] = jnp.zeros_like(y_ref)
@@ -135,9 +363,10 @@
         one(down_oth_ref, gd_oth_ref)
 
 
-def feed(me, own, oth, cot, up_own, up_oth, down_own, down_oth, bias):
-    tokens, half_width = own.shape
-    model_width = cot.shape[1]
+def feed(me, owns, oths, cot, up_own, up_oth, down_own, down_oth, bias):
+    sequences = len(owns)
+    length, half_width = owns[0].shape
+    tokens, model_width = cot.shape
     ff_width = up_own.shape[1]
     z_size, block, _ = down_own.shape
 
@@ -149,18 +378,20 @@
     first = lambda j, me_ref: (jnp.minimum(j, z_size - 1), 0, 0)
     second = lambda j, me_ref: (jnp.maximum(j - z_size, 0), 0, 0)
     halves = [pl.BlockSpec((tokens, half_width), whole)] * 2
+    pieces = [pl.BlockSpec((length, half_width), whole)] * (2 * sequences)
     columns = [pl.BlockSpec((half_width, block), column)] * 2
     downs = [pl.BlockSpec((1, block, model_width), first), pl.BlockSpec((1, block, model_width), second)]
     line = pl.BlockSpec((1, block), column)
     all_rows = pl.BlockSpec((tokens, model_width), whole)
     return pl.pallas_call(
-        feed_kernel,
+        functools.partial(feed_kernel, sequences),
         grid_spec=pltpu.PrefetchScalarGridSpec(
             num_scalar_prefetch=1,
             grid=(2 * z_size,),
-            in_specs=[*halves, all_rows, *columns, *downs, line],
+            in_specs=[*pieces, all_rows, *columns, *downs, line],
             out_specs=[all_rows, *halves, *downs, *columns, line],
-            scratch_shapes=[pltpu.VMEM((half_width, tokens), BF)] * 2,
+            scratch_shapes=[pltpu.VMEM((tokens, half_width), BF)] * 2
+            + [pltpu.VMEM((half_width, tokens), BF)] * 2,
         ),
         out_shape=[
             jax.ShapeDtypeStruct((tokens, model_width), F32),
@@ -173,13 +404,9 @@
             jax.ShapeDtypeStruct((1, ff_width), F32),
         ],
         compiler_params=pltpu.CompilerParams(vmem_limit_bytes=VMEM_BYTES),
-        cost_estimate=pl.CostEstimate(
-            flops=12 * tokens * model_width * ff_width,
-            bytes_accessed=8 * model_width * ff_width + 12 * tokens * model_width,
-            transcendentals=tokens * ff_width,
-        ),
+        cost_estimate=LIGHT,
         name="feed",
-    )(me, own, oth, cot, up_own, up_oth, down_own, down_oth, bias)
+    )(me, *owns, *oths, cot, up_own, up_oth, down_own, down_oth, bias)
 
 
 def project_kernel(x_ref, gain_ref, shift_ref, w_ref, bias_ref, low_ref, q_ref, k_ref, v_ref, kt_ref, vt_ref):
@@ -225,11 +452,7 @@
         + [jax.ShapeDtypeStruct((length, width), BF)] * 3
         + [jax.ShapeDtypeStruct((width, length), BF)] * 2,
         compiler_params=pltpu.CompilerParams(vmem_limit_bytes=VMEM_BYTES),
-        cost_estimate=pl.CostEstimate(
-            flops=2 * length * model_width * 3 * width,
-            bytes_accessed=4 * length * model_width + 10 * length * width,
-            transcendentals=0,
-        ),
+        cost_estimate=LIGHT,
         name="project",
     )(rows, gain, shift, weight, bias)
 
@@ -312,11 +535,7 @@
         ],
         scratch_shapes=[pltpu.VMEM((length, block), F32), pltpu.VMEM((block, width), F32)],
         compiler_params=pltpu.CompilerParams(vmem_limit_bytes=VMEM_BYTES),
-        cost_estimate=pl.CostEstimate(
-            flops=8 * heads * length * length * HD,
-            bytes_accessed=8 * length * width,
-            transcendentals=heads * length * length // 2,
-        ),
+        cost_estimate=LIGHT,
         name="attend",
     )(slopes, queries, keys, values_t)
 
@@ -414,11 +633,7 @@
             pltpu.VMEM((block, width), F32),
         ],
         compiler_params=pltpu.CompilerParams(vmem_limit_bytes=VMEM_BYTES),
-        cost_estimate=pl.CostEstimate(
-            flops=20 * heads * length * length * HD,
-            bytes_accessed=16 * length * width,
-            transcendentals=heads * length * length // 2,
-        ),
+        cost_estimate=LIGHT,
         name="attend_back",
     )(slopes, queries, keys, keys_t, values, grads, lse)
 
@@ -456,17 +671,6 @@
 
     me = lax.axis_index("core")
 
-    def split(values):
-        values = values.reshape(tokens, z_size, 2, -1)
-        return (
-            at_index(values, me, 2).reshape(tokens, -1),
-            at_index(values, 1 - me, 2).reshape(tokens, -1),
-        )
-
-    def unsplit(own, oth):
-        own, oth = own.reshape(tokens, z_size, -1), oth.reshape(tokens, z_size, -1)
-        return merge_pair(own, oth, "core", 2).reshape(tokens, -1)
-
     small_parts = (norm1_gain, norm1_bias, qv_bias, out_bias, norm2_gain, norm2_bias, up_bias, down_bias)
     small_here = jnp.concatenate(small_parts)
     small_all = lax.all_to_all(
@@ -487,55 +691,60 @@
     bias_mine = lax.dynamic_index_in_dim(bias_parts, place, 1, keepdims=False)
     bias_heads = jnp.concatenate([bias_mine[0], jnp.zeros((width,), F32), bias_mine[1]])
 
-    orders = (("fx", "fy"), ("fy", "fx"), ("fy", "fx"))
-    along_z = [
-        lax.all_gather(weight, "z", axis=0, tiled=False) for weight in (up_weight, down_weight, out_weight)
-    ]
-    along_z = [after(weight, w_heads, small_all) for weight in along_z]
-    sent = [send_axis(w, order[0], 1) for w, order in zip(along_z, orders)]
-    pairs = [join_axis(w, o, order[0], 1) for w, o, order in zip(along_z, sent, orders)]
-    second_place = [1 if order[1] == "fy" else 2 for order in orders]
-    sent = [send_axis(w, order[1], at) for w, order, at in zip(pairs, orders, second_place)]
+    low_z = lax.all_gather(jnp.concatenate([out_weight, down_weight], 0), "z", axis=0, tiled=False)
+    low_z = after(low_z, small_all)
+    down_z, out_z = low_z[:, rows_each:], low_z[:, :rows_each]
+    down_sent, out_sent = send_axis(down_z, "fy", 1), send_axis(out_z, "fy", 1)
+    down_pair = join_axis(down_z, down_sent, "fy", 1)
+    out_pair = join_axis(out_z, out_sent, "fy", 1)
+    up_z = line_gather(after(up_weight, columns), "z", down_pair, out_pair, w_heads)
+    up_sent = send_axis(up_z, "fx", 1)
+    down_sent, out_sent = send_axis(down_pair, "fx", 2), send_axis(out_pair, "fx", 2)
 
     kept = []
     returned = []
+    ahead = (up_z, down_pair, out_pair)
     for n in range(sequences):
-        rows = lax.all_gather(hidden_in[n], SEQ, axis=0, tiled=True)
-        if n == sequences - 1:
-            sent = [after(o, kept[0][-1]) if kept else o for o in sent]
-            mine = [
-                join_axis(w, o, order[1], at)
-                for w, o, order, at in zip(pairs, sent, orders, second_place)
-            ]
-            theirs = [swap(w, "core") for w in mine]
+        rows = after(lax.all_gather(hidden_in[n], SEQ, axis=0, tiled=True), *ahead)
         first_low, q, k, v, kt, vt = project(
             rows, first_gain[None], first_shift[None], w_heads, bias_heads[None]
         )
         attended, lse = attend(slopes, q, k, vt)
-        returned.append(lax.all_to_all(attended, SEQ, split_axis=0, concat_axis=1, tiled=True))
+        attended = attended.reshape(seq_devices, local_len, width)
+        returned.append(lax.all_to_all(attended, SEQ, split_axis=0, concat_axis=0, tiled=True))
         kept.append((first_low, q, k, v, kt, lse))
-    attended_low = jnp.stack(returned).reshape(tokens, model_width)
+        ahead = (returned[n],)
+        if n == 0:
+            up_sent, down_sent, out_sent, _ = lax.optimization_barrier(
+                (up_sent, down_sent, out_sent, lse)
+            )
+            up_pair = join_axis(up_z, up_sent, "fx", 1)
+            up_sent = send_axis(up_pair, "fy", 1)
+            down_own = join_axis(down_pair, after(down_sent, up_pair), "fx", 2)
+            out_own = join_axis(out_pair, after(out_sent, up_pair), "fx", 2)
+            down_oth, out_oth = swap(down_own, "core"), swap(out_own, "core")
+            ahead = (*ahead, up_pair, down_own, out_own)
+    up_own = join_axis(up_pair, after(up_sent, lse), "fy", 1)
+    up_oth = swap(up_own, "core")
     half_width = model_width // 2
-    up_own, up_oth = (w.reshape(half_width, ff_width) for w in (mine[0], theirs[0]))
-    down_own, down_oth = (w.reshape(z_size, -1, model_width) for w in (mine[1], theirs[1]))
-    out_own, out_oth = (w.reshape(half_width, model_width) for w in (mine[2], theirs[2]))
-
-    flat_in = hidden_in.reshape(tokens, model_width).astype(F32)
-    att_own, att_oth = split(attended_low)
-    middle = (
-        flat_in
-        + jnp.dot(att_own, out_own, preferred_element_type=F32)
-        + jnp.dot(att_oth, out_oth, preferred_element_type=F32)
-        + b_out
+    up_own, up_oth = (w.reshape(half_width, ff_width) for w in (up_own, up_oth))
+    down_own, down_oth = (w.reshape(z_size, -1, model_width) for w in (down_own, down_oth))
+    out_own, out_oth = (w.reshape(z_size, -1, model_width) for w in (out_own, out_oth))
+
+    mine_core = me.reshape(1)
+    middles, owns, oths = zip(
+        *[
+            branch(
+                mine_core, returned[n], hidden_in[n], out_own, out_oth,
+                b_out[None], second_gain[None], second_shift[None],
+            )
+            for n in range(sequences)
+        ]
     )
-    second_norm, second_back = jax.vjp(layer_norm, middle, second_gain, second_shift)
-    second_own, second_oth = split(second_norm.astype(BF))
     cot_low = out_grad.reshape(tokens, model_width)
-    cotangent = cot_low.astype(F32)
     y, gs_own, gs_oth, gd_own, gd_oth, gu_own, gu_oth, grad_up_bias = feed(
-        me.reshape(1), second_own, second_oth, cot_low, up_own, up_oth, down_own, down_oth, b_up[None]
+        mine_core, owns, oths, cot_low, up_own, up_oth, down_own, down_oth, b_up[None]
     )
-    block_out = (middle + y + b_down).astype(BF).reshape(sequences, local_len, model_width)
 
     cells = (z_size, y_size, x_size)
     to_up = gu_own.reshape(*cells, rows_each, ff_width)
@@ -543,51 +752,56 @@
     sum_up = [to_up, swap(gu_oth, "core").reshape(to_up.shape)]
     sum_down = [to_down, swap(gd_oth, "core").reshape(to_down.shape)]
 
-    grad_second = unsplit(gs_own, gs_oth)
-    grad_mid_norm, grad_gain_two, grad_shift_two = second_back(grad_second)
-    grad_middle = cotangent + grad_mid_norm
-    grad_branch = grad_middle.astype(BF)
-    grad_attended = unsplit(
-        times_rows(grad_branch, out_own).astype(BF), times_rows(grad_branch, out_oth).astype(BF)
-    )
-    grad_attended = grad_attended.reshape(sequences, local_len, model_width)
-    grad_heads = [
-        lax.all_to_all(grad_attended[n], SEQ, split_axis=1, concat_axis=0, tiled=True)
-        for n in range(sequences)
-    ]
-    go_own = outer_sum(att_own, grad_branch).astype(BF).reshape(*cells, rows_each, model_width)
-    go_oth = outer_sum(att_oth, grad_branch).astype(BF)
-    sum_out = [go_own, swap(go_oth, "core").reshape(go_own.shape)]
-    sum_up = reduce_axis(sum_up, "fy", 1)
-    sum_down = reduce_axis(sum_down, "fx", 2)
-    sum_out = reduce_axis(sum_out, "fx", 2)
-
-    rear = [
-        jnp.sum(grad_branch.astype(F32), 0),
-        grad_gain_two,
-        grad_shift_two,
-        grad_up_bias,
-        jnp.sum(cotangent, 0),
-    ]
+    block_out = None
+    grad_middles, grad_branches, grad_heads, sums = [], [], [], []
+    for n in range(sequences):
+        grad_middle, grad_branch, grad_att, four, block_out = middle_back(
+            n, sequences, mine_core, gs_own, gs_oth, middles[n], out_grad[n], y,
+            b_down[None], second_gain[None], out_own, out_oth, block_out,
+        )
+        grad_middles.append(grad_middle)
+        grad_branches.append(grad_branch)
+        sums.append(four)
+        grad_heads.append(grad_att)
+    grad_heads = jnp.stack(grad_heads, 1)
+    grad_heads = lax.all_to_all(grad_heads, SEQ, split_axis=0, concat_axis=0, tiled=True)
+    go_own, go_oth = out_weight_grad(mine_core, returned, grad_branches)
+    to_out = go_own.reshape(*cells, rows_each, model_width)
+    sum_out = [to_out, swap(go_oth, "core").reshape(to_out.shape)]
+    parts = (give_part(sum_up, "fy", 1), give_part(sum_down, "fx", 2), give_part(sum_out, "fx", 2))
+    sum_up = take_part(sum_up, parts[0], "fy", 1)
+    sum_down = take_part(sum_down, parts[1], "fx", 2)
+    sum_out = take_part(sum_out, parts[2], "fx", 2)
+
+    four = total_of(sums)
+    rear = [four[0], four[1], four[2], grad_up_bias, four[3]]
     rear_wide = jnp.concatenate([part.reshape(devices, -1) for part in rear], 1)
     rear_sum = jnp.sum(lax.all_to_all(rear_wide, ALL, split_axis=0, concat_axis=0, tiled=True), 0)
+
+    grad_heads = after(grad_heads, *parts)
 
     grad_qkvw = jnp.zeros((model_width, 3 * width), F32)
     column_sums = jnp.zeros((3 * width,), F32)
     grad_first = []
     for n in range(sequences):
         first_low, q, k, v, kt, lse = kept[n]
-        dq, dk, dv = attend_back(slopes, q, k, kt, v, grad_heads[n], lse)
-        if n == sequences - 1:
-            sum_up, sum_down, sum_out = (
-                terms[:-1] + [after(terms[-1], dq)] for terms in (sum_up, sum_down, sum_out)
-            )
-            sum_up = reduce_axis(sum_up, "fx", 1)
-            sum_down = reduce_axis(sum_down, "fy", 1)
-            sum_out = reduce_axis(sum_out, "fy", 1)
+        q = after(q, *parts)
+        grads = grad_heads[:, n].reshape(q.shape)
+        dq, dk, dv = attend_back(slopes, q, k, kt, v, grads, lse)
+        last = [terms[-1] for terms in (sum_up, sum_down, sum_out)]
+        dq, dk, dv, *last = lax.optimization_barrier((dq, dk, dv, *last))
+        sum_up, sum_down, sum_out = (
+            [*terms[:-1], recent] for terms, recent in zip((sum_up, sum_down, sum_out), last)
+        )
         grad_projected = jnp.concatenate([dq, dk, dv], 1)
         partial = times_rows(grad_projected, w_heads).astype(BF)
         grad_first.append(lax.psum_scatter(partial, SEQ, scatter_dimension=0, tiled=True))
+        parts = (partial,)
+        if n == 0:
+            parts = (partial, give_part(sum_up, "fx", 1), give_part(sum_down, "fy", 1), give_part(sum_out, "fy", 1))
+            sum_up = take_part(sum_up, parts[1], "fx", 1)
+            sum_down = take_part(sum_down, parts[2], "fy", 1)
+            sum_out = take_part(sum_out, parts[3], "fy", 1)
         grad_qkvw = grad_qkvw + outer_sum(first_low, grad_projected)
         column_sums = column_sums + jnp.sum(grad_projected.astype(F32), 0)
 
@@ -598,15 +812,19 @@
     out_qkvw = wide.reshape(rows_each, 3 * model_width)
 
     low_sum = jnp.concatenate([total_of(sum_out).astype(BF), total_of(sum_down).astype(BF)], 1)
-    low_sum = lax.psum_scatter(low_sum, "z", scatter_dimension=0, tiled=False).astype(F32)
+    low_sum = line_reduce(low_sum, "z")
     out_outw, out_down = low_sum[:rows_each], low_sum[rows_each:]
-    out_up = total_of(sum_up).astype(BF)
-    out_up = lax.psum_scatter(out_up, "z", scatter_dimension=0, tiled=False).astype(F32)
-
-    grad_first = jnp.stack(grad_first).reshape(tokens, model_width).astype(F32)
-    _, first_back = jax.vjp(layer_norm, flat_in, first_gain, first_shift)
-    grad_in_norm, grad_gain_one, grad_shift_one = first_back(grad_first)
-    input_grad = (grad_middle + grad_in_norm).reshape(sequences, local_len, model_width)
+    out_up = line_reduce(total_of(sum_up).astype(BF), "z")
+
+    input_grad = None
+    sums = []
+    for n in range(sequences):
+        two, input_grad = first_back(
+            n, sequences, grad_first[n], hidden_in[n], first_gain[None], grad_middles[n], input_grad
+        )
+        sums.append(two)
+    two = total_of(sums)
+    grad_gain_one, grad_shift_one = two[0], two[1]
 
     qv_here = jnp.zeros((2, seq_devices, width), F32)
     qv_mine = jnp.stack([column_sums[:width], column_sums[2 * width :]])

time: 648 us -> 574 us (0.89)
  starting transfers between devices: 48.7 us -> 92.6 us
  waiting for transfers between devices: 220 us -> 179 us
  blocking collectives: 45.5 us -> 12.1 us
  local copies, waits for them, and re-layouts: 76.3 us -> 44.9 us
  Pallas kernels: 124 us -> 144 us
  other arithmetic: 79.6 us -> 63.2 us
  matrix products: 28.3 us -> 13.6 us
    ppermute x0 -> x18, waiting for transfers between devices: none -> 40.7 us  [the longest x6 32.3 us: line_reduce(): up = lax.ppermute(up, axis, [(i, i + 1) for i in range(step)]).astype(F32)]
    ppermute x0 -> x18, starting transfers between devices: none -> 39.1 us  [the longest x6 23.3 us: line_reduce(): up = lax.ppermute(up, axis, [(i, i + 1) for i in range(step)]).astype(F32)]
    all_gather x4 -> x3, waiting for transfers between devices: 35.6 us -> 0.02 us  [the longest x1 0.02 us: body(): lax.all_gather(jnp.concatenate([out_weight, down_weight], 0), 'z', axis=0...]
    all_to_all x1, waiting for transfers between devices: 35.1 us -> 6.07 us  [body(): lax.all_to_all(rear_wide, ALL, split_axis=0, concat_axis=0, tiled=True)]
    broadcast_in_dim x16 -> x6, local copies, waits for them, and re-layouts: 20.4 us -> 0.42 us  [merge_pair(): jnp.where(slot == lax.axis_index(axis), jnp.expand_dims(mine, position),...]
    all_to_all x1 -> x0, blocking collectives: 18.2 us -> none  [body(): lax.all_to_all(grad_attended[n], SEQ, split_axis=1, concat_axis=0, tiled=...]
    pallas_call x1 -> x8, Pallas kernels: 35.2 us -> 52.7 us  [the longest x1 35.3 us: feed(): pl.pallas_call(functools.partial(feed_kernel, sequences), grid_spec=pltpu...]
    all_gather x1 -> x0, blocking collectives: 16.1 us -> none  [body(): lax.all_gather(weight, 'z', axis=0, tiled=False)]
  transfers between devices with their start and end apart: 36 -> 51, of which waited for: 16 -> 17; matrix products, arithmetic and copies ran while one was open for 20% -> 17% of each run, Pallas kernels for 10% -> 19%
where the time goes in v3:
time: 574 us; the launch traced here: 564 us
  waiting for transfers between devices  179 us (31%)
  Pallas kernels  144 us (25%)
  starting transfers between devices  92.6 us (16%)
  other arithmetic  63.2 us (11%)
  local copies, waits for them, and re-layouts  44.9 us (8%)
  between operations  15.3 us (3%)
  matrix products  13.6 us (2%)
  blocking collectives  12.1 us (2%)
    ppermute x20, waiting for transfers between devices, swap(): return lax.ppermute(values, axis, [(0, 1), (1, 0)])  86.6 us
    pallas_call x2, Pallas kernels, attend_back(): pl.pallas_call(attend_back_kernel, grid=(length // block, heads), in_spec...  44.5 us
    pallas_call x1, Pallas kernels, feed(): pl.pallas_call(functools.partial(feed_kernel, sequences), grid_spec=pltpu...  35.3 us
    ppermute x6, waiting for transfers between devices, line_reduce(): up = lax.ppermute(up, axis, [(i, i + 1) for i in range(step)]).astype(F32)  32.3 us
    pallas_call x2, Pallas kernels, attend(): pl.pallas_call(attend_kernel, grid=(length // block, heads), in_specs=[pl...  31.3 us
    select_n x9, other arithmetic, merge_pair(): jnp.where(slot == lax.axis_index(axis), jnp.expand_dims(mine, position),...  25.9 us
    ppermute x6, starting transfers between devices, line_reduce(): up = lax.ppermute(up, axis, [(i, i + 1) for i in range(step)]).astype(F32)  23.3 us
    unnamed x161, local copies, waits for them, and re-layouts  19.9 us
  transfers between devices with their start and end apart: 51, of which 17 were waited for; matrix products, arithmetic and copies ran while one was open for 17% of the time, Pallas kernels for 19%

profile of v3, /device:TPU:0, one launch (start us, length us, event | category | flops | bytes accessed | tf_op | source)
XLA Modules:
  0.0 564.0 jit_solution(9063369327753149675)
XLA Ops:
  14.1 7.3 %all-to-all-start.1 = ((bf16[32,2,192]{2,1,0:T(2,128)(2,1)}), bf16[32,2,192]{2,1,0:T(2,128)(2,1)S(1)}, u32[]{:S(2)}, u32[]{:S(2)}) async-start(bf16[32,2,192]{2,1,0:T(2,128)(2,1)} %reshape.424), calls=%async_computation.1 | async-start | bytes 65536 | tf_op jit(solution)/shard_map/all_to_all | solution.py:676
  22.4 6.6 %all-to-all-done.1 = bf16[32,2,192]{2,1,0:T(2,128)(2,1)S(1)} async-done(((bf16[32,2,192]{2,1,0:T(2,128)(2,1)}), bf16[32,2,192]{2,1,0:T(2,128)(2,1)S(1)}, u32[]{:S(2)}, u32[]{:S(2)}) %all-to-all-start.1) | async-done | bytes 24608 | tf_op jit(solution)/shard_map/all_to_all | solution.py:676
  33.2 12.7 %all-to-all-done = bf16[8,32,384]{2,1,0:T(8,128)(2,1)S(1)} async-done(((bf16[8,32,384]{2,1,0:T(8,128)(2,1)}), bf16[8,32,384]{2,1,0:T(8,128)(2,1)S(1)}, u32[]{:S(2)}, u32[]{:S(2)}) %all-to-all-start) | async-done | bytes 196640 | tf_op jit(solution)/shard_map/all_to_all | solution.py:688
  50.5 12.1 %all-gather.2 = bf16[8,128,384]{2,1,0:T(8,128)(2,1)S(1)} all-gather(bf16[8,32,384]{2,1,0:T(8,128)(2,1)} %copy-done.59), channel_id=4, replica_groups=mesh['z'=4,'core'=2,'fy'=2,'fx'=2] {'fy','fx'}, dimensions={1}, use_global_device_ids=true | all-gather | bytes 983040 | tf_op jit(solution)/shard_map/all_gather | solution.py:689
  72.6 26.8 %collective-permute-done.5 = bf16[4,32,1024]{2,1,0:T(8,128)(2,1)S(1)} collective-permute-done((bf16[4,32,1024]{2,1,0:T(8,128)(2,1)S(1)}, bf16[4,32,1024]{2,1,0:T(8,128)(2,1)S(1)}, u32[]{:S(2)}, u32[]{:S(2)}) %collective-permute-start.5) | collective-permute-done | bytes 262176 | tf_op jit(solution)/shard_map/ppermute | solution.py:39
  105.4 8.3 %collective-permute-done.7 = bf16[32,4096]{1,0:T(8,128)(2,1)S(1)} collective-permute-done((bf16[32,4096]{1,0:T(8,128)(2,1)}, bf16[32,4096]{1,0:T(8,128)(2,1)S(1)}, u32[]{:S(2)}, u32[]{:S(2)}) %collective-permute-start.7) | collective-permute-done | bytes 262176 | tf_op jit(solution)/shard_map/ppermute | solution.py:64
  117.3 7.6 %project.2 = (bf16[2048,1024]{1,0:T(8,128)(2,1)}, bf16[2048,128]{1,0:T(8,128)(2,1)S(1)}, bf16[2048,128]{1,0:T(8,128)(2,1)S(1)}, bf16[2048,128]{1,0:T(8,128)(2,1)...) custom-call(bf16[2048,1024]{1,0:T(8,128)(2,1)} %bitcast.237, f32[1,1024]{1,0:T(1,128)S(1)} %reshape.361.gain_ref, ...), custom_call_target="tpu_custom_call" | custom-call | flops 1024 | bytes 1024 | tf_op jit(solution)/shard_map/project/pallas_call | solution.py:433
  125.8 15.7 %attend.2 = (bf16[2048,128]{1,0:T(8,128)(2,1)}, f32[2,1,2048]{2,1,0:T(1,128)S(1)}) custom-call(f32[2]{0:T(128)S(1)} %dynamic_slice.154.slope_ref, bf16[2048,128]{1,0:T(8,128)(2,1)S(1)} %get-tuple-element.134.q_ref, bf16[2048,128]{1,0:T(8,128)(2,1)S(1)} %get-tuple-element.99.k_ref, bf16[128,2048]{1,0:T(8,128)(2,1)S(1)} %get-tuple-element.100.vt_ref), custom_call_target="tpu_custom_call" | custom-call | flops 1024 | bytes 1024 | tf_op jit(solution)/shard_map/attend/pallas_call | solution.py:519
  141.5 42.1 %collective-permute-done.10 = bf16[4,2,32,1024]{3,2,1,0:T(8,128)(2,1)S(1)} collective-permute-done((bf16[4,2,32,1024]{3,2,1,0:T(8,128)(2,1)}, bf16[4,2,32,1024]{3,2,1,0:T(8,128)(2,1)S(1)}, u32[]{:S(2)}, u32[]{:S(2)}) %collective-permute-start.10) | collective-permute-done | bytes 524320 | tf_op jit(solution)/shard_map/ppermute | solution.py:39
  187.0 6.9 %all-to-all-start.2 = ((bf16[8,256,128]{2,1,0:T(8,128)(2,1)}), bf16[8,256,128]{2,1,0:T(8,128)(2,1)S(1)}, u32[]{:S(2)}, u32[]{:S(2)}) async-start(bf16[8,256,128]{2,1,0:T(8,128)(2,1)} %bitcast.14), calls=%async_computation.2 | async-start | bytes 1048576 | tf_op jit(solution)/shard_map/all_to_all | solution.py:714
  200.2 9.0 %all-to-all-done.2.att_ref.refs_0_.refs_2_ = bf16[8,256,128]{2,1,0:T(8,128)(2,1)S(1)} async-done(((bf16[8,256,128]{2,1,0:T(8,128)(2,1)}), bf16[8,256,128]{2,1,0:T(8,128)(2,1)S(1)}, u32[]{:S(2)}, u32[]{:S(2)}) %all-to-all-start.2) | async-done | bytes 524320 | tf_op jit(solution)/shard_map/all_to_all | solution.py:714
  209.2 7.5 %project.3 = (bf16[2048,1024]{1,0:T(8,128)(2,1)}, bf16[2048,128]{1,0:T(8,128)(2,1)S(1)}, bf16[2048,128]{1,0:T(8,128)(2,1)S(1)}, bf16[2048,128]{1,0:T(8,128)(2,1)...) custom-call(bf16[2048,1024]{1,0:T(8,128)(2,1)} %bitcast.236, f32[1,1024]{1,0:T(1,128)S(1)} %reshape.361.gain_ref, ...), custom_call_target="tpu_custom_call" | custom-call | flops 1024 | bytes 1024 | tf_op jit(solution)/shard_map/project/pallas_call | solution.py:433
  217.5 15.7 %attend.3 = (bf16[2048,128]{1,0:T(8,128)(2,1)}, f32[2,1,2048]{2,1,0:T(1,128)S(1)}) custom-call(f32[2]{0:T(128)S(1)} %dynamic_slice.154.slope_ref, bf16[2048,128]{1,0:T(8,128)(2,1)S(1)} %get-tuple-element.149.q_ref, bf16[2048,128]{1,0:T(8,128)(2,1)S(1)} %get-tuple-element.111.k_ref, bf16[128,2048]{1,0:T(8,128)(2,1)S(1)} %get-tuple-element.112.vt_ref), custom_call_target="tpu_custom_call" | custom-call | flops 1024 | bytes 1024 | tf_op jit(solution)/shard_map/attend/pallas_call | solution.py:519
  252.3 5.7 %all-to-all-done.3.att_ref.refs_1_.refs_3_ = bf16[8,256,128]{2,1,0:T(8,128)(2,1)S(1)} async-done(((bf16[8,256,128]{2,1,0:T(8,128)(2,1)}), bf16[8,256,128]{2,1,0:T(8,128)(2,1)S(1)}, u32[]{:S(2)}, u32[]{:S(2)}) %all-to-all-start.3) | async-done | bytes 524320 | tf_op jit(solution)/shard_map/all_to_all | solution.py:714
  264.9 35.3 %feed.1 = (f32[512,1024]{1,0:T(8,128)}, f32[512,512]{1,0:T(8,128)S(1)}, f32[512,512]{1,0:T(8,128)S(1)}, bf16[4,512,1024]{2,1,0:T(8,128)(2,1)}, bf16[4,512,1024]{...) custom-call(s32[1]{0:T(128)} %bitcast.me_ref, ...), custom_call_target="tpu_custom_call" | custom-call | flops 1024 | bytes 1024 | tf_op jit(solution)/shard_map/feed/pallas_call | solution.py:386
  340.1 8.6 %all-to-all-done.4 = bf16[8,2,256,128]{3,2,1,0:T(8,128)(2,1)} async-done(((bf16[8,2,256,128]{3,2,1,0:T(8,128)(2,1)}), bf16[8,2,256,128]{3,2,1,0:T(8,128)(2,1)}, u32[]{:S(2)}, u32[]{:S(2)}) %all-to-all-start.4) | async-done | bytes 1048608 | tf_op jit(solution)/shard_map/all_to_all | solution.py:767
  350.0 22.1 %attend_back.2 = (bf16[2048,128]{1,0:T(8,128)(2,1)S(1)}, bf16[2048,128]{1,0:T(8,128)(2,1)S(1)}, bf16[2048,128]{1,0:T(8,128)(2,1)S(1)}) custom-call(f32[2]{0:T(128)S(1)} %dynamic_slice.154.slope_ref, bf16[2048,128]{1,0:T(8,128)(2,1)S(1)} %copy-done.17, bf16[2048,128]{1,0:T(8,128)(2,1)S(1)} %copy-done.19, bf16[128,2048]{1,0:T(8,128)(2,1)S(1)} %copy-done.40, ...), custom_call_target="tpu_custom_call" | custom-call | flops 1024 | bytes 1024 | tf_op jit(solution)/shard_map/attend_back/pallas_call | solution.py:610
  372.1 14.2 %collective-permute-done.20 = bf16[4,2,32,1024]{3,2,0,1:T(8,128)(2,1)S(1)} collective-permute-done((bf16[4,2,32,1024]{3,2,0,1:T(8,128)(2,1)}, bf16[4,2,32,1024]{3,2,0,1:T(8,128)(2,1)S(1)}, u32[]{:S(2)}, u32[]{:S(2)}) %collective-permute-start.20) | collective-permute-done | bytes 524320 | tf_op jit(solution)/shard_map/ppermute | solution.py:39
  401.6 22.5 %attend_back.3 = (bf16[2048,128]{1,0:T(8,128)(2,1)S(1)}, bf16[2048,128]{1,0:T(8,128)(2,1)S(1)}, bf16[2048,128]{1,0:T(8,128)(2,1)S(1)}) custom-call(f32[2]{0:T(128)S(1)} %dynamic_slice.154.slope_ref, bf16[2048,128]{1,0:T(8,128)(2,1)S(1)} %copy-done.13, bf16[2048,128]{1,0:T(8,128)(2,1)S(1)} %copy-done.15, bf16[128,2048]{1,0:T(8,128)(2,1)S(1)} %copy-done.36, ...), custom_call_target="tpu_custom_call" | custom-call | flops 1024 | bytes 1024 | tf_op jit(solution)/shard_map/attend_back/pallas_call | solution.py:610
  466.5 5.1 collective-permute-start.27
  477.9 5.7 %collective-permute-start.34 = (bf16[32,4096]{1,0:T(8,128)(2,1)}, bf16[32,4096]{1,0:T(8,128)(2,1)}, u32[]{:S(2)}, u32[]{:S(2)}) collective-permute-start(bf16[32,4096]{1,0:T(8,128)(2,1)} %get-tuple-element.184), channel_id=1, source_target_pairs={{0,8},{8,16},{16,24},{1,9},{9,17},{17,25},{2,10},{10,18},{18,26},{... | collective-permute-start | bytes 786440 | tf_op jit(solution)/shard_map/ppermute | solution.py:78
  490.9 5.0 collective-permute-start.28
  499.6 26.1 %collective-permute-done.28 = bf16[160,1024]{1,0:T(8,128)(2,1)S(1)} collective-permute-done((bf16[160,1024]{1,0:T(8,128)(2,1)S(1)}, bf16[160,1024]{1,0:T(8,128)(2,1)S(1)}, u32[]{:S(2)}, u32[]{:S(2)}) %collective-permute-start.28) | collective-permute-done | bytes 327712 | tf_op jit(solution)/shard_map/ppermute | solution.py:78
  549.9 6.1 %all-to-all-done.7 = f32[32,1,256]{2,1,0:T(1,128)S(1)} async-done(((f32[32,1,256]{2,1,0:T(1,128)}), f32[32,1,256]{2,1,0:T(1,128)S(1)}, u32[]{:S(2)}, u32[]{:S(2)}) %all-to-all-start.7) | async-done | bytes 32800 | tf_op jit(solution)/shard_map/all_to_all | solution.py:779
  (371 shorter events, 214.3 us)
Async XLA Ops:
  7.2 60.1 %all-gather.10.cloned.1.call-start = ((), (), s32[]{:S(2)}) async-start(), calls=%async_computation.13 | async-start | bytes 1638400 | tf_op jit(solution)/shard_map/all_gather | solution.py:694
  9.0 108.3 %all-gather.8.cloned.1.call-start = ((), (), s32[]{:S(2)}) async-start(), calls=%async_computation.12 | async-start | bytes 4718592 | tf_op jit(solution)/shard_map/all_gather | solution.py:708
  32.3 167.8 %all-gather.12.cloned.1.call-start = ((), (), s32[]{:S(2)}) async-start(), calls=%async_computation.14 | async-start | bytes 4718592 | tf_op jit(solution)/shard_map/all_gather | solution.py:708
  64.0 38.7 %collective-permute-start.3 = (bf16[32,4096]{1,0:T(8,128)(2,1)}, bf16[32,4096]{1,0:T(8,128)(2,1)}, u32[]{:S(2)}, u32[]{:S(2)}) collective-permute-start(bf16[32,4096]{1,0:T(8,128)(2,1)} %collective-permute-done.1), channel_id=1, source_target_pairs={{8,0},{16,8},{9,1},{17,9},{10,2},{18,10},{11,3},{19,11},{12,4},{20... | collective-permute-start | bytes 786440 | tf_op jit(solution)/shard_map/ppermute | solution.py:64
  69.5 30.8 %collective-permute-start.4 = (bf16[4,128,1024]{2,1,0:T(8,128)(2,1)S(1)}, bf16[4,128,1024]{2,1,0:T(8,128)(2,1)S(1)}, u32[]{:S(2)}, u32[]{:S(2)}) collective-permute-start(bf16[4,128,1024]{2,1,0:T(8,128)(2,1)S(1)} %slice.118), channel_id=1, source_target_pairs={{0,2},{2,0},{1,3},{3,1},{4,6},{6,4},{5,7},{7,5},{8,10},{10,8},{9,1... | collective-permute-start | bytes 3145736 | tf_op jit(solution)/shard_map/ppermute | solution.py:39
  70.1 29.3 %collective-permute-start.5 = (bf16[4,32,1024]{2,1,0:T(8,128)(2,1)S(1)}, bf16[4,32,1024]{2,1,0:T(8,128)(2,1)S(1)}, u32[]{:S(2)}, u32[]{:S(2)}) collective-permute-start(bf16[4,32,1024]{2,1,0:T(8,128)(2,1)S(1)} %slice.119), channel_id=1, source_target_pairs={{0,2},{2,0},{1,3},{3,1},{4,6},{6,4},{5,7},{7,5},{8,10},{10,8},{9,1... | collective-permute-start | bytes 786440 | tf_op jit(solution)/shard_map/ppermute | solution.py:39
  103.7 79.8 %collective-permute-start.9 = (bf16[4,2,128,1024]{3,2,1,0:T(8,128)(2,1)}, bf16[4,2,128,1024]{3,2,1,0:T(8,128)(2,1)}, u32[]{:S(2)}, u32[]{:S(2)}) collective-permute-start(bf16[4,2,128,1024]{3,2,1,0:T(8,128)(2,1)} %broadcast_select_fusion.3), channel_id=1, source_target_pairs={{0,1},{1,0},{2,3},{3,2},{4,5},{5,4},{6,7},{7,6},{8,9},{9,8},{10,11... | collective-permute-start | bytes 6291464 | tf_op jit(solution)/shard_map/ppermute | solution.py:39
  114.8 68.7 %collective-permute-start.8 = (bf16[4,32,4096]{2,1,0:T(8,128)(2,1)}, bf16[4,32,4096]{2,1,0:T(8,128)(2,1)S(1)}, u32[]{:S(2)}, u32[]{:S(2)}) collective-permute-start(bf16[4,32,4096]{2,1,0:T(8,128)(2,1)} %slice.154), channel_id=1, source_target_pairs={{0,1},{1,0},{2,3},{3,2},{4,5},{5,4},{6,7},{7,6},{8,9},{9,8},{10,11... | collective-permute-start | bytes 3145736 | tf_op jit(solution)/shard_map/ppermute | solution.py:39
  116.4 67.1 %collective-permute-start.10 = (bf16[4,2,32,1024]{3,2,1,0:T(8,128)(2,1)}, bf16[4,2,32,1024]{3,2,1,0:T(8,128)(2,1)S(1)}, u32[]{:S(2)}, u32[]{:S(2)}) collective-permute-start(bf16[4,2,32,1024]{3,2,1,0:T(8,128)(2,1)} %broadcast_select_fusion.5), channel_id=1, source_target_pairs={{0,1},{1,0},{2,3},{3,2},{4,5},{5,4},{6,7},{7,6},{8,9},{9,8},{10,11... | collective-permute-start | bytes 1572872 | tf_op jit(solution)/shard_map/ppermute | solution.py:39
  186.6 46.6 %collective-permute-start.12 = (bf16[4,2,32,4096]{3,2,1,0:T(8,128)(2,1)}, bf16[4,2,32,4096]{3,2,1,0:T(8,128)(2,1)}, u32[]{:S(2)}, u32[]{:S(2)}) collective-permute-start(bf16[4,2,32,4096]{3,2,1,0:T(8,128)(2,1)} %broadcast_select_fusion.2), channel_id=1, source_target_pairs={{0,2},{2,0},{1,3},{3,1},{4,6},{6,4},{5,7},{7,5},{8,10},{10,8},{9,1... | collective-permute-start | bytes 6291464 | tf_op jit(solution)/shard_map/ppermute | solution.py:39
  198.6 66.3 %collective-permute-start.14 = (bf16[4,2,2,128,1024]{4,3,2,1,0:T(8,128)(2,1)}, bf16[4,2,2,128,1024]{4,3,2,1,0:T(8,128)(2,1)}, u32[]{:S(2)}, u32[]{:S(2)}) collective-permute-start(bf16[4,2,2,128,1024]{4,3,2,1,0:T(8,128)(2,1)} %broadcast_select_fusion.1), channel_id=1, source_target_pairs={{0,4},{4,0},{1,5},{5,1},{2,6},{6,2},{3,7},{7,3},{8,12},{12,8},{9,1... | collective-permute-start | bytes 12582920 | tf_op jit(solution)/shard_map/ppermute | solution.py:39
  317.9 30.9 %all-to-all-start.4 = ((bf16[8,2,256,128]{3,2,1,0:T(8,128)(2,1)}), bf16[8,2,256,128]{3,2,1,0:T(8,128)(2,1)}, u32[]{:S(2)}, u32[]{:S(2)}) async-start(bf16[8,2,256,128]{3,2,1,0:T(8,128)(2,1)} %copy.126), calls=%async_computation.4 | async-start | bytes 2097152 | tf_op jit(solution)/shard_map/all_to_all | solution.py:767
  322.1 205.3 %reduce-scatter.5.cloned.1.call-start = ((), (), s32[]{:S(2)}) async-start(), calls=%async_computation.11 | async-start | bytes 4718592 | tf_op jit(solution)/shard_map/reduce_scatter | solution.py:798
  327.0 59.3 %collective-permute-start.19 = (bf16[4,2,128,1024]{3,2,0,1:T(8,128)(2,1)}, bf16[4,2,128,1024]{3,2,0,1:T(8,128)(2,1)}, u32[]{:S(2)}, u32[]{:S(2)}) collective-permute-start(bf16[4,2,128,1024]{3,2,0,1:T(8,128)(2,1)} %fusion.1), channel_id=1, source_target_pairs={{0,1},{1,0},{2,3},{3,2},{4,5},{5,4},{6,7},{7,6},{8,9},{9,8},{10,11... | collective-permute-start | bytes 6291464 | tf_op jit(solution)/shard_map/ppermute | solution.py:39
  331.9 54.4 %collective-permute-start.18 = (bf16[4,2,32,4096]{3,2,0,1:T(8,128)(2,1)}, bf16[4,2,32,4096]{3,2,0,1:T(8,128)(2,1)}, u32[]{:S(2)}, u32[]{:S(2)}) collective-permute-start(bf16[4,2,32,4096]{3,2,0,1:T(8,128)(2,1)} %fusion), channel_id=1, source_target_pairs={{0,2},{2,0},{1,3},{3,1},{4,6},{6,4},{5,7},{7,5},{8,10},{10,8},{9,1... | collective-permute-start | bytes 6291464 | tf_op jit(solution)/shard_map/ppermute | solution.py:39
  339.0 47.3 %collective-permute-start.20 = (bf16[4,2,32,1024]{3,2,0,1:T(8,128)(2,1)}, bf16[4,2,32,1024]{3,2,0,1:T(8,128)(2,1)S(1)}, u32[]{:S(2)}, u32[]{:S(2)}) collective-permute-start(bf16[4,2,32,1024]{3,2,0,1:T(8,128)(2,1)} %fusion.13), channel_id=1, source_target_pairs={{0,1},{1,0},{2,3},{3,2},{4,5},{5,4},{6,7},{7,6},{8,9},{9,8},{10,11... | collective-permute-start | bytes 1572872 | tf_op jit(solution)/shard_map/ppermute | solution.py:39
  391.9 138.4 %reduce-scatter.3.cloned.1.call-start = ((), (), s32[]{:S(2)}) async-start(), calls=%async_computation.10 | async-start | bytes 4718592 | tf_op jit(solution)/shard_map/reduce_scatter | solution.py:798
  394.7 30.3 %collective-permute-start.22 = (bf16[4,128,1024]{2,1,0:T(8,128)(2,1)S(1)}, bf16[4,128,1024]{2,1,0:T(8,128)(2,1)S(1)}, u32[]{:S(2)}, u32[]{:S(2)}) collective-permute-start(bf16[4,128,1024]{2,1,0:T(8,128)(2,1)S(1)} %fusion.6), channel_id=1, source_target_pairs={{0,2},{2,0},{1,3},{3,1},{4,6},{6,4},{5,7},{7,5},{8,10},{10,8},{9,1... | collective-permute-start | bytes 3145736 | tf_op jit(solution)/shard_map/ppermute | solution.py:39
  441.3 32.8 %collective-permute-start.35 = (bf16[32,4096]{1,0:T(8,128)(2,1)}, bf16[32,4096]{1,0:T(8,128)(2,1)}, u32[]{:S(2)}, u32[]{:S(2)}) collective-permute-start(bf16[32,4096]{1,0:T(8,128)(2,1)} %get-tuple-element.187), channel_id=1, source_target_pairs={{24,16},{25,17},{26,18},{27,19},{28,20},{29,21},{30,22},{31,23}} | collective-permute-start | bytes 786440 | tf_op jit(solution)/shard_map/ppermute | solution.py:79
  477.9 59.7 %collective-permute-start.34 = (bf16[32,4096]{1,0:T(8,128)(2,1)}, bf16[32,4096]{1,0:T(8,128)(2,1)}, u32[]{:S(2)}, u32[]{:S(2)}) collective-permute-start(bf16[32,4096]{1,0:T(8,128)(2,1)} %get-tuple-element.184), channel_id=1, source_target_pairs={{0,8},{8,16},{16,24},{1,9},{9,17},{17,25},{2,10},{10,18},{18,26},{... | collective-permute-start | bytes 786440 | tf_op jit(solution)/shard_map/ppermute | solution.py:78
  484.4 49.6 %all-to-all-start.6 = ((f32[8,32,384]{2,1,0:T(8,128)}), f32[8,32,384]{2,1,0:T(8,128)}, u32[]{:S(2)}, u32[]{:S(2)}) async-start(f32[8,32,384]{2,1,0:T(8,128)} %fusion.24), calls=%async_computation.8 | async-start | bytes 786432 | tf_op jit(solution)/shard_map/all_to_all | solution.py:810
  490.9 34.8 %collective-permute-start.28 = (bf16[160,1024]{1,0:T(8,128)(2,1)S(1)}, bf16[160,1024]{1,0:T(8,128)(2,1)S(1)}, u32[]{:S(2)}, u32[]{:S(2)}) collective-permute-start(bf16[160,1024]{1,0:T(8,128)(2,1)S(1)} %get-tuple-element.178), channel_id=1, source_target_pairs={{0,8},{8,16},{16,24},{1,9},{9,17},{17,25},{2,10},{10,18},{18,26},{... | collective-permute-start | bytes 983048 | tf_op jit(solution)/shard_map/ppermute | solution.py:78
  495.9 29.9 %collective-permute-start.31 = (bf16[160,1024]{1,0:T(8,128)(2,1)S(1)}, bf16[160,1024]{1,0:T(8,128)(2,1)S(1)}, u32[]{:S(2)}, u32[]{:S(2)}) collective-permute-start(bf16[160,1024]{1,0:T(8,128)(2,1)S(1)} %get-tuple-element.179), channel_id=1, source_target_pairs={{8,0},{16,8},{24,16},{9,1},{17,9},{25,17},{10,2},{18,10},{26,18},{... | collective-permute-start | bytes 983048 | tf_op jit(solution)/shard_map/ppermute | solution.py:79
  498.0 39.6 %collective-permute-start.37 = (bf16[32,4096]{1,0:T(8,128)(2,1)}, bf16[32,4096]{1,0:T(8,128)(2,1)}, u32[]{:S(2)}, u32[]{:S(2)}) collective-permute-start(bf16[32,4096]{1,0:T(8,128)(2,1)} %fusion.15), channel_id=1, source_target_pairs={{8,0},{16,8},{24,16},{9,1},{17,9},{25,17},{10,2},{18,10},{26,18},{... | collective-permute-start | bytes 786440 | tf_op jit(solution)/shard_map/ppermute | solution.py:79
  (103 other events, 1293.4 us)
Sparse Core Ops, SparseCore 0:
  10.2 40.3 all-gather.9
  52.7 53.4 all-gather.7
  108.4 45.6 all-gather.11
  392.0 50.2 reduce-scatter.4
  444.4 82.1 reduce-scatter.2
